TPU v7x, 32 devices: a whole 2x2x4 slice. The times are simulated.
32 devices in a mesh: tm: 8 (over z, y), panel: 4 (over x, core).
Axes of the slice: x: 2, y: 2, z: 4, core: 2. Of those that a mesh axis runs over, the one named last changes fastest.
Arguments:
- record: bfloat16 [16384, 1024], P('tm'), may hold values from -6 to 6
- eigvecs: bfloat16 [16384, 32], P(('tm', 'panel')), may hold values from -2.5 to 2.5
- starts: int32 [8], P('panel'), may hold values from 0 to 15616, as said below
- kernel_width: float32 [1], replicated, may hold values from 0.025 to 0.1
Outputs:
- applied: float32 [8, 768, 32], P('panel', 'tm')
Inputs may be any that keep to these rules, and one draw needn't show every extreme that they name: Some panel starts at 0 and some at 15616.
All inputs are finite; a program needn't handle non-finite values.
Results may differ from a plain program's by a relative error of at most 0.0003.
Values may be sent and summed in bfloat16 or wider, within the bound.
No kernel may reach another device: no remote copies, remote signals or barrier semaphores. Data moves between devices by JAX's collectives and lax.ppermute only.
A program may use at most 128 MiB of HBM per device.

v0:
```python
import jax
import jax.numpy as jnp
from jax import lax
from jax.sharding import PartitionSpec as P

CHANNELS = 1024
DELAYS = 64
PANEL = 768
PAN_DEV = 2


def shifted(value, axis, steps):
    count = lax.axis_size(axis)
    initial, last = (max(0, -steps), min(count, count - steps))
    return lax.ppermute(value, axis, [(source, source + steps) for source in range(initial, last)])


def lag_sums(summed):
    stride = 1
    while stride < DELAYS:
        if summed.ndim == 2:
            summed = summed[:-stride, :-stride] + summed[stride:, stride:]
        else:
            summed = summed[:-stride] + summed[stride:]
        stride = stride * 2
    return summed


def body(record, eigvecs, starts, kernel_width):
    columns = record.shape[0]
    record_length = PANEL + DELAYS - 1
    vectors = lax.all_gather(eigvecs, "panel", axis=0, tiled=True)
    rim_rows = shifted(record[columns - (DELAYS - 1) :], "tm", 1)
    extended = jnp.concatenate([rim_rows, record], axis=0)
    column_norms = lag_sums(jnp.sum(jnp.square(extended.astype(jnp.float32)), axis=1))
    offset = lax.axis_index("tm") * columns
    blank = jnp.zeros((record_length, CHANNELS), jnp.bfloat16)
    bordered = jnp.concatenate([blank, record, blank], axis=0)

    def segment_lookup(begin):
        located = jnp.clip(begin - offset, -record_length, columns) + record_length
        return lax.dynamic_slice_in_dim(bordered, located, record_length, 0)

    opening_positions = [starts[number] - (DELAYS - 1) for number in range(PAN_DEV)]
    pieces = jnp.stack([segment_lookup(begin) for begin in opening_positions])
    windows = lax.psum(pieces, "tm").astype(jnp.float32).astype(jnp.bfloat16)
    spread = kernel_width[0] * (DELAYS * CHANNELS)
    numers = []
    totals = []
    for number in range(PAN_DEV):
        window = windows[number]
        row_norms = lag_sums(jnp.sum(jnp.square(window.astype(jnp.float32)), axis=1))
        gram = lax.dot_general(
            window, extended, (((1,), (1,)), ((), ())), preferred_element_type=jnp.float32
        )
        inner = lag_sums(gram)
        distance = row_norms[:, None] + column_norms[None, :] - 2.0 * inner
        kernel = jnp.exp(-distance / spread)
        totals.append(jnp.sum(kernel, axis=1))
        numers.append(
            jnp.dot(kernel.astype(jnp.bfloat16), vectors, preferred_element_type=jnp.float32)
        )
    numer = jnp.stack(numers)
    total = jnp.stack(totals)
    numer, total = lax.psum((numer, total), "tm")
    portion = PANEL // lax.axis_size("tm")
    first_row = lax.axis_index("tm") * portion
    numer = lax.dynamic_slice_in_dim(numer, first_row, portion, 1)
    total = lax.dynamic_slice_in_dim(total, first_row, portion, 1)
    return numer / total[:, :, None]


def solution(mesh):
    placed = (P("tm", None), P(("tm", "panel"), None), P("panel"), P())
    return jax.shard_map(
        body, mesh=mesh, in_specs=placed, out_specs=P("panel", "tm", None), check_vma=False
    )
```

profile of v0, /device:TPU:0, one launch (start us, length us, event | category | flops | bytes accessed | tf_op | source)
XLA Modules:
  0.0 357.6 jit_solution(5805464547031043593)
XLA Ops:
  6.5 1.4 fusion.28
  9.3 0.2 broadcast_in_dim.2
  9.5 32.9 %concatenate.6 = bf16[3710,1024]{1,0:T(8,128)(2,1)} concatenate(bf16[831,1024]{1,0:T(8,128)(2,1)S(1)} %broadcast_in_dim.2, bf16[2048,1024]{1,0:T(8,128)(2,1)} %param.4, bf16[831,1024]{1,0:T(8,128)(2,1)S(1)} %broadcast_in_dim.2), dimensions={0} | concatenate | bytes 15196160 | tf_op jit(solution)/shard_map/concatenate | solution.py:38
  42.4 2.9 dynamic-slice_bitcast_fusion.1
  45.3 2.0 pad_maximum_fusion.1
  47.4 0.9 slice.210
  48.3 4.9 %collective-permute-start = (bf16[63,1024]{1,0:T(8,128)(2,1)S(1)}, bf16[63,1024]{1,0:T(8,128)(2,1)S(1)}, u32[]{:S(2)}, u32[]{:S(2)}) collective-permute-start(bf16[63,1024]{1,0:T(8,128)(2,1)S(1)} %slice.210), channel_id=1, source_target_pairs={{0,4},{4,8},{8,12},{12,16},{16,20},{20,24},{24,28},{1,5},{5,9},{9,... | collective-permute-start | bytes 387080 | tf_op jit(solution)/shard_map/ppermute | solution.py:15
  53.9 5.4 %all_gather.3 = bf16[2048,32]{0,1:T(8,128)(2,1)S(1)} all-gather(bf16[512,32]{0,1:T(8,128)(2,1)S(1)} %copy-done.1), channel_id=1, replica_groups=mesh['tm'=8,'panel'=4] {'panel'}, dimensions={0}, use_global_device_ids=true | all-gather | bytes 163840 | tf_op jit(solution)/shard_map/all_gather | solution.py:32
  59.3 3.7 %multiply_reduce_fusion = f32[2111]{0:T(1024)S(1)} fusion(bf16[2048,1024]{1,0:T(8,128)(2,1)} %param.4, bf16[63,1024]{1,0:T(8,128)(2,1)S(1)} %collective-permute-done), kind=kLoop, calls=%fused_computation | loop fusion | flops 12967873 | bytes 4331772 | tf_op jit(solution)/shard_map/reduce_sum | solution.py:35
  63.2 0.1 slice_add_fusion.13
  63.3 0.1 slice_add_fusion.12
  63.4 123.4 %all-reduce.3.cloned.1.call-done = bf16[2,831,1024]{2,1,0:T(8,128)(2,1)} async-done(((bf16[2,831,1024]{2,1,0:T(8,128)(2,1)}), bf16[2,831,1024]{2,1,0:T(8,128)(2,1)}) %all-reduce.3.cloned.1.call-update) | async-done | bytes 3403792 | tf_op jit(solution)/shard_map/psum | solution.py:46
  186.9 2.7 multiply_reduce_fusion.2
  190.4 9.8 %fusion.14 = f32[831,2111]{1,0:T(8,128)} fusion(bf16[2,831,1024]{2,1,0:T(8,128)(2,1)} %all-reduce.3.cloned.1.call-done, bf16[2048,1024]{1,0:T(8,128)(2,1)} %param.4, bf16[63,1024]{1,0:T(8,128)(2,1)S(1)} %collective-permute-done), kind=kOutput, calls=%fused_computation.35 | convolution fusion | flops 3601332224 | bytes 13044228 | tf_op jit(solution)/shard_map/dot_general | solution.py:53
  200.3 7.8 %slice_add_fusion.3 = f32[830,2110]{1,0:T(8,128)S(1)} fusion(f32[831,2111]{1,0:T(8,128)} %fusion.14), kind=kLoop, calls=%fused_computation.4 | loop fusion | flops 1751300 | bytes 21015600 | tf_op jit(solution)/shard_map/add | solution.py:22
  208.1 5.7 %slice_add_fusion.2 = f32[828,2108]{1,0:T(8,128)} fusion(f32[830,2110]{1,0:T(8,128)S(1)} %slice_add_fusion.3), kind=kLoop, calls=%fused_computation.3 | loop fusion | flops 1745424 | bytes 20945088 | tf_op jit(solution)/shard_map/add | solution.py:22
  213.8 7.9 %slice_add_fusion.5 = f32[824,2104]{1,0:T(8,128)S(1)} fusion(f32[828,2108]{1,0:T(8,128)} %slice_add_fusion.2), kind=kLoop, calls=%fused_computation.6 | loop fusion | flops 1733696 | bytes 20804352 | tf_op jit(solution)/shard_map/add | solution.py:22
  221.8 4.8 %slice_add_fusion.7 = f32[816,2096]{1,0:T(8,128)} fusion(f32[824,2104]{1,0:T(8,128)S(1)} %slice_add_fusion.5), kind=kLoop, calls=%fused_computation.8 | loop fusion | flops 1710336 | bytes 20524032 | tf_op jit(solution)/shard_map/add | solution.py:22
  226.6 7.8 %fusion.15 = f32[831,2111]{1,0:T(8,128)} fusion(bf16[2,831,1024]{2,1,0:T(8,128)(2,1)} %all-reduce.3.cloned.1.call-done, bf16[2048,1024]{1,0:T(8,128)(2,1)S(1)} %copy-done, bf16[63,1024]{1,0:T(8,128)(2,1)S(1)} %collective-permute-done), kind=kOutput, calls=%fused_computation.36 | convolution fusion | flops 3601332224 | bytes 13044228 | tf_op jit(solution)/shard_map/dot_general | solution.py:53
  234.4 7.8 %slice_add_fusion.1 = f32[830,2110]{1,0:T(8,128)S(1)} fusion(f32[831,2111]{1,0:T(8,128)} %fusion.15), kind=kLoop, calls=%fused_computation.2 | loop fusion | flops 1751300 | bytes 21015600 | tf_op jit(solution)/shard_map/add | solution.py:22
  242.2 5.7 %slice_add_fusion = f32[828,2108]{1,0:T(8,128)} fusion(f32[830,2110]{1,0:T(8,128)S(1)} %slice_add_fusion.1), kind=kLoop, calls=%fused_computation.1 | loop fusion | flops 1745424 | bytes 20945088 | tf_op jit(solution)/shard_map/add | solution.py:22
  247.9 7.7 %slice_add_fusion.4 = f32[824,2104]{1,0:T(8,128)S(1)} fusion(f32[828,2108]{1,0:T(8,128)} %slice_add_fusion), kind=kLoop, calls=%fused_computation.5 | loop fusion | flops 1733696 | bytes 20804352 | tf_op jit(solution)/shard_map/add | solution.py:22
  255.7 4.8 %slice_add_fusion.6 = f32[816,2096]{1,0:T(8,128)} fusion(f32[824,2104]{1,0:T(8,128)S(1)} %slice_add_fusion.4), kind=kLoop, calls=%fused_computation.7 | loop fusion | flops 1710336 | bytes 20524032 | tf_op jit(solution)/shard_map/add | solution.py:22
  260.5 10.9 %slice_add_fusion.8 = (f32[800,2080]{1,0:T(8,128)S(1)}, f32[800,2080]{1,0:T(8,128)S(1)}) fusion(f32[816,2096]{1,0:T(8,128)} %slice_add_fusion.6, f32[816,2096]{1,0:T(8,128)} %slice_add_fusion.7), kind=kLoop, calls=%fused_computation.9 | loop fusion | flops 3328000 | bytes 39936000 | tf_op jit(solution)/shard_map/add | solution.py:22
  271.4 5.7 %fusion.24 = (f32[768]{0:T(1024)S(1)}, bf16[768,2048]{1,0:T(8,128)(2,1)S(1)}, f32[768]{0:T(1024)S(1)}, bf16[768,2048]{1,0:T(8,128)(2,1)S(1)}) fusion(f32[]{:T(128)} %bitcast.5, f32[800,2080]{1,0:T(8,128)S(1)} %get-tuple-element.20, f32[2048]{0:T(1024)S(1)} %slice_add_fusion.17, f32[768]{0:T(1024)S(1)} %slice_add_fusion.24, ...), kind=kLoop, calls=%fused_computation.63 | loop fusion | flops 25164288 | bytes 31477764 | tf_op jit(solution)/shard_map/reduce_sum | solution.py:59
  277.1 1.0 fusion.16
  278.1 1.0 fusion.19
  279.2 0.7 pad_maximum_fusion.4
  279.9 19.5 %psum.23 = f32[2,768]{1,0:T(2,128)S(1)} all-reduce(f32[2,768]{1,0:T(2,128)S(1)} %pad_maximum_fusion.5), channel_id=1, replica_groups=mesh['tm'=8,'panel'=4] {'tm'}, use_global_device_ids=true, to_apply=%region_7.8 | all-reduce | flops 1536 | bytes 12288 | tf_op jit(solution)/shard_map/psum | solution.py:65
  299.4 0.1 constant_dynamic-slice_fusion
  299.5 49.7 %all-reduce.5.cloned.1.call-done = f32[2,768,32]{1,2,0:T(8,128)} async-done(((f32[2,768,32]{1,2,0:T(8,128)}), f32[2,768,32]{1,2,0:T(8,128)}) %all-reduce.5.cloned.1.call-update) | async-done | bytes 196624 | tf_op jit(solution)/shard_map/psum | solution.py:65
  349.3 1.5 dynamic-slice_divide_fusion
  (27 shorter events, 1.2 us)
Async XLA Ops:
  6.5 180.4 %all-reduce.3.cloned.1.call-start = ((), (), s32[]{:S(2)}) async-start(), calls=%async_computation | async-start | bytes 6815744 | tf_op jit(solution)/shard_map/psum | solution.py:46
  45.3 8.6 %copy-start.1 = (bf16[512,32]{0,1:T(8,128)(2,1)S(1)}, bf16[512,32]{0,1:T(8,128)(2,1)}, u32[]{:S(2)}) copy-start(bf16[512,32]{0,1:T(8,128)(2,1)} %param.5) | copy-start | bytes 98308
  47.3 301.9 %all-reduce.5.cloned.1.call-start = ((), (), s32[]{:S(2)}) async-start(), calls=%async_computation.1 | async-start | bytes 393216 | tf_op jit(solution)/shard_map/psum | solution.py:65
  48.3 11.0 %collective-permute-start = (bf16[63,1024]{1,0:T(8,128)(2,1)S(1)}, bf16[63,1024]{1,0:T(8,128)(2,1)S(1)}, u32[]{:S(2)}, u32[]{:S(2)}) collective-permute-start(bf16[63,1024]{1,0:T(8,128)(2,1)S(1)} %slice.210), channel_id=1, source_target_pairs={{0,4},{4,8},{8,12},{12,16},{16,20},{20,24},{24,28},{1,5},{5,9},{9,... | collective-permute-start | bytes 387080 | tf_op jit(solution)/shard_map/ppermute | solution.py:15
  221.7 4.8 %copy-start = (bf16[2048,1024]{1,0:T(8,128)(2,1)S(1)}, bf16[2048,1024]{1,0:T(8,128)(2,1)}, u32[]{:S(2)}) copy-start(bf16[2048,1024]{1,0:T(8,128)(2,1)} %param.4) | copy-start | bytes 12582916
Sparse Core Ops, SparseCore 0:
  47.5 139.3 all-reduce.2
  280.0 69.2 all-reduce.4
where the time goes:
time: 359 us; the launch traced here: 358 us
  waiting for transfers between devices  173 us (48%)
  other arithmetic  80.9 us (23%)
  local copies, waits for them, and re-layouts  38.4 us (11%)
  blocking collectives  25 us (7%)
  matrix products  19.7 us (5%)
  between operations  15.5 us (4%)
  starting transfers between devices  4.92 us (1%)
    psum x1, waiting for transfers between devices, body(): windows = lax.psum(pieces, 'tm').astype(jnp.float32).astype(jnp.bfloat16)  123 us
    add x9, other arithmetic, lag_sums(): summed = summed[:-stride, :-stride] + summed[stride:, stride:]  63.3 us
    psum x1, waiting for transfers between devices, body(): numer, total = lax.psum((numer, total), 'tm')  49.7 us
    concatenate x1, local copies, waits for them, and re-layouts, body(): bordered = jnp.concatenate([blank, record, blank], axis=0)  32.9 us
    psum x1, blocking collectives, body(): numer, total = lax.psum((numer, total), 'tm')  19.5 us
    dot_general x2, matrix products, body(): lax.dot_general(window, extended, (((1,), (1,)), ((), ())), preferred_ele...  17.6 us
  transfers between devices with their start and end apart: 3, of which 2 were waited for; matrix products, arithmetic and copies ran while one was open for 1% of the time, Pallas kernels for 0%

commit v1 on v0

v1 whole, which is shorter than its diff:
```python
import jax
import jax.numpy as jnp
from jax import lax
from jax.experimental import pallas as pl
from jax.experimental.pallas import tpu as pltpu
from jax.sharding import PartitionSpec as P

DELAYS = 64
PANEL = 768
SLOTS = 2
GROUP = 16
LANES = 128
MODES = 32
BIG = 1e30


def panel_kernel(homes, parts, meta, scale, record, rim, vectors, norms, *rest):
    shards = rest[:parts]
    out, window, turned, gram, strips, weights, sums, result = rest[parts:]
    columns = record.shape[0]
    width = columns + LANES
    tiles = width // LANES
    rows = window.shape[0]
    used = turned.shape[0]
    kept = used - DELAYS
    modes = MODES
    for number in range(parts):
        first = meta[number]
        for step in range(shards[number].shape[0]):
            place = pl.multiple_of((first + homes * step) * GROUP, GROUP)
            window[pl.ds(place, GROUP), :] = shards[number][step]
    low = 0
    while low < used:
        count = min(LANES, used - low)
        turn = lax.broadcasted_iota(jnp.int32, (count, count), 0) + lax.broadcasted_iota(jnp.int32, (count, count), 1)
        flip = jnp.where(turn == count - 1, 2.0, 0.0).astype(jnp.bfloat16)
        block = jnp.dot(flip, window[used - low - count : used - low, :], preferred_element_type=jnp.float32)
        turned[low : low + count, :] = block.astype(jnp.bfloat16)
        energy = jnp.sum(block * block, axis=1, keepdims=True) * 0.25
        strips[tiles, low : low + count, :] = jnp.broadcast_to(energy, (count, LANES))
        low += count
    low = 0
    while low < used:
        count = min(LANES, used - low)
        block = turned[low : low + count, :]
        gram[:count, :columns] = lax.dot_general(
            block, record[...], (((1,), (1,)), ((), ())), preferred_element_type=jnp.float32
        )
        gram[:count, columns:] = lax.dot_general(
            block, rim[...], (((1,), (1,)), ((), ())), preferred_element_type=jnp.float32
        )
        for row in range(0, count, 8):
            line = pltpu.roll(gram[row : row + 8, :], (low + row) % width, 1, stride=1, stride_axis=0)
            for tile in range(tiles):
                strips[tile, low + row : low + row + 8, :] = line[:, tile * LANES : (tile + 1) * LANES]
        low += count

    def add_lags(tile, carry):
        value = strips[tile]
        stride = 1
        while stride < DELAYS:
            value = value[stride:] + value[:-stride]
            stride *= 2
        strips[tile, DELAYS:used, :] = value[1:]
        return carry

    lax.fori_loop(0, tiles + 1, add_lags, 0)
    factor = scale[0]
    for row in range(DELAYS, used, 16):
        halves = []
        for part in range(2):
            at = row + 8 * part
            line = jnp.concatenate([strips[tile, at : at + 8, :] for tile in range(tiles)], axis=1)
            line = pltpu.roll(line, (DELAYS - 1 - at) % width, 1)
            own = jnp.concatenate([strips[tiles, at : at + 8, :]] * tiles, axis=1)
            value = jnp.exp2(((own + norms[...]) - line) * factor)
            total = value[:, :LANES]
            for tile in range(1, tiles):
                total = total + value[:, tile * LANES : (tile + 1) * LANES]
            sums[at - DELAYS : at - DELAYS + 8, :] = total
            halves.append(value)
        weights[row - DELAYS : row - DELAYS + 16, :] = jnp.concatenate(halves, axis=0).astype(jnp.bfloat16)
    product = jnp.dot(weights[...], vectors[...], preferred_element_type=jnp.float32)
    lane = lax.broadcasted_iota(jnp.int32, (kept, 2 * LANES), 1)
    sub = lax.broadcasted_iota(jnp.int32, (kept, 2 * LANES), 0)
    product = jnp.where(lane // modes == sub % 8, product, 0.0)
    product = product[:, :LANES] + product[:, LANES:]
    product = product + pltpu.roll(product, 64, 1)
    product = product + pltpu.roll(product, 32, 1)
    lane = lax.broadcasted_iota(jnp.int32, (kept, LANES), 1)
    total = jnp.sum(sums[...], axis=1, keepdims=True)
    product = jnp.where(lane == modes, total, product)
    result[...] = jnp.where(lane <= modes, product, 0.0)
    share = PANEL // homes
    third = share // 3
    offset = meta[parts]
    for home in range(homes):
        start = kept - share * (home + 1) - offset
        packed = result[pl.ds(start, third), :]
        for part in range(1, 3):
            packed = packed + pltpu.roll(result[pl.ds(start + part * third, third), :], 40 * part, 1)
        out[home] = packed


def panel_call(homes, deal, shards, record, rim, vectors, norms, meta, scale):
    parts = len(shards)
    columns = record.shape[0]
    width = columns + LANES
    tiles = width // LANES
    used = -(-(PANEL + DELAYS - 1 + GROUP - 1) // GROUP) * GROUP
    kept = used - DELAYS
    share = PANEL // homes
    vm = pl.BlockSpec(memory_space=pltpu.VMEM)
    sm = pl.BlockSpec(memory_space=pltpu.SMEM)
    return pl.pallas_call(
        lambda *refs: panel_kernel(homes, parts, *refs),
        out_shape=jax.ShapeDtypeStruct((homes, share // 3, LANES), jnp.float32),
        in_specs=[sm, sm] + [vm] * (4 + parts),
        out_specs=vm,
        scratch_shapes=[
            pltpu.VMEM((homes * deal * GROUP, record.shape[1]), jnp.bfloat16),
            pltpu.VMEM((used, record.shape[1]), jnp.bfloat16),
            pltpu.VMEM((LANES, width), jnp.float32),
            pltpu.VMEM((tiles + 1, used, LANES), jnp.float32),
            pltpu.VMEM((kept, width), jnp.bfloat16),
            pltpu.VMEM((kept, LANES), jnp.float32),
            pltpu.VMEM((kept, LANES), jnp.float32),
        ],
        compiler_params=pltpu.CompilerParams(vmem_limit_bytes=56 * 1024 * 1024),
        cost_estimate=pl.CostEstimate(flops=2 * used * width * record.shape[1], bytes_accessed=8_000_000, transcendentals=kept * width),
    )(meta, scale, record, rim, vectors, norms, *shards)


def fan(vectors, width):
    columns, modes = vectors.shape
    padded = jnp.concatenate([vectors, jnp.zeros((width - columns, modes), vectors.dtype)], axis=0)
    return jnp.concatenate([jnp.roll(padded, shift, axis=0) for shift in range(8)], axis=1)


def slant(norms, width):
    padded = jnp.concatenate([norms, jnp.full((width - norms.shape[0],), BIG, jnp.float32)])
    return jnp.stack([jnp.roll(padded, shift) for shift in range(8)])


def pick_kernel(count, index, store, *outs):
    place = 0
    for out in outs:
        for row in range(out.shape[0]):
            at = index[place + row]

            @pl.when(at >= 0)
            def _():
                out[row] = store[at]

            @pl.when(at < 0)
            def _():
                out[row] = jnp.zeros(out.shape[1:], out.dtype)

        place += out.shape[0]


def pick(store, index, counts):
    vm = pl.BlockSpec(memory_space=pltpu.VMEM)
    sm = pl.BlockSpec(memory_space=pltpu.SMEM)
    return pl.pallas_call(
        lambda *refs: pick_kernel(counts, *refs),
        out_shape=[jax.ShapeDtypeStruct((count,) + store.shape[1:], store.dtype) for count in counts],
        in_specs=[sm, vm],
        out_specs=[vm] * len(counts),
    )(index, store)


def lag_sums(summed):
    stride = 1
    while stride < DELAYS:
        summed = summed[:-stride] + summed[stride:]
        stride = stride * 2
    return summed


def tour(homes):
    if homes == 8:
        return [0, 2, 4, 6, 7, 5, 3, 1]
    return list(range(homes))


def share_round(value):
    sharers = lax.axis_size("panel")
    found = [value]
    for hop in range(1, sharers):
        found.append(lax.ppermute(value, "panel", [((i + hop) % sharers, i) for i in range(sharers)]))
    rows = value.shape[0]
    first = (sharers - lax.axis_index("panel")) % sharers * rows
    return lax.dynamic_slice_in_dim(jnp.concatenate(found + found[:-1], axis=0), first, rows * sharers, 0)


def step_round(value, order, way):
    homes = len(order)
    return lax.ppermute(value, "tm", [(order[i], order[(i + way) % homes]) for i in range(homes)])


def body(record, eigvecs, starts, kernel_width):
    homes = lax.axis_size("tm")
    sharers = lax.axis_size("panel")
    home = lax.axis_index("tm")
    sharer = lax.axis_index("panel")
    columns, channels = record.shape
    width = columns + LANES
    groups = columns // GROUP
    turns = groups // (homes * sharers)
    deal = -(-(-(-(PANEL + DELAYS - 1 + GROUP - 1) // GROUP)) // homes)
    each = -(-deal // sharers)
    with jax.named_scope("deal_record"):
        cards = record.reshape(turns, sharers, homes, GROUP, channels)
        cards = lax.dynamic_index_in_dim(cards, sharer, 1, keepdims=False).transpose(1, 0, 2, 3)
        store = lax.all_to_all(cards, "tm", 0, 0).reshape(homes * turns, GROUP, channels)
    rim = lax.ppermute(record[columns - LANES :], "tm", [(i, i + 1) for i in range(homes - 1)])
    vectors = share_round(eigvecs)
    begins = share_round(starts) - (DELAYS - 1)
    with jax.named_scope("column_norms"):
        energy = jnp.sum(jnp.square(record.astype(jnp.float32)), axis=1)
        edge = jnp.sum(jnp.square(rim[LANES - DELAYS + 1 :].astype(jnp.float32)), axis=1)
        norms = slant(lag_sums(jnp.concatenate([edge, energy])), width)
        fanned = fan(vectors, width)
    with jax.named_scope("hand_over"):
        first = begins // GROUP
        opening = -((home - first) // homes)
        lowest = -((sharer - opening) // sharers)
        index = lowest[:, None] + jnp.arange(each)[None, :]
        index = jnp.where((index >= 0) & (index < homes * turns), index, -1).reshape(-1)
        sent = pick(store, index.astype(jnp.int32), [sharers * SLOTS * each])[0]
        sent = sent.reshape(sharers, SLOTS * each, GROUP, channels)
        held = lax.all_to_all(sent, "panel", 0, 0).reshape(sharers * SLOTS * each, GROUP, channels)
        own_first = starts - (DELAYS - 1)
        offset = own_first % GROUP
        own_first = own_first // GROUP
        own_opening = -((home - own_first) // homes)
        step = jnp.arange(deal)[None, :]
        index = ((own_opening[:, None] + step) % sharers) * (SLOTS * each) + jnp.arange(SLOTS)[:, None] * each
        index = index + step // sharers
        shards = pick(held, index.reshape(-1).astype(jnp.int32), [deal] * SLOTS)
    order = tour(homes)
    place_of = [order.index(i) for i in range(homes)]
    place = jnp.array(place_of, jnp.int32)[home]
    ring = jnp.array(order, jnp.int32)
    scale = -1.4426950408889634 / (kernel_width * (DELAYS * channels))
    results = []
    for slot in range(SLOTS):
        own = shards[slot]
        arrived = [(0, 0, own)]
        ahead = back = own
        for hop in range(1, homes // 2):
            ahead = step_round(ahead, order, 1)
            back = step_round(back, order, -1)
            arrived += [(-hop, 0, ahead), (hop, 0, back)]
        cut = (deal + 1) // 2
        arrived.append((homes // 2, 0, step_round(ahead[:cut], order, 1)))
        arrived.append((homes // 2, cut, step_round(back[cut:], order, -1)))
        meta = []
        for hop, skipped, _ in arrived:
            source = ring[(place + hop) % homes]
            meta.append((source - own_first[slot]) % homes + homes * skipped)
        meta.append(offset[slot])
        meta = jnp.stack(meta).astype(jnp.int32)
        parts = [part for _, _, part in arrived]
        with jax.named_scope("panel"):
            partial = panel_call(homes, deal, parts, record, rim, fanned, norms, meta, scale)
        results.append(lax.all_to_all(partial, "tm", 0, 0))
    finished = []
    for result in results:
        total = jnp.sum(result, axis=0)
        rows = jnp.concatenate([total[:, 40 * part : 40 * part + MODES + 1] for part in range(3)], axis=0)
        rows = jnp.flip(rows, axis=0)
        finished.append(rows[:, :MODES] / rows[:, MODES:])
    return jnp.stack(finished)


def solution(mesh):
    placed = (P("tm", None), P(("tm", "panel"), None), P("panel"), P())
    return jax.shard_map(
        body, mesh=mesh, in_specs=placed, out_specs=P("panel", "tm", None), check_vma=False
    )
```

time: 359 us -> 189 us (0.53)
  waiting for transfers between devices: 173 us -> 33.4 us
  other arithmetic: 80.9 us -> 6.88 us
  Pallas kernels: 0 us -> 44.8 us
  starting transfers between devices: 4.92 us -> 47.1 us
  blocking collectives: 25 us -> 0 us
  matrix products: 19.7 us -> 0 us
  between operations: 15.5 us -> 28.8 us
  local copies, waits for them, and re-layouts: 38.4 us -> 26.5 us
    psum x2 -> x0, waiting for transfers between devices: 173 us -> none  [the longest x1 123 us: body(): windows = lax.psum(pieces, 'tm').astype(jnp.float32).astype(jnp.bfloat16)]
    add x9 -> x3, other arithmetic: 63.3 us -> 0.64 us  [the longest x1 0.49 us: body(): index = index + step // sharers]
    pallas_call x0 -> x4, Pallas kernels: none -> 44.8 us  [the longest x2 40.5 us: panel_call(): pl.pallas_call(lambda *refs: panel_kernel(homes, parts, *refs), out_shape...]
    ppermute x1 -> x23, starting transfers between devices: 4.88 us -> 27.5 us  [the longest x16 16.6 us: step_round(): lax.ppermute(value, 'tm', [(order[i], order[(i + way) % homes]) for i in...]
    concatenate x1 -> x19, local copies, waits for them, and re-layouts: 32.9 us -> 12.4 us  [the longest x1 6.26 us: fan(): jnp.concatenate([jnp.roll(padded, shift, axis=0) for shift in range(8)],...]
    dot_general x4 -> x0, matrix products: 19.7 us -> none  [the longest x2 17.6 us: body(): lax.dot_general(window, extended, (((1,), (1,)), ((), ())), preferred_ele...]
    all_to_all x0 -> x4, starting transfers between devices: none -> 19.6 us  [the longest x2 10.3 us: body(): results.append(lax.all_to_all(partial, 'tm', 0, 0))]
    psum x1 -> x0, blocking collectives: 19.5 us -> none  [body(): numer, total = lax.psum((numer, total), 'tm')]
  transfers between devices with their start and end apart: 3 -> 27, of which waited for: 2 -> 12; matrix products, arithmetic and copies ran while one was open for 1% -> 15% of each run, Pallas kernels for 0% -> 22%
where the time goes in v1:
time: 189 us; the launch traced here: 187 us
  starting transfers between devices  47.1 us (25%)
  Pallas kernels  44.8 us (24%)
  waiting for transfers between devices  33.4 us (18%)
  between operations  28.8 us (15%)
  local copies, waits for them, and re-layouts  26.5 us (14%)
  other arithmetic  6.88 us (4%)
    pallas_call x2, Pallas kernels, panel_call(): pl.pallas_call(lambda *refs: panel_kernel(homes, parts, *refs), out_shape...  40.5 us
    ppermute x16, waiting for transfers between devices, step_round(): lax.ppermute(value, 'tm', [(order[i], order[(i + way) % homes]) for i in...  17.8 us
    ppermute x16, starting transfers between devices, step_round(): lax.ppermute(value, 'tm', [(order[i], order[(i + way) % homes]) for i in...  16.6 us
    all_to_all x2, starting transfers between devices, body(): results.append(lax.all_to_all(partial, 'tm', 0, 0))  10.3 us
    all_to_all x1, waiting for transfers between devices, body(): lax.all_to_all(sent, 'panel', 0, 0)  8.66 us
    all_to_all x2, waiting for transfers between devices, body(): results.append(lax.all_to_all(partial, 'tm', 0, 0))  6.83 us
    concatenate x1, local copies, waits for them, and re-layouts, fan(): jnp.concatenate([jnp.roll(padded, shift, axis=0) for shift in range(8)],...  6.26 us
    ppermute x6, starting transfers between devices, share_round(): lax.ppermute(value, 'panel', [((i + hop) % sharers, i) for i in range(sha...  6.21 us
  transfers between devices with their start and end apart: 27, of which 12 were waited for; matrix products, arithmetic and copies ran while one was open for 15% of the time, Pallas kernels for 22%

profile of v1, /device:TPU:0, one launch (start us, length us, event | category | flops | bytes accessed | tf_op | source)
XLA Modules:
  0.0 187.4 jit_solution(307046892590661137)
XLA Ops:
  0.0 2.4 %collective-permute-start.1 = (bf16[512,32]{0,1:T(8,128)(2,1)}, bf16[512,32]{0,1:T(8,128)(2,1)S(1)}, u32[]{:S(2)}, u32[]{:S(2)}) collective-permute-start(bf16[512,32]{0,1:T(8,128)(2,1)} %param.7), channel_id=1, source_target_pairs={{1,0},{2,1},{3,2},{0,3},{5,4},{6,5},{7,6},{4,7},{9,8},{10,9},{11,1... | collective-permute-start | bytes 98312 | tf_op jit(solution)/shard_map/ppermute | solution.py:191
  3.3 1.6 collective-permute-start.4
  4.8 1.4 collective-permute-start.5
  6.2 2.3 %copy_bitcast_fusion = bf16[8,4,16,1024]{3,2,1,0:T(8,128)(2,1)} fusion(bf16[4,4,8,16,1024]{4,3,2,1,0:T(8,128)(2,1)} %bitcast.49, s32[]{:T(128)S(6)} %select_n.260), kind=kLoop, calls=%fused_computation.1 | loop fusion | bytes 2097156 | tf_op jit(solution)/shard_map/deal_record/transpose | solution.py:215
  8.6 5.8 %all-to-all-start = ((bf16[8,4,16,1024]{3,2,1,0:T(8,128)(2,1)}), bf16[8,4,16,1024]{3,2,1,0:T(8,128)(2,1)S(1)}, u32[]{:S(2)}, u32[]{:S(2)}) async-start(bf16[8,4,16,1024]{3,2,1,0:T(8,128)(2,1)} %copy_bitcast_fusion), calls=%async_computation | async-start | bytes 2097152 | tf_op jit(solution)/shard_map/deal_record/all_to_all | solution.py:216
  33.7 3.1 %multiply_reduce_fusion = f32[2048]{0:T(1024)S(1)} fusion(bf16[2048,1024]{1,0:T(8,128)(2,1)} %refs_2_.3), kind=kLoop, calls=%fused_computation | loop fusion | flops 6289408 | bytes 4202496 | tf_op jit(solution)/shard_map/column_norms/reduce_sum | solution.py:221
  49.7 1.3 stack.105.refs_0_
  51.0 1.3 stack.125.refs_0_
  52.3 4.6 %collective-permute-start = (bf16[128,1024]{1,0:T(8,128)(2,1)S(1)}, bf16[128,1024]{1,0:T(8,128)(2,1)}, u32[]{:S(2)}, u32[]{:S(2)}) collective-permute-start(bf16[128,1024]{1,0:T(8,128)(2,1)S(1)} %slice.210), channel_id=1, source_target_pairs={{0,4},{4,8},{8,12},{12,16},{16,20},{20,24},{24,28},{1,5},{5,9},{9,... | collective-permute-start | bytes 786440 | tf_op jit(solution)/shard_map/ppermute | solution.py:217
  64.5 6.3 %concatenate.89.refs_4_ = bf16[2176,256]{1,0:T(8,128)(2,1)} concatenate(bf16[2176,32]{1,0:T(8,128)(2,1)S(1)} %concatenate.81, bf16[2176,32]{1,0:T(8,128)(2,1)S(1)} %concatenate.82, bf16[2176,32]{1,0:T(8,128)(2,1)S(1)} %concatenate.83, bf16[2176,32]{1,0:T(8,128)(2,1)} %concatenate.84, bf16[2176,32]{1,0:T(8,128)(2,1)} %concatenate.85, bf16[2176,32]{1,0:T(8,128)(2,1)} %concatenate.86, ...), dimensions={1} | concatenate | bytes 2228224 | tf_op jit(solution)/shard_map/column_norms/concatenate | solution.py:137
  72.9 2.2 %hand_over.2 = bf16[16,16,1024]{2,1,0:T(8,128)(2,1)} custom-call(s32[16]{0:T(128)} %and_select_fusion.refs_0_, bf16[32,16,1024]{2,1,0:T(8,128)(2,1)} %bitcast.50), custom_call_target="tpu_custom_call" | custom-call | tf_op jit(solution)/shard_map/hand_over/pallas_call | solution.py:165
  75.1 3.5 %all-to-all-start.1 = ((bf16[4,4,16,1024]{3,2,1,0:T(8,128)(2,1)}), bf16[4,4,16,1024]{3,2,1,0:T(8,128)(2,1)S(1)}, u32[]{:S(2)}, u32[]{:S(2)}) async-start(bf16[4,4,16,1024]{3,2,1,0:T(8,128)(2,1)} %bitcast.52), calls=%async_computation.1 | async-start | bytes 1048576 | tf_op jit(solution)/shard_map/hand_over/all_to_all | solution.py:233
  78.7 8.7 %all-to-all-done.1 = bf16[4,4,16,1024]{3,2,1,0:T(8,128)(2,1)S(1)} async-done(((bf16[4,4,16,1024]{3,2,1,0:T(8,128)(2,1)}), bf16[4,4,16,1024]{3,2,1,0:T(8,128)(2,1)S(1)}, u32[]{:S(2)}, u32[]{:S(2)}) %all-to-all-start.1) | async-done | bytes 524320 | tf_op jit(solution)/shard_map/hand_over/all_to_all | solution.py:233
  88.2 2.0 %hand_over.3 = (bf16[7,16,1024]{2,1,0:T(8,128)(2,1)}, bf16[7,16,1024]{2,1,0:T(8,128)(2,1)}) custom-call(s32[14]{0:T(128)} %fusion.3.refs_0_, bf16[16,16,1024]{2,1,0:T(8,128)(2,1)} %bitcast.51), custom_call_target="tpu_custom_call" | custom-call | tf_op jit(solution)/shard_map/hand_over/pallas_call | solution.py:165
  91.0 1.3 collective-permute-start.8
  93.1 1.3 collective-permute-start.16
  94.4 4.5 %collective-permute-done.7.refs_7_ = bf16[7,16,1024]{2,1,0:T(8,128)(2,1)S(1)} collective-permute-done((bf16[7,16,1024]{2,1,0:T(8,128)(2,1)}, bf16[7,16,1024]{2,1,0:T(8,128)(2,1)S(1)}, u32[]{:S(2)}, u32[]{:S(2)}) %collective-permute-start.7) | collective-permute-done | bytes 229408 | tf_op jit(solution)/shard_map/ppermute | solution.py:199
  99.8 1.3 collective-permute-start.10
  101.1 2.8 %collective-permute-done.15.refs_7_ = bf16[7,16,1024]{2,1,0:T(8,128)(2,1)S(1)} collective-permute-done((bf16[7,16,1024]{2,1,0:T(8,128)(2,1)}, bf16[7,16,1024]{2,1,0:T(8,128)(2,1)S(1)}, u32[]{:S(2)}, u32[]{:S(2)}) %collective-permute-start.15) | collective-permute-done | bytes 229408 | tf_op jit(solution)/shard_map/ppermute | solution.py:199
  104.7 1.3 collective-permute-start.18
  106.0 2.8 %collective-permute-done.9.refs_9_ = bf16[7,16,1024]{2,1,0:T(8,128)(2,1)S(1)} collective-permute-done((bf16[7,16,1024]{2,1,0:T(8,128)(2,1)S(1)}, bf16[7,16,1024]{2,1,0:T(8,128)(2,1)S(1)}, u32[]{:S(2)}, u32[]{:S(2)}) %collective-permute-start.9) | collective-permute-done | bytes 229408 | tf_op jit(solution)/shard_map/ppermute | solution.py:199
  110.9 2.8 %collective-permute-done.17.refs_9_ = bf16[7,16,1024]{2,1,0:T(8,128)(2,1)S(1)} collective-permute-done((bf16[7,16,1024]{2,1,0:T(8,128)(2,1)S(1)}, bf16[7,16,1024]{2,1,0:T(8,128)(2,1)S(1)}, u32[]{:S(2)}, u32[]{:S(2)}) %collective-permute-start.17) | collective-permute-done | bytes 229408 | tf_op jit(solution)/shard_map/ppermute | solution.py:199
  114.5 1.3 collective-permute-start.20
  115.8 2.8 %collective-permute-done.11.refs_11_ = bf16[7,16,1024]{2,1,0:T(8,128)(2,1)S(1)} collective-permute-done((bf16[7,16,1024]{2,1,0:T(8,128)(2,1)S(1)}, bf16[7,16,1024]{2,1,0:T(8,128)(2,1)S(1)}, u32[]{:S(2)}, u32[]{:S(2)}) %collective-permute-start.11) | collective-permute-done | bytes 229408 | tf_op jit(solution)/shard_map/ppermute | solution.py:199
  120.0 1.3 collective-permute-start.14
  122.1 1.4 collective-permute-done.19.refs_11_
  124.4 1.5 collective-permute-start.22
  127.0 20.3 %panel.2 = f32[8,32,128]{2,1,0:T(8,128)} custom-call(s32[10]{0:T(128)} %stack.105.refs_0_, f32[1]{0:T(128)S(6)} %div.89.refs_1_, bf16[2048,1024]{1,0:T(8,128)(2,1)} %refs_2_.3, bf16[128,1024]{1,0:T(8,128)(2,1)} %collective-permute-done.refs_3_, bf16[2176,256]{1,0:T(8,128)(2,1)} %concatenate.89.refs_4_, f32[8,2176]{1,0:T(8,128)} %stack.114.refs_5_, ...), custom_call_target="tpu_custom_call" | custom-call | flops 3779067904 | bytes 8000000 | tf_op jit(solution)/shard_map/panel/pallas_call | solution.py:115
  147.3 4.3 %all-to-all-start.2 = ((f32[8,32,128]{2,1,0:T(8,128)}), f32[8,32,128]{2,1,0:T(8,128)S(1)}, u32[]{:S(2)}, u32[]{:S(2)}) async-start(f32[8,32,128]{2,1,0:T(8,128)} %panel.2), calls=%async_computation.2 | async-start | bytes 262144 | tf_op jit(solution)/shard_map/all_to_all | solution.py:268
  152.3 20.3 %panel.3 = f32[8,32,128]{2,1,0:T(8,128)} custom-call(s32[10]{0:T(128)} %stack.125.refs_0_, f32[1]{0:T(128)S(6)} %div.89.refs_1_, bf16[2048,1024]{1,0:T(8,128)(2,1)} %refs_2_.3, bf16[128,1024]{1,0:T(8,128)(2,1)} %collective-permute-done.refs_3_, bf16[2176,256]{1,0:T(8,128)(2,1)} %concatenate.89.refs_4_, f32[8,2176]{1,0:T(8,128)} %stack.114.refs_5_, ...), custom_call_target="tpu_custom_call" | custom-call | flops 3779067904 | bytes 8000000 | tf_op jit(solution)/shard_map/panel/pallas_call | solution.py:115
  172.5 6.0 %all-to-all-start.3 = ((f32[8,32,128]{2,1,0:T(8,128)}), f32[8,32,128]{2,1,0:T(8,128)S(1)}, u32[]{:S(2)}, u32[]{:S(2)}) async-start(f32[8,32,128]{2,1,0:T(8,128)} %panel.3), calls=%async_computation.3 | async-start | bytes 262144 | tf_op jit(solution)/shard_map/all_to_all | solution.py:268
  179.1 6.8 %all-to-all-done.3 = f32[8,32,128]{2,1,0:T(8,128)S(1)} async-done(((f32[8,32,128]{2,1,0:T(8,128)}), f32[8,32,128]{2,1,0:T(8,128)S(1)}, u32[]{:S(2)}, u32[]{:S(2)}) %all-to-all-start.3) | async-done | bytes 131104 | tf_op jit(solution)/shard_map/all_to_all | solution.py:268
  (173 shorter events, 28.3 us)
Async XLA Ops:
  0.0 32.6 %copy-start.2 = (bf16[512,32]{0,1:T(8,128)(2,1)S(1)}, bf16[512,32]{0,1:T(8,128)(2,1)}, u32[]{:S(2)}) copy-start(bf16[512,32]{0,1:T(8,128)(2,1)} %param.7) | copy-start | bytes 98308
  0.0 57.8 %collective-permute-start.1 = (bf16[512,32]{0,1:T(8,128)(2,1)}, bf16[512,32]{0,1:T(8,128)(2,1)S(1)}, u32[]{:S(2)}, u32[]{:S(2)}) collective-permute-start(bf16[512,32]{0,1:T(8,128)(2,1)} %param.7), channel_id=1, source_target_pairs={{1,0},{2,1},{3,2},{0,3},{5,4},{6,5},{7,6},{4,7},{9,8},{10,9},{11,1... | collective-permute-start | bytes 98312 | tf_op jit(solution)/shard_map/ppermute | solution.py:191
  2.4 55.3 %collective-permute-start.2 = (bf16[512,32]{0,1:T(8,128)(2,1)}, bf16[512,32]{0,1:T(8,128)(2,1)S(1)}, u32[]{:S(2)}, u32[]{:S(2)}) collective-permute-start(bf16[512,32]{0,1:T(8,128)(2,1)} %param.7), channel_id=1, source_target_pairs={{2,0},{3,1},{0,2},{1,3},{6,4},{7,5},{4,6},{5,7},{10,8},{11,9},{8,1... | collective-permute-start | bytes 98312 | tf_op jit(solution)/shard_map/ppermute | solution.py:191
  3.1 54.7 %collective-permute-start.3 = (bf16[512,32]{0,1:T(8,128)(2,1)}, bf16[512,32]{0,1:T(8,128)(2,1)S(1)}, u32[]{:S(2)}, u32[]{:S(2)}) collective-permute-start(bf16[512,32]{0,1:T(8,128)(2,1)} %param.7), channel_id=1, source_target_pairs={{3,0},{0,1},{1,2},{2,3},{7,4},{4,5},{5,6},{6,7},{11,8},{8,9},{9,10... | collective-permute-start | bytes 98312 | tf_op jit(solution)/shard_map/ppermute | solution.py:191
  3.3 49.0 %collective-permute-start.4 = (s32[2]{0:T(128)}, s32[2]{0:T(128)S(1)}, u32[]{:S(2)}, u32[]{:S(2)}) collective-permute-start(s32[2]{0:T(128)} %param.8), channel_id=1, source_target_pairs={{1,0},{2,1},{3,2},{0,3},{5,4},{6,5},{7,6},{4,7},{9,8},{10,9},{11,1... | collective-permute-start | bytes 32 | tf_op jit(solution)/shard_map/ppermute | solution.py:191
  4.8 47.4 %collective-permute-start.5 = (s32[2]{0:T(128)}, s32[2]{0:T(128)S(1)}, u32[]{:S(2)}, u32[]{:S(2)}) collective-permute-start(s32[2]{0:T(128)} %param.8), channel_id=1, source_target_pairs={{2,0},{3,1},{0,2},{1,3},{6,4},{7,5},{4,6},{5,7},{10,8},{11,9},{8,1... | collective-permute-start | bytes 32 | tf_op jit(solution)/shard_map/ppermute | solution.py:191
  8.6 63.3 %all-to-all-start = ((bf16[8,4,16,1024]{3,2,1,0:T(8,128)(2,1)}), bf16[8,4,16,1024]{3,2,1,0:T(8,128)(2,1)S(1)}, u32[]{:S(2)}, u32[]{:S(2)}) async-start(bf16[8,4,16,1024]{3,2,1,0:T(8,128)(2,1)} %copy_bitcast_fusion), calls=%async_computation | async-start | bytes 2097152 | tf_op jit(solution)/shard_map/deal_record/all_to_all | solution.py:216
  52.3 4.7 %collective-permute-start.6 = (s32[2]{0:T(128)S(1)}, s32[2]{0:T(128)S(1)}, u32[]{:S(2)}, u32[]{:S(2)}) collective-permute-start(s32[2]{0:T(128)S(1)} %copy-done.8), channel_id=1, source_target_pairs={{3,0},{0,1},{1,2},{2,3},{7,4},{4,5},{5,6},{6,7},{11,8},{8,9},{9,10... | collective-permute-start | bytes 32 | tf_op jit(solution)/shard_map/ppermute | solution.py:191
  52.3 18.5 %collective-permute-start = (bf16[128,1024]{1,0:T(8,128)(2,1)S(1)}, bf16[128,1024]{1,0:T(8,128)(2,1)}, u32[]{:S(2)}, u32[]{:S(2)}) collective-permute-start(bf16[128,1024]{1,0:T(8,128)(2,1)S(1)} %slice.210), channel_id=1, source_target_pairs={{0,4},{4,8},{8,12},{12,16},{16,20},{20,24},{24,28},{1,5},{5,9},{9,... | collective-permute-start | bytes 786440 | tf_op jit(solution)/shard_map/ppermute | solution.py:217
  75.1 12.3 %all-to-all-start.1 = ((bf16[4,4,16,1024]{3,2,1,0:T(8,128)(2,1)}), bf16[4,4,16,1024]{3,2,1,0:T(8,128)(2,1)S(1)}, u32[]{:S(2)}, u32[]{:S(2)}) async-start(bf16[4,4,16,1024]{3,2,1,0:T(8,128)(2,1)} %bitcast.52), calls=%async_computation.1 | async-start | bytes 1048576 | tf_op jit(solution)/shard_map/hand_over/all_to_all | solution.py:233
  90.2 8.7 %collective-permute-start.7 = (bf16[7,16,1024]{2,1,0:T(8,128)(2,1)}, bf16[7,16,1024]{2,1,0:T(8,128)(2,1)S(1)}, u32[]{:S(2)}, u32[]{:S(2)}) collective-permute-start(bf16[7,16,1024]{2,1,0:T(8,128)(2,1)} %get-tuple-element.7.refs_6_), channel_id=1, source_target_pairs={{0,8},{8,16},{16,24},{24,28},{28,20},{20,12},{12,4},{4,0},{1,9},{9... | collective-permute-start | bytes 688136 | tf_op jit(solution)/shard_map/ppermute | solution.py:199
  91.0 8.8 %collective-permute-start.8 = (bf16[7,16,1024]{2,1,0:T(8,128)(2,1)}, bf16[7,16,1024]{2,1,0:T(8,128)(2,1)S(1)}, u32[]{:S(2)}, u32[]{:S(2)}) collective-permute-start(bf16[7,16,1024]{2,1,0:T(8,128)(2,1)} %get-tuple-element.7.refs_6_), channel_id=1, source_target_pairs={{0,4},{8,0},{16,8},{24,16},{28,24},{20,28},{12,20},{4,12},{1,5},{9... | collective-permute-start | bytes 688136 | tf_op jit(solution)/shard_map/ppermute | solution.py:199
  92.4 11.5 %collective-permute-start.15 = (bf16[7,16,1024]{2,1,0:T(8,128)(2,1)}, bf16[7,16,1024]{2,1,0:T(8,128)(2,1)S(1)}, u32[]{:S(2)}, u32[]{:S(2)}) collective-permute-start(bf16[7,16,1024]{2,1,0:T(8,128)(2,1)} %get-tuple-element.8.refs_6_), channel_id=1, source_target_pairs={{0,8},{8,16},{16,24},{24,28},{28,20},{20,12},{12,4},{4,0},{1,9},{9... | collective-permute-start | bytes 688136 | tf_op jit(solution)/shard_map/ppermute | solution.py:199
  93.1 11.6 %collective-permute-start.16 = (bf16[7,16,1024]{2,1,0:T(8,128)(2,1)}, bf16[7,16,1024]{2,1,0:T(8,128)(2,1)S(1)}, u32[]{:S(2)}, u32[]{:S(2)}) collective-permute-start(bf16[7,16,1024]{2,1,0:T(8,128)(2,1)} %get-tuple-element.8.refs_6_), channel_id=1, source_target_pairs={{0,4},{8,0},{16,8},{24,16},{28,24},{20,28},{12,20},{4,12},{1,5},{9... | collective-permute-start | bytes 688136 | tf_op jit(solution)/shard_map/ppermute | solution.py:199
  98.9 9.8 %collective-permute-start.9 = (bf16[7,16,1024]{2,1,0:T(8,128)(2,1)S(1)}, bf16[7,16,1024]{2,1,0:T(8,128)(2,1)S(1)}, u32[]{:S(2)}, u32[]{:S(2)}) collective-permute-start(bf16[7,16,1024]{2,1,0:T(8,128)(2,1)S(1)} %collective-permute-done.7.refs_7_), channel_id=1, source_target_pairs={{0,8},{8,16},{16,24},{24,28},{28,20},{20,12},{12,4},{4,0},{1,9},{9... | collective-permute-start | bytes 688136 | tf_op jit(solution)/shard_map/ppermute | solution.py:199
  99.8 9.8 %collective-permute-start.10 = (bf16[7,16,1024]{2,1,0:T(8,128)(2,1)S(1)}, bf16[7,16,1024]{2,1,0:T(8,128)(2,1)S(1)}, u32[]{:S(2)}, u32[]{:S(2)}) collective-permute-start(bf16[7,16,1024]{2,1,0:T(8,128)(2,1)S(1)} %collective-permute-done.8.refs_8_), channel_id=1, source_target_pairs={{0,4},{8,0},{16,8},{24,16},{28,24},{20,28},{12,20},{4,12},{1,5},{9... | collective-permute-start | bytes 688136 | tf_op jit(solution)/shard_map/ppermute | solution.py:199
  103.8 43.4 %copy-start.9 = (bf16[7,16,1024]{2,1,0:T(8,128)(2,1)}, bf16[7,16,1024]{2,1,0:T(8,128)(2,1)S(1)}, u32[]{:S(2)}) copy-start(bf16[7,16,1024]{2,1,0:T(8,128)(2,1)S(1)} %collective-permute-done.15.refs_7_) | copy-start | bytes 688132
  103.9 9.8 %collective-permute-start.17 = (bf16[7,16,1024]{2,1,0:T(8,128)(2,1)S(1)}, bf16[7,16,1024]{2,1,0:T(8,128)(2,1)S(1)}, u32[]{:S(2)}, u32[]{:S(2)}) collective-permute-start(bf16[7,16,1024]{2,1,0:T(8,128)(2,1)S(1)} %collective-permute-done.15.refs_7_), channel_id=1, source_target_pairs={{0,8},{8,16},{16,24},{24,28},{28,20},{20,12},{12,4},{4,0},{1,9},{9... | collective-permute-start | bytes 688136 | tf_op jit(solution)/shard_map/ppermute | solution.py:199
  104.7 42.6 %copy-start.10 = (bf16[7,16,1024]{2,1,0:T(8,128)(2,1)}, bf16[7,16,1024]{2,1,0:T(8,128)(2,1)S(1)}, u32[]{:S(2)}) copy-start(bf16[7,16,1024]{2,1,0:T(8,128)(2,1)S(1)} %collective-permute-done.16.refs_8_) | copy-start | bytes 688132
  104.7 9.8 %collective-permute-start.18 = (bf16[7,16,1024]{2,1,0:T(8,128)(2,1)S(1)}, bf16[7,16,1024]{2,1,0:T(8,128)(2,1)S(1)}, u32[]{:S(2)}, u32[]{:S(2)}) collective-permute-start(bf16[7,16,1024]{2,1,0:T(8,128)(2,1)S(1)} %collective-permute-done.16.refs_8_), channel_id=1, source_target_pairs={{0,4},{8,0},{16,8},{24,16},{28,24},{20,28},{12,20},{4,12},{1,5},{9... | collective-permute-start | bytes 688136 | tf_op jit(solution)/shard_map/ppermute | solution.py:199
  108.8 9.8 %collective-permute-start.11 = (bf16[7,16,1024]{2,1,0:T(8,128)(2,1)S(1)}, bf16[7,16,1024]{2,1,0:T(8,128)(2,1)S(1)}, u32[]{:S(2)}, u32[]{:S(2)}) collective-permute-start(bf16[7,16,1024]{2,1,0:T(8,128)(2,1)S(1)} %collective-permute-done.9.refs_9_), channel_id=1, source_target_pairs={{0,8},{8,16},{16,24},{24,28},{28,20},{20,12},{12,4},{4,0},{1,9},{9... | collective-permute-start | bytes 688136 | tf_op jit(solution)/shard_map/ppermute | solution.py:199
  109.6 10.3 %collective-permute-start.12 = (bf16[7,16,1024]{2,1,0:T(8,128)(2,1)S(1)}, bf16[7,16,1024]{2,1,0:T(8,128)(2,1)S(1)}, u32[]{:S(2)}, u32[]{:S(2)}) collective-permute-start(bf16[7,16,1024]{2,1,0:T(8,128)(2,1)S(1)} %collective-permute-done.10.refs_10_), channel_id=1, source_target_pairs={{0,4},{8,0},{16,8},{24,16},{28,24},{20,28},{12,20},{4,12},{1,5},{9... | collective-permute-start | bytes 688136 | tf_op jit(solution)/shard_map/ppermute | solution.py:199
  113.7 38.0 %copy-start.13 = (bf16[7,16,1024]{2,1,0:T(8,128)(2,1)}, bf16[7,16,1024]{2,1,0:T(8,128)(2,1)S(1)}, u32[]{:S(2)}) copy-start(bf16[7,16,1024]{2,1,0:T(8,128)(2,1)S(1)} %collective-permute-done.17.refs_9_) | copy-start | bytes 688132
  113.7 9.8 %collective-permute-start.19 = (bf16[7,16,1024]{2,1,0:T(8,128)(2,1)S(1)}, bf16[7,16,1024]{2,1,0:T(8,128)(2,1)S(1)}, u32[]{:S(2)}, u32[]{:S(2)}) collective-permute-start(bf16[7,16,1024]{2,1,0:T(8,128)(2,1)S(1)} %collective-permute-done.17.refs_9_), channel_id=1, source_target_pairs={{0,8},{8,16},{16,24},{24,28},{28,20},{20,12},{12,4},{4,0},{1,9},{9... | collective-permute-start | bytes 688136 | tf_op jit(solution)/shard_map/ppermute | solution.py:199
  114.5 37.1 %copy-start.14 = (bf16[7,16,1024]{2,1,0:T(8,128)(2,1)}, bf16[7,16,1024]{2,1,0:T(8,128)(2,1)S(1)}, u32[]{:S(2)}) copy-start(bf16[7,16,1024]{2,1,0:T(8,128)(2,1)S(1)} %collective-permute-done.18.refs_10_) | copy-start | bytes 688132
  114.5 9.8 %collective-permute-start.20 = (bf16[7,16,1024]{2,1,0:T(8,128)(2,1)S(1)}, bf16[7,16,1024]{2,1,0:T(8,128)(2,1)S(1)}, u32[]{:S(2)}, u32[]{:S(2)}) collective-permute-start(bf16[7,16,1024]{2,1,0:T(8,128)(2,1)S(1)} %collective-permute-done.18.refs_10_), channel_id=1, source_target_pairs={{0,4},{8,0},{16,8},{24,16},{28,24},{20,28},{12,20},{4,12},{1,5},{9... | collective-permute-start | bytes 688136 | tf_op jit(solution)/shard_map/ppermute | solution.py:199
  118.6 7.7 %collective-permute-start.13 = (bf16[4,16,1024]{2,1,0:T(8,128)(2,1)S(1)}, bf16[4,16,1024]{2,1,0:T(8,128)(2,1)S(1)}, u32[]{:S(2)}, u32[]{:S(2)}) collective-permute-start(bf16[4,16,1024]{2,1,0:T(8,128)(2,1)S(1)} %slice.271), channel_id=1, source_target_pairs={{0,8},{8,16},{16,24},{24,28},{28,20},{20,12},{12,4},{4,0},{1,9},{9... | collective-permute-start | bytes 393224 | tf_op jit(solution)/shard_map/ppermute | solution.py:199
  120.0 5.9 %collective-permute-start.14 = (bf16[3,16,1024]{2,1,0:T(8,128)(2,1)S(1)}, bf16[3,16,1024]{2,1,0:T(8,128)(2,1)}, u32[]{:S(2)}, u32[]{:S(2)}) collective-permute-start(bf16[3,16,1024]{2,1,0:T(8,128)(2,1)S(1)} %slice.272), channel_id=1, source_target_pairs={{0,4},{8,0},{16,8},{24,16},{28,24},{20,28},{12,20},{4,12},{1,5},{9... | collective-permute-start | bytes 294920 | tf_op jit(solution)/shard_map/ppermute | solution.py:199
  123.5 28.1 %collective-permute-start.21 = (bf16[4,16,1024]{2,1,0:T(8,128)(2,1)S(1)}, bf16[4,16,1024]{2,1,0:T(8,128)(2,1)}, u32[]{:S(2)}, u32[]{:S(2)}) collective-permute-start(bf16[4,16,1024]{2,1,0:T(8,128)(2,1)S(1)} %slice.277), channel_id=1, source_target_pairs={{0,8},{8,16},{16,24},{24,28},{28,20},{20,12},{12,4},{4,0},{1,9},{9... | collective-permute-start | bytes 393224 | tf_op jit(solution)/shard_map/ppermute | solution.py:199
  124.4 27.3 %collective-permute-start.22 = (bf16[3,16,1024]{2,1,0:T(8,128)(2,1)S(1)}, bf16[3,16,1024]{2,1,0:T(8,128)(2,1)S(1)}, u32[]{:S(2)}, u32[]{:S(2)}) collective-permute-start(bf16[3,16,1024]{2,1,0:T(8,128)(2,1)S(1)} %slice.278), channel_id=1, source_target_pairs={{0,4},{8,0},{16,8},{24,16},{28,24},{20,28},{12,20},{4,12},{1,5},{9... | collective-permute-start | bytes 294920 | tf_op jit(solution)/shard_map/ppermute | solution.py:199
  147.3 25.2 %all-to-all-start.2 = ((f32[8,32,128]{2,1,0:T(8,128)}), f32[8,32,128]{2,1,0:T(8,128)S(1)}, u32[]{:S(2)}, u32[]{:S(2)}) async-start(f32[8,32,128]{2,1,0:T(8,128)} %panel.2), calls=%async_computation.2 | async-start | bytes 262144 | tf_op jit(solution)/shard_map/all_to_all | solution.py:268
  172.5 13.3 %all-to-all-start.3 = ((f32[8,32,128]{2,1,0:T(8,128)}), f32[8,32,128]{2,1,0:T(8,128)S(1)}, u32[]{:S(2)}, u32[]{:S(2)}) async-start(f32[8,32,128]{2,1,0:T(8,128)} %panel.3), calls=%async_computation.3 | async-start | bytes 262144 | tf_op jit(solution)/shard_map/all_to_all | solution.py:268
  (15 other events, 209.9 us)

commit v2 on v1

v2 whole, which is shorter than its diff:
```python
import jax
import jax.numpy as jnp
from jax import lax
from jax.experimental import pallas as pl
from jax.experimental.pallas import tpu as pltpu
from jax.sharding import PartitionSpec as P

DELAYS = 64
PANEL = 768
SLOTS = 2
GROUP = 16
LANES = 128
MODES = 32
BIG = 1e30


def panel_kernel(homes, slot, places, starts, scale, record, rim, vectors, norms, *rest):
    parts = len(places)
    shards = rest[:parts]
    out, window, turned, gram, strips, weights, sums, result = rest[parts:]
    columns = record.shape[0]
    width = columns + LANES
    tiles = width // LANES
    rows = window.shape[0]
    used = turned.shape[0]
    kept = used - DELAYS
    modes = MODES
    position = ring_position(homes)
    for number, (hop, skipped, deal) in enumerate(places):
        chunk = lax.rem(position + (hop % homes), homes)
        for step in range(shards[number].shape[0]):
            place = pl.multiple_of((chunk * deal + (skipped + step)) * GROUP, GROUP)
            window[pl.ds(place, GROUP), :] = shards[number][step]
    low = 0
    while low < used:
        count = min(LANES, used - low)
        turn = lax.broadcasted_iota(jnp.int32, (count, count), 0) + lax.broadcasted_iota(jnp.int32, (count, count), 1)
        flip = jnp.where(turn == count - 1, 2.0, 0.0).astype(jnp.bfloat16)
        block = jnp.dot(flip, window[used - low - count : used - low, :], preferred_element_type=jnp.float32)
        turned[low : low + count, :] = block.astype(jnp.bfloat16)
        energy = jnp.sum(block * block, axis=1, keepdims=True) * 0.25
        strips[tiles, low : low + count, :] = jnp.broadcast_to(energy, (count, LANES))
        low += count
    low = 0
    while low < used:
        count = min(LANES, used - low)
        block = turned[low : low + count, :]
        gram[:count, :columns] = lax.dot_general(
            block, record[...], (((1,), (1,)), ((), ())), preferred_element_type=jnp.float32
        )
        gram[:count, columns:] = lax.dot_general(
            block, rim[...], (((1,), (1,)), ((), ())), preferred_element_type=jnp.float32
        )
        for row in range(0, count, 8):
            line = pltpu.roll(gram[row : row + 8, :], (low + row) % width, 1, stride=1, stride_axis=0)
            for tile in range(tiles):
                strips[tile, low + row : low + row + 8, :] = line[:, tile * LANES : (tile + 1) * LANES]
        low += count

    def add_lags(tile, carry):
        value = strips[tile]
        stride = 1
        while stride < DELAYS:
            value = value[stride:] + value[:-stride]
            stride *= 2
        strips[tile, DELAYS:used, :] = value[1:]
        return carry

    lax.fori_loop(0, tiles + 1, add_lags, 0)
    factor = scale[0]
    for row in range(DELAYS, used, 16):
        halves = []
        for part in range(2):
            at = row + 8 * part
            line = jnp.concatenate([strips[tile, at : at + 8, :] for tile in range(tiles)], axis=1)
            line = pltpu.roll(line, (DELAYS - 1 - at) % width, 1)
            own = jnp.concatenate([strips[tiles, at : at + 8, :]] * tiles, axis=1)
            value = jnp.exp2(((own + norms[...]) - line) * factor)
            total = value[:, :LANES]
            for tile in range(1, tiles):
                total = total + value[:, tile * LANES : (tile + 1) * LANES]
            sums[at - DELAYS : at - DELAYS + 8, :] = total
            halves.append(value)
        weights[row - DELAYS : row - DELAYS + 16, :] = jnp.concatenate(halves, axis=0).astype(jnp.bfloat16)
    product = jnp.dot(weights[...], vectors[...], preferred_element_type=jnp.float32)
    lane = lax.broadcasted_iota(jnp.int32, (kept, 2 * LANES), 1)
    sub = lax.broadcasted_iota(jnp.int32, (kept, 2 * LANES), 0)
    product = jnp.where(lane // modes == sub % 8, product, 0.0)
    product = product[:, :LANES] + product[:, LANES:]
    product = product + pltpu.roll(product, 64, 1)
    product = product + pltpu.roll(product, 32, 1)
    lane = lax.broadcasted_iota(jnp.int32, (kept, LANES), 1)
    total = jnp.sum(sums[...], axis=1, keepdims=True)
    product = jnp.where(lane == modes, total, product)
    result[...] = jnp.where(lane <= modes, product, 0.0)
    share = PANEL // homes
    third = share // 3
    offset = lax.bitwise_and(starts[slot] - (DELAYS - 1), GROUP - 1)
    for home in range(homes):
        start = kept - share * (home + 1) - offset
        packed = result[pl.ds(start, third), :]
        for part in range(1, 3):
            packed = packed + pltpu.roll(result[pl.ds(start + part * third, third), :], 40 * part, 1)
        out[home] = packed


def panel_call(homes, slot, arrived, record, rim, vectors, norms, starts, scale):
    deal = arrived[0][2].shape[0]
    parts = len(arrived)
    places = [(hop, skipped, deal) for hop, skipped, _ in arrived]
    shards = [part for _, _, part in arrived]
    columns = record.shape[0]
    width = columns + LANES
    tiles = width // LANES
    used = -(-(PANEL + DELAYS - 1 + GROUP - 1) // GROUP) * GROUP
    kept = used - DELAYS
    share = PANEL // homes
    vm = pl.BlockSpec(memory_space=pltpu.VMEM)
    sm = pl.BlockSpec(memory_space=pltpu.SMEM)
    return pl.pallas_call(
        lambda *refs: panel_kernel(homes, slot, places, *refs),
        out_shape=jax.ShapeDtypeStruct((homes, share // 3, LANES), jnp.float32),
        in_specs=[sm, sm] + [vm] * (4 + parts),
        out_specs=vm,
        scratch_shapes=[
            pltpu.VMEM((homes * deal * GROUP, record.shape[1]), jnp.bfloat16),
            pltpu.VMEM((used, record.shape[1]), jnp.bfloat16),
            pltpu.VMEM((LANES, width), jnp.float32),
            pltpu.VMEM((tiles + 1, used, LANES), jnp.float32),
            pltpu.VMEM((kept, width), jnp.bfloat16),
            pltpu.VMEM((kept, LANES), jnp.float32),
            pltpu.VMEM((kept, LANES), jnp.float32),
        ],
        compiler_params=pltpu.CompilerParams(vmem_limit_bytes=56 * 1024 * 1024),
        cost_estimate=pl.CostEstimate(flops=2 * used * width * record.shape[1], bytes_accessed=8_000_000, transcendentals=kept * width),
    )(starts, scale, record, rim, vectors, norms, *shards)


def ring_position(homes):
    home = lax.axis_index("tm")
    if homes != 8:
        return home
    return jnp.where(lax.bitwise_and(home, 1) == 0, home, 2 * homes - 1 - home) // 2


def tour(homes):
    if homes != 8:
        return list(range(homes))
    return [0, 2, 4, 6, 7, 5, 3, 1]


def step_round(value, way):
    homes = lax.axis_size("tm")
    order = tour(homes)
    return lax.ppermute(value, "tm", [(order[i], order[(i + way) % homes]) for i in range(homes)])


def own_kernel(homes, deal, starts, record, *outs):
    home = lax.axis_index("tm")
    position = ring_position(homes)
    held = record.shape[0] // GROUP
    for slot in range(SLOTS):
        first = lax.shift_right_arithmetic(starts[slot] - (DELAYS - 1), 4) - home * held
        for hop in range(homes):
            out = outs[slot * homes + hop]
            chunk = lax.rem(position + hop, homes)
            for step in range(deal):
                group = first + chunk * deal + step
                inside = (group >= 0) & (group < held)

                @pl.when(inside)
                def _():
                    out[step] = record[pl.ds(pl.multiple_of(group * GROUP, GROUP), GROUP), :]

                @pl.when(jnp.logical_not(inside))
                def _():
                    out[step] = jnp.zeros(out.shape[1:], out.dtype)


def own_rows(homes, deal, starts, record):
    vm = pl.BlockSpec(memory_space=pltpu.VMEM)
    sm = pl.BlockSpec(memory_space=pltpu.SMEM)
    shape = jax.ShapeDtypeStruct((deal, GROUP, record.shape[1]), record.dtype)
    flat = pl.pallas_call(
        lambda *refs: own_kernel(homes, deal, *refs),
        out_shape=[shape] * (SLOTS * homes),
        in_specs=[sm, vm],
        out_specs=[vm] * (SLOTS * homes),
        compiler_params=pltpu.CompilerParams(vmem_limit_bytes=40 * 1024 * 1024),
    )(starts, record)
    return [flat[slot * homes : (slot + 1) * homes] for slot in range(SLOTS)]


def prepare_kernel(record, rim, *rest):
    pieces = rest[:-4]
    norms, fanned, energy, spread = rest[-4:]
    columns = record.shape[0]
    width = columns + LANES
    sharers = len(pieces)
    sharer = lax.axis_index("panel")
    for source, low, high in ((record, 0, columns), (rim, columns, width)):
        for row in range(low, high, LANES):
            value = source[row - low : row - low + LANES, :].astype(jnp.float32)
            value = value * value
            total = value[:, :LANES]
            for lane in range(LANES, value.shape[1], LANES):
                total = total + value[:, lane : lane + LANES]
            energy[:, row : row + LANES] = lax.dot_general(
                jnp.ones((8, LANES), jnp.float32),
                total,
                (((1,), (1,)), ((), ())),
                precision=lax.Precision.HIGHEST,
                preferred_element_type=jnp.float32,
            )
    value = energy[...]
    stride = 1
    while stride < DELAYS:
        value = value + pltpu.roll(value, stride, 1)
        stride *= 2
    lane = lax.broadcasted_iota(jnp.int32, (8, width), 1)
    value = jnp.where(lane < columns, value, BIG)
    norms[...] = pltpu.roll(value, 0, 1, stride=1, stride_axis=0)
    lane = lax.broadcasted_iota(jnp.int32, (MODES, LANES), 1)
    mode = lax.broadcasted_iota(jnp.int32, (MODES, LANES), 0)
    copies = jnp.where(lax.bitwise_and(lane, MODES - 1) == mode, 1.0, 0.0).astype(jnp.bfloat16)
    rows = columns // sharers
    for hop in range(sharers):
        place = pl.multiple_of(lax.rem(sharer + hop, sharers) * rows, rows)
        spread[pl.ds(place, rows), :] = jnp.dot(pieces[hop][...], copies, preferred_element_type=jnp.float32)
    spread[columns:, :] = jnp.zeros((LANES, LANES), jnp.float32)
    value = spread[...]
    block = lax.broadcasted_iota(jnp.int32, (width, LANES), 1) // MODES
    per = LANES // MODES
    for half in range(2):
        result = jnp.zeros((width, LANES), jnp.float32)
        for part in range(per):
            result = jnp.where(block == part, pltpu.roll(value, half * per + part, 0), result)
        fanned[:, half * LANES : (half + 1) * LANES] = result.astype(jnp.bfloat16)


def prepare(record, rim, pieces):
    width = record.shape[0] + LANES
    vm = pl.BlockSpec(memory_space=pltpu.VMEM)
    return pl.pallas_call(
        prepare_kernel,
        out_shape=[
            jax.ShapeDtypeStruct((8, width), jnp.float32),
            jax.ShapeDtypeStruct((width, 2 * LANES), jnp.bfloat16),
        ],
        in_specs=[vm] * (2 + len(pieces)),
        out_specs=[vm] * 2,
        scratch_shapes=[pltpu.VMEM((8, width), jnp.float32), pltpu.VMEM((width, LANES), jnp.float32)],
        compiler_params=pltpu.CompilerParams(vmem_limit_bytes=40 * 1024 * 1024),
    )(record, rim, *pieces)


def body(record, eigvecs, starts, kernel_width):
    homes = lax.axis_size("tm")
    sharers = lax.axis_size("panel")
    columns, channels = record.shape
    groups = -(-(PANEL + DELAYS - 1 + GROUP - 1) // GROUP)
    deal = -(-groups // homes)
    half = homes // 2
    cut = (deal + 1) // 2
    with jax.named_scope("own_rows"):
        chunks = own_rows(homes, deal, starts, record)
    shards = []
    for slot in range(SLOTS):
        with jax.named_scope("scatter"):
            mine = chunks[slot]
            ahead = step_round(mine[half][:cut], 1)
            back = step_round(mine[half][cut:], -1)
            ahead = mine[half - 1].at[:cut].add(ahead)
            back = mine[half + 1].at[cut:].add(back)
            for hop in range(half - 2, -1, -1):
                ahead = mine[hop] + step_round(ahead, 1)
                back = step_round(back, -1)
                back = back if hop == 0 else mine[homes - hop] + back
            shards.append(ahead + back)
    rim = lax.ppermute(record[columns - LANES :], "tm", [(i, i + 1) for i in range(homes - 1)])
    pieces = [eigvecs]
    for hop in range(1, sharers):
        pieces.append(lax.ppermute(eigvecs, "panel", [((i + hop) % sharers, i) for i in range(sharers)]))
    with jax.named_scope("prepare"):
        norms, fanned = prepare(record, rim, pieces)
    scale = -1.4426950408889634 / (kernel_width * (DELAYS * channels))
    results = []
    for slot in range(SLOTS):
        with jax.named_scope("gather"):
            ahead = back = shards[slot]
            arrived = [(0, 0, ahead)]
            for hop in range(1, half):
                ahead = step_round(ahead, 1)
                back = step_round(back, -1)
                arrived += [(-hop, 0, ahead), (hop, 0, back)]
            arrived.append((half, 0, step_round(ahead[:cut], 1)))
            arrived.append((half, cut, step_round(back[cut:], -1)))
        with jax.named_scope("panel"):
            partial = panel_call(homes, slot, arrived, record, rim, fanned, norms, starts, scale)
        results.append(lax.all_to_all(partial, "tm", 0, 0))
    finished = []
    for result in results:
        total = jnp.sum(result, axis=0)
        rows = jnp.concatenate([total[:, 40 * part : 40 * part + MODES + 1] for part in range(3)], axis=0)
        rows = jnp.flip(rows, axis=0)
        finished.append(rows[:, :MODES] / rows[:, MODES:])
    return jnp.stack(finished)


def solution(mesh):
    placed = (P("tm", None), P(("tm", "panel"), None), P("panel"), P())
    return jax.shard_map(
        body, mesh=mesh, in_specs=placed, out_specs=P("panel", "tm", None), check_vma=False
    )
```

time: 189 us -> 157 us (0.83)
  between operations: 28.8 us -> 1.06 us
  local copies, waits for them, and re-layouts: 26.5 us -> 10.1 us
  waiting for transfers between devices: 33.4 us -> 48.1 us
  other arithmetic: 6.88 us -> 1.76 us
  starting transfers between devices: 47.1 us -> 49.6 us
    ppermute x16 -> x32, starting transfers between devices: 16.6 us -> 35.1 us  [step_round(): lax.ppermute(value, 'tm', [(order[i], order[(i + way) % homes]) for i in...]
    ppermute x16 -> x32, waiting for transfers between devices: 17.8 us -> 32.7 us  [step_round(): lax.ppermute(value, 'tm', [(order[i], order[(i + way) % homes]) for i in...]
    concatenate x19 -> x0, local copies, waits for them, and re-layouts: 12.4 us -> none  [the longest x1 6.26 us: fan(): jnp.concatenate([jnp.roll(padded, shift, axis=0) for shift in range(8)],...]
    all_to_all x2 -> x0, starting transfers between devices: 9.3 us -> none  [the longest x1 5.84 us: body(): lax.all_to_all(cards, 'tm', 0, 0).reshape(homes * turns, GROUP, channels)]
    all_to_all x2 -> x0, waiting for transfers between devices: 8.66 us -> none  [the longest x1 8.66 us: body(): lax.all_to_all(sent, 'panel', 0, 0)]
    ppermute x6 -> x3, waiting for transfers between devices: 0.02 us -> 8.1 us  [body(): lax.ppermute(eigvecs, 'panel', [((i + hop) % sharers, i) for i in range(s...]
    unnamed x47 -> x49, local copies, waits for them, and re-layouts: 3.43 us -> 8.09 us
    ppermute x6 -> x3, starting transfers between devices: 6.21 us -> 1.61 us  [body(): lax.ppermute(eigvecs, 'panel', [((i + hop) % sharers, i) for i in range(s...]
  transfers between devices with their start and end apart: 27 -> 38, of which waited for: 12 -> 17; matrix products, arithmetic and copies ran while one was open for 15% -> 2% of each run, Pallas kernels for 22% -> 28%
where the time goes in v2:
time: 157 us; the launch traced here: 156 us
  starting transfers between devices  49.6 us (32%)
  waiting for transfers between devices  48.1 us (31%)
  Pallas kernels  45.7 us (29%)
  local copies, waits for them, and re-layouts  10.1 us (6%)
  other arithmetic  1.76 us (1%)
    pallas_call x2, Pallas kernels, panel_call(): pl.pallas_call(lambda *refs: panel_kernel(homes, slot, places, *refs), ou...  40.6 us
    ppermute x32, starting transfers between devices, step_round(): lax.ppermute(value, 'tm', [(order[i], order[(i + way) % homes]) for i in...  35.1 us
    ppermute x32, waiting for transfers between devices, step_round(): lax.ppermute(value, 'tm', [(order[i], order[(i + way) % homes]) for i in...  32.7 us
    all_to_all x2, starting transfers between devices, body(): results.append(lax.all_to_all(partial, 'tm', 0, 0))  9.61 us
    ppermute x3, waiting for transfers between devices, body(): lax.ppermute(eigvecs, 'panel', [((i + hop) % sharers, i) for i in range(s...  8.1 us
    unnamed x49, local copies, waits for them, and re-layouts  8.09 us
    all_to_all x2, waiting for transfers between devices, body(): results.append(lax.all_to_all(partial, 'tm', 0, 0))  7.34 us
    pallas_call x1, Pallas kernels, prepare(): pl.pallas_call(prepare_kernel, out_shape=[jax.ShapeDtypeStruct((8, width)...  3.39 us
  transfers between devices with their start and end apart: 38, of which 17 were waited for; matrix products, arithmetic and copies ran while one was open for 2% of the time, Pallas kernels for 28%

profile of v2, /device:TPU:0, one launch (start us, length us, event | category | flops | bytes accessed | tf_op | source)
XLA Modules:
  0.0 156.5 jit_solution(4142651289572573375)
XLA Ops:
  0.0 2.2 %copy-done = bf16[2048,1024]{1,0:T(8,128)(2,1)S(1)} copy-done((bf16[2048,1024]{1,0:T(8,128)(2,1)S(1)}, bf16[2048,1024]{1,0:T(8,128)(2,1)}, u32[]{:S(2)}) %copy-start) | copy-done | bytes 4194328
  2.8 1.8 %own_rows.1 = (bf16[7,16,1024]{2,1,0:T(8,128)(2,1)S(1)}, bf16[7,16,1024]{2,1,0:T(8,128)(2,1)S(1)}, bf16[7,16,1024]{2,1,0:T(8,128)(2,1)S(1)}, bf16[7,16,1024]{2,1...) custom-call(s32[2]{0:T(128)S(1)} %copy-done.3, ...), custom_call_target="tpu_custom_call" | custom-call | tf_op jit(solution)/shard_map/own_rows/pallas_call | solution.py:184
  4.7 3.0 %collective-permute-start.8 = (bf16[3,16,1024]{2,1,0:T(8,128)(2,1)S(1)}, bf16[3,16,1024]{2,1,0:T(8,128)(2,1)S(1)}, u32[]{:S(2)}, u32[]{:S(2)}) collective-permute-start(bf16[3,16,1024]{2,1,0:T(8,128)(2,1)S(1)} %slice.169), channel_id=1, source_target_pairs={{0,4},{8,0},{16,8},{24,16},{28,24},{20,28},{12,20},{4,12},{1,5},{9... | collective-permute-start | bytes 294920 | tf_op jit(solution)/shard_map/scatter/ppermute | solution.py:155
  11.2 2.0 %collective-permute-start.9 = (bf16[7,16,1024]{2,1,0:T(8,128)(2,1)S(1)}, bf16[7,16,1024]{2,1,0:T(8,128)(2,1)S(1)}, u32[]{:S(2)}, u32[]{:S(2)}) collective-permute-start(bf16[7,16,1024]{2,1,0:T(8,128)(2,1)S(1)} %add_dynamic-update-slice_fusion.3), channel_id=1, source_target_pairs={{0,4},{8,0},{16,8},{24,16},{28,24},{20,28},{12,20},{4,12},{1,5},{9... | collective-permute-start | bytes 688136 | tf_op jit(solution)/shard_map/scatter/ppermute | solution.py:155
  13.3 1.9 %collective-permute-start.25 = (bf16[7,16,1024]{2,1,0:T(8,128)(2,1)S(1)}, bf16[7,16,1024]{2,1,0:T(8,128)(2,1)S(1)}, u32[]{:S(2)}, u32[]{:S(2)}) collective-permute-start(bf16[7,16,1024]{2,1,0:T(8,128)(2,1)S(1)} %add_dynamic-update-slice_fusion.2), channel_id=1, source_target_pairs={{0,4},{8,0},{16,8},{24,16},{28,24},{20,28},{12,20},{4,12},{1,5},{9... | collective-permute-start | bytes 688136 | tf_op jit(solution)/shard_map/scatter/ppermute | solution.py:155
  15.2 1.6 %collective-permute-done.4 = bf16[4,16,1024]{2,1,0:T(8,128)(2,1)S(1)} collective-permute-done((bf16[4,16,1024]{2,1,0:T(8,128)(2,1)S(1)}, bf16[4,16,1024]{2,1,0:T(8,128)(2,1)S(1)}, u32[]{:S(2)}, u32[]{:S(2)}) %collective-permute-start.4) | collective-permute-done | bytes 131104 | tf_op jit(solution)/shard_map/scatter/ppermute | solution.py:155
  17.9 2.0 %collective-permute-done.9 = bf16[7,16,1024]{2,1,0:T(8,128)(2,1)S(1)} collective-permute-done((bf16[7,16,1024]{2,1,0:T(8,128)(2,1)S(1)}, bf16[7,16,1024]{2,1,0:T(8,128)(2,1)S(1)}, u32[]{:S(2)}, u32[]{:S(2)}) %collective-permute-start.9) | collective-permute-done | bytes 229408 | tf_op jit(solution)/shard_map/scatter/ppermute | solution.py:155
  20.0 1.9 %collective-permute-start.10 = (bf16[7,16,1024]{2,1,0:T(8,128)(2,1)S(1)}, bf16[7,16,1024]{2,1,0:T(8,128)(2,1)S(1)}, u32[]{:S(2)}, u32[]{:S(2)}) collective-permute-start(bf16[7,16,1024]{2,1,0:T(8,128)(2,1)S(1)} %add.69), channel_id=1, source_target_pairs={{0,4},{8,0},{16,8},{24,16},{28,24},{20,28},{12,20},{4,12},{1,5},{9... | collective-permute-start | bytes 688136 | tf_op jit(solution)/shard_map/scatter/ppermute | solution.py:155
  21.9 3.6 %collective-permute-done.5 = bf16[7,16,1024]{2,1,0:T(8,128)(2,1)S(1)} collective-permute-done((bf16[7,16,1024]{2,1,0:T(8,128)(2,1)S(1)}, bf16[7,16,1024]{2,1,0:T(8,128)(2,1)S(1)}, u32[]{:S(2)}, u32[]{:S(2)}) %collective-permute-start.5) | collective-permute-done | bytes 229408 | tf_op jit(solution)/shard_map/scatter/ppermute | solution.py:155
  27.7 2.7 %collective-permute-done.21 = bf16[7,16,1024]{2,1,0:T(8,128)(2,1)S(1)} collective-permute-done((bf16[7,16,1024]{2,1,0:T(8,128)(2,1)S(1)}, bf16[7,16,1024]{2,1,0:T(8,128)(2,1)S(1)}, u32[]{:S(2)}, u32[]{:S(2)}) %collective-permute-start.21) | collective-permute-done | bytes 229408 | tf_op jit(solution)/shard_map/scatter/ppermute | solution.py:155
  32.7 2.7 %collective-permute-done.6 = bf16[7,16,1024]{2,1,0:T(8,128)(2,1)S(1)} collective-permute-done((bf16[7,16,1024]{2,1,0:T(8,128)(2,1)S(1)}, bf16[7,16,1024]{2,1,0:T(8,128)(2,1)S(1)}, u32[]{:S(2)}, u32[]{:S(2)}) %collective-permute-start.6) | collective-permute-done | bytes 229408 | tf_op jit(solution)/shard_map/scatter/ppermute | solution.py:155
  37.6 2.7 %collective-permute-done.22 = bf16[7,16,1024]{2,1,0:T(8,128)(2,1)S(1)} collective-permute-done((bf16[7,16,1024]{2,1,0:T(8,128)(2,1)S(1)}, bf16[7,16,1024]{2,1,0:T(8,128)(2,1)S(1)}, u32[]{:S(2)}, u32[]{:S(2)}) %collective-permute-start.22) | collective-permute-done | bytes 229408 | tf_op jit(solution)/shard_map/scatter/ppermute | solution.py:155
  40.8 4.3 %collective-permute-done.7 = bf16[7,16,1024]{2,1,0:T(8,128)(2,1)S(1)} collective-permute-done((bf16[7,16,1024]{2,1,0:T(8,128)(2,1)S(1)}, bf16[7,16,1024]{2,1,0:T(8,128)(2,1)S(1)}, u32[]{:S(2)}, u32[]{:S(2)}) %collective-permute-start.7) | collective-permute-done | bytes 229408 | tf_op jit(solution)/shard_map/scatter/ppermute | solution.py:155
  45.2 1.8 %collective-permute-start.13 = (bf16[7,16,1024]{2,1,0:T(8,128)(2,1)S(1)}, bf16[7,16,1024]{2,1,0:T(8,128)(2,1)S(1)}, u32[]{:S(2)}, u32[]{:S(2)}) collective-permute-start(bf16[7,16,1024]{2,1,0:T(8,128)(2,1)S(1)} %add_add_fusion.1.refs_6_), channel_id=1, source_target_pairs={{0,4},{8,0},{16,8},{24,16},{28,24},{20,28},{12,20},{4,12},{1,5},{9... | collective-permute-start | bytes 688136 | tf_op jit(solution)/shard_map/gather/ppermute | solution.py:155
  47.3 2.8 %collective-permute-done.23 = bf16[7,16,1024]{2,1,0:T(8,128)(2,1)S(1)} collective-permute-done((bf16[7,16,1024]{2,1,0:T(8,128)(2,1)S(1)}, bf16[7,16,1024]{2,1,0:T(8,128)(2,1)S(1)}, u32[]{:S(2)}, u32[]{:S(2)}) %collective-permute-start.23) | collective-permute-done | bytes 229408 | tf_op jit(solution)/shard_map/scatter/ppermute | solution.py:155
  50.1 1.8 %collective-permute-start.29 = (bf16[7,16,1024]{2,1,0:T(8,128)(2,1)S(1)}, bf16[7,16,1024]{2,1,0:T(8,128)(2,1)S(1)}, u32[]{:S(2)}, u32[]{:S(2)}) collective-permute-start(bf16[7,16,1024]{2,1,0:T(8,128)(2,1)S(1)} %add_add_fusion.refs_6_), channel_id=1, source_target_pairs={{0,4},{8,0},{16,8},{24,16},{28,24},{20,28},{12,20},{4,12},{1,5},{9... | collective-permute-start | bytes 688136 | tf_op jit(solution)/shard_map/gather/ppermute | solution.py:155
  52.2 3.3 %collective-permute-done.12.refs_7_ = bf16[7,16,1024]{2,1,0:T(8,128)(2,1)S(1)} collective-permute-done((bf16[7,16,1024]{2,1,0:T(8,128)(2,1)S(1)}, bf16[7,16,1024]{2,1,0:T(8,128)(2,1)S(1)}, u32[]{:S(2)}, u32[]{:S(2)}) %collective-permute-start.12) | collective-permute-done | bytes 229408 | tf_op jit(solution)/shard_map/gather/ppermute | solution.py:155
  55.8 1.7 %collective-permute-start.15 = (bf16[7,16,1024]{2,1,0:T(8,128)(2,1)S(1)}, bf16[7,16,1024]{2,1,0:T(8,128)(2,1)S(1)}, u32[]{:S(2)}, u32[]{:S(2)}) collective-permute-start(bf16[7,16,1024]{2,1,0:T(8,128)(2,1)S(1)} %collective-permute-done.13.refs_8_), channel_id=1, source_target_pairs={{0,4},{8,0},{16,8},{24,16},{28,24},{20,28},{12,20},{4,12},{1,5},{9... | collective-permute-start | bytes 688136 | tf_op jit(solution)/shard_map/gather/ppermute | solution.py:155
  58.7 1.7 %collective-permute-start.31 = (bf16[7,16,1024]{2,1,0:T(8,128)(2,1)S(1)}, bf16[7,16,1024]{2,1,0:T(8,128)(2,1)S(1)}, u32[]{:S(2)}, u32[]{:S(2)}) collective-permute-start(bf16[7,16,1024]{2,1,0:T(8,128)(2,1)S(1)} %collective-permute-done.29.refs_8_), channel_id=1, source_target_pairs={{0,4},{8,0},{16,8},{24,16},{28,24},{20,28},{12,20},{4,12},{1,5},{9... | collective-permute-start | bytes 688136 | tf_op jit(solution)/shard_map/gather/ppermute | solution.py:155
  60.7 4.6 %collective-permute-done.14.refs_9_ = bf16[7,16,1024]{2,1,0:T(8,128)(2,1)S(1)} collective-permute-done((bf16[7,16,1024]{2,1,0:T(8,128)(2,1)S(1)}, bf16[7,16,1024]{2,1,0:T(8,128)(2,1)S(1)}, u32[]{:S(2)}, u32[]{:S(2)}) %collective-permute-start.14) | collective-permute-done | bytes 229408 | tf_op jit(solution)/shard_map/gather/ppermute | solution.py:155
  65.7 1.7 %collective-permute-start.17 = (bf16[7,16,1024]{2,1,0:T(8,128)(2,1)S(1)}, bf16[7,16,1024]{2,1,0:T(8,128)(2,1)S(1)}, u32[]{:S(2)}, u32[]{:S(2)}) collective-permute-start(bf16[7,16,1024]{2,1,0:T(8,128)(2,1)S(1)} %collective-permute-done.15.refs_10_), channel_id=1, source_target_pairs={{0,4},{8,0},{16,8},{24,16},{28,24},{20,28},{12,20},{4,12},{1,5},{9... | collective-permute-start | bytes 688136 | tf_op jit(solution)/shard_map/gather/ppermute | solution.py:155
  68.5 3.4 %collective-permute-done.3.rest_3_ = bf16[512,32]{1,0:T(8,128)(2,1)S(1)} collective-permute-done((bf16[512,32]{1,0:T(8,128)(2,1)S(1)}, bf16[512,32]{1,0:T(8,128)(2,1)S(1)}, u32[]{:S(2)}, u32[]{:S(2)}) %collective-permute-start.3) | collective-permute-done | bytes 32800 | tf_op jit(solution)/shard_map/ppermute | solution.py:283
  71.9 3.4 %collective-permute-start = (bf16[128,1024]{1,0:T(8,128)(2,1)S(1)}, bf16[128,1024]{1,0:T(8,128)(2,1)S(1)}, u32[]{:S(2)}, u32[]{:S(2)}) collective-permute-start(bf16[128,1024]{1,0:T(8,128)(2,1)S(1)} %slice.165), channel_id=1, source_target_pairs={{0,4},{4,8},{8,12},{12,16},{16,20},{20,24},{24,28},{1,5},{5,9},{9,... | collective-permute-start | bytes 786440 | tf_op jit(solution)/shard_map/ppermute | solution.py:280
  75.7 1.7 %collective-permute-start.32 = (bf16[7,16,1024]{2,1,0:T(8,128)(2,1)S(1)}, bf16[7,16,1024]{2,1,0:T(8,128)(2,1)S(1)}, u32[]{:S(2)}, u32[]{:S(2)}) collective-permute-start(bf16[7,16,1024]{2,1,0:T(8,128)(2,1)S(1)} %collective-permute-done.30.refs_9_), channel_id=1, source_target_pairs={{0,8},{8,16},{16,24},{24,28},{28,20},{20,12},{12,4},{4,0},{1,9},{9... | collective-permute-start | bytes 688136 | tf_op jit(solution)/shard_map/gather/ppermute | solution.py:155
  79.0 3.4 %collective-permute-done.2.rest_2_ = bf16[512,32]{1,0:T(8,128)(2,1)S(1)} collective-permute-done((bf16[512,32]{1,0:T(8,128)(2,1)S(1)}, bf16[512,32]{1,0:T(8,128)(2,1)S(1)}, u32[]{:S(2)}, u32[]{:S(2)}) %collective-permute-start.2) | collective-permute-done | bytes 32800 | tf_op jit(solution)/shard_map/ppermute | solution.py:283
  85.9 2.2 %copy-done.1 = bf16[2048,1024]{1,0:T(8,128)(2,1)S(1)} copy-done((bf16[2048,1024]{1,0:T(8,128)(2,1)S(1)}, bf16[2048,1024]{1,0:T(8,128)(2,1)}, u32[]{:S(2)}) %copy-start.1) | copy-done | bytes 4194328
  88.1 3.4 %prepare.1 = (f32[8,2176]{1,0:T(8,128)S(1)}, bf16[2176,256]{1,0:T(8,128)(2,1)S(1)}) custom-call(bf16[2048,1024]{1,0:T(8,128)(2,1)S(1)} %copy-done.1, bf16[128,1024]{1,0:T(8,128)(2,1)S(1)} %collective-permute-done.rim.refs_3_, bf16[512,32]{1,0:T(8,128)(2,1)S(1)} %copy.22.rest_0_, bf16[512,32]{1,0:T(8,128)(2,1)S(1)} %collective-permute-done.1.rest_1_, ...), custom_call_target="tpu_custom_call" | custom-call | tf_op jit(solution)/shard_map/prepare/pallas_call | solution.py:244
  96.2 20.3 %panel.2 = f32[8,32,128]{2,1,0:T(8,128)} custom-call(s32[2]{0:T(128)} %refs_0_.5, f32[1]{0:T(128)S(6)} %div.23.refs_1_, bf16[2048,1024]{1,0:T(8,128)(2,1)} %refs_2_.3, bf16[128,1024]{1,0:T(8,128)(2,1)} %copy-done.2, bf16[2176,256]{1,0:T(8,128)(2,1)} %copy-done.4, f32[8,2176]{1,0:T(8,128)} %copy-done.5, bf16[7,16,1024]{2,1,0:T(8,128)(2,1)} %copy-done.7, ...), custom_call_target="tpu_custom_call" | custom-call | flops 3779067904 | bytes 8000000 | tf_op jit(solution)/shard_map/panel/pallas_call | solution.py:120
  116.6 3.6 %all-to-all-start = ((f32[8,32,128]{2,1,0:T(8,128)}), f32[8,32,128]{2,1,0:T(8,128)S(1)}, u32[]{:S(2)}, u32[]{:S(2)}) async-start(f32[8,32,128]{2,1,0:T(8,128)} %panel.2), calls=%async_computation | async-start | bytes 262144 | tf_op jit(solution)/shard_map/all_to_all | solution.py:300
  120.8 20.3 %panel.3 = f32[8,32,128]{2,1,0:T(8,128)} custom-call(s32[2]{0:T(128)} %refs_0_.5, f32[1]{0:T(128)S(6)} %div.23.refs_1_, bf16[2048,1024]{1,0:T(8,128)(2,1)} %refs_2_.3, bf16[128,1024]{1,0:T(8,128)(2,1)} %copy-done.2, bf16[2176,256]{1,0:T(8,128)(2,1)} %copy-done.4, f32[8,2176]{1,0:T(8,128)} %copy-done.5, bf16[7,16,1024]{2,1,0:T(8,128)(2,1)} %copy-done.6, ...), custom_call_target="tpu_custom_call" | custom-call | flops 3779067904 | bytes 8000000 | tf_op jit(solution)/shard_map/panel/pallas_call | solution.py:120
  141.1 6.0 %all-to-all-start.1 = ((f32[8,32,128]{2,1,0:T(8,128)}), f32[8,32,128]{2,1,0:T(8,128)S(1)}, u32[]{:S(2)}, u32[]{:S(2)}) async-start(f32[8,32,128]{2,1,0:T(8,128)} %panel.3), calls=%async_computation.1 | async-start | bytes 262144 | tf_op jit(solution)/shard_map/all_to_all | solution.py:300
  147.6 7.3 %all-to-all-done.1 = f32[8,32,128]{2,1,0:T(8,128)S(1)} async-done(((f32[8,32,128]{2,1,0:T(8,128)}), f32[8,32,128]{2,1,0:T(8,128)S(1)}, u32[]{:S(2)}, u32[]{:S(2)}) %all-to-all-start.1) | async-done | bytes 131104 | tf_op jit(solution)/shard_map/all_to_all | solution.py:300
  (142 shorter events, 28.7 us)
Async XLA Ops:
  9.3 8.1 %collective-permute-start.20 = (bf16[4,16,1024]{2,1,0:T(8,128)(2,1)S(1)}, bf16[4,16,1024]{2,1,0:T(8,128)(2,1)S(1)}, u32[]{:S(2)}, u32[]{:S(2)}) collective-permute-start(bf16[4,16,1024]{2,1,0:T(8,128)(2,1)S(1)} %slice.180), channel_id=1, source_target_pairs={{0,8},{8,16},{16,24},{24,28},{28,20},{20,12},{12,4},{4,0},{1,9},{9... | collective-permute-start | bytes 393224 | tf_op jit(solution)/shard_map/scatter/ppermute | solution.py:155
  11.2 8.7 %collective-permute-start.9 = (bf16[7,16,1024]{2,1,0:T(8,128)(2,1)S(1)}, bf16[7,16,1024]{2,1,0:T(8,128)(2,1)S(1)}, u32[]{:S(2)}, u32[]{:S(2)}) collective-permute-start(bf16[7,16,1024]{2,1,0:T(8,128)(2,1)S(1)} %add_dynamic-update-slice_fusion.3), channel_id=1, source_target_pairs={{0,4},{8,0},{16,8},{24,16},{28,24},{20,28},{12,20},{4,12},{1,5},{9... | collective-permute-start | bytes 688136 | tf_op jit(solution)/shard_map/scatter/ppermute | solution.py:155
  13.3 12.8 %collective-permute-start.25 = (bf16[7,16,1024]{2,1,0:T(8,128)(2,1)S(1)}, bf16[7,16,1024]{2,1,0:T(8,128)(2,1)S(1)}, u32[]{:S(2)}, u32[]{:S(2)}) collective-permute-start(bf16[7,16,1024]{2,1,0:T(8,128)(2,1)S(1)} %add_dynamic-update-slice_fusion.2), channel_id=1, source_target_pairs={{0,4},{8,0},{16,8},{24,16},{28,24},{20,28},{12,20},{4,12},{1,5},{9... | collective-permute-start | bytes 688136 | tf_op jit(solution)/shard_map/scatter/ppermute | solution.py:155
  16.9 8.6 %collective-permute-start.5 = (bf16[7,16,1024]{2,1,0:T(8,128)(2,1)S(1)}, bf16[7,16,1024]{2,1,0:T(8,128)(2,1)S(1)}, u32[]{:S(2)}, u32[]{:S(2)}) collective-permute-start(bf16[7,16,1024]{2,1,0:T(8,128)(2,1)S(1)} %add_dynamic-update-slice_fusion.1), channel_id=1, source_target_pairs={{0,8},{8,16},{16,24},{24,28},{28,20},{20,12},{12,4},{4,0},{1,9},{9... | collective-permute-start | bytes 688136 | tf_op jit(solution)/shard_map/scatter/ppermute | solution.py:155
  17.5 12.9 %collective-permute-start.21 = (bf16[7,16,1024]{2,1,0:T(8,128)(2,1)S(1)}, bf16[7,16,1024]{2,1,0:T(8,128)(2,1)S(1)}, u32[]{:S(2)}, u32[]{:S(2)}) collective-permute-start(bf16[7,16,1024]{2,1,0:T(8,128)(2,1)S(1)} %add_dynamic-update-slice_fusion), channel_id=1, source_target_pairs={{0,8},{8,16},{16,24},{24,28},{28,20},{20,12},{12,4},{4,0},{1,9},{9... | collective-permute-start | bytes 688136 | tf_op jit(solution)/shard_map/scatter/ppermute | solution.py:155
  20.0 11.0 %collective-permute-start.10 = (bf16[7,16,1024]{2,1,0:T(8,128)(2,1)S(1)}, bf16[7,16,1024]{2,1,0:T(8,128)(2,1)S(1)}, u32[]{:S(2)}, u32[]{:S(2)}) collective-permute-start(bf16[7,16,1024]{2,1,0:T(8,128)(2,1)S(1)} %add.69), channel_id=1, source_target_pairs={{0,4},{8,0},{16,8},{24,16},{28,24},{20,28},{12,20},{4,12},{1,5},{9... | collective-permute-start | bytes 688136 | tf_op jit(solution)/shard_map/scatter/ppermute | solution.py:155
  25.5 9.8 %collective-permute-start.6 = (bf16[7,16,1024]{2,1,0:T(8,128)(2,1)S(1)}, bf16[7,16,1024]{2,1,0:T(8,128)(2,1)S(1)}, u32[]{:S(2)}, u32[]{:S(2)}) collective-permute-start(bf16[7,16,1024]{2,1,0:T(8,128)(2,1)S(1)} %add.65), channel_id=1, source_target_pairs={{0,8},{8,16},{16,24},{24,28},{28,20},{20,12},{12,4},{4,0},{1,9},{9... | collective-permute-start | bytes 688136 | tf_op jit(solution)/shard_map/scatter/ppermute | solution.py:155
  26.1 9.8 %collective-permute-start.26 = (bf16[7,16,1024]{2,1,0:T(8,128)(2,1)S(1)}, bf16[7,16,1024]{2,1,0:T(8,128)(2,1)S(1)}, u32[]{:S(2)}, u32[]{:S(2)}) collective-permute-start(bf16[7,16,1024]{2,1,0:T(8,128)(2,1)S(1)} %add.77), channel_id=1, source_target_pairs={{0,4},{8,0},{16,8},{24,16},{28,24},{20,28},{12,20},{4,12},{1,5},{9... | collective-permute-start | bytes 688136 | tf_op jit(solution)/shard_map/scatter/ppermute | solution.py:155
  30.5 9.8 %collective-permute-start.22 = (bf16[7,16,1024]{2,1,0:T(8,128)(2,1)S(1)}, bf16[7,16,1024]{2,1,0:T(8,128)(2,1)S(1)}, u32[]{:S(2)}, u32[]{:S(2)}) collective-permute-start(bf16[7,16,1024]{2,1,0:T(8,128)(2,1)S(1)} %add.73), channel_id=1, source_target_pairs={{0,8},{8,16},{16,24},{24,28},{28,20},{20,12},{12,4},{4,0},{1,9},{9... | collective-permute-start | bytes 688136 | tf_op jit(solution)/shard_map/scatter/ppermute | solution.py:155
  31.0 9.8 %collective-permute-start.11 = (bf16[7,16,1024]{2,1,0:T(8,128)(2,1)S(1)}, bf16[7,16,1024]{2,1,0:T(8,128)(2,1)S(1)}, u32[]{:S(2)}, u32[]{:S(2)}) collective-permute-start(bf16[7,16,1024]{2,1,0:T(8,128)(2,1)S(1)} %add.70), channel_id=1, source_target_pairs={{0,4},{8,0},{16,8},{24,16},{28,24},{20,28},{12,20},{4,12},{1,5},{9... | collective-permute-start | bytes 688136 | tf_op jit(solution)/shard_map/scatter/ppermute | solution.py:155
  35.4 9.8 %collective-permute-start.7 = (bf16[7,16,1024]{2,1,0:T(8,128)(2,1)S(1)}, bf16[7,16,1024]{2,1,0:T(8,128)(2,1)S(1)}, u32[]{:S(2)}, u32[]{:S(2)}) collective-permute-start(bf16[7,16,1024]{2,1,0:T(8,128)(2,1)S(1)} %add.66), channel_id=1, source_target_pairs={{0,8},{8,16},{16,24},{24,28},{28,20},{20,12},{12,4},{4,0},{1,9},{9... | collective-permute-start | bytes 688136 | tf_op jit(solution)/shard_map/scatter/ppermute | solution.py:155
  35.9 11.3 %collective-permute-start.27 = (bf16[7,16,1024]{2,1,0:T(8,128)(2,1)S(1)}, bf16[7,16,1024]{2,1,0:T(8,128)(2,1)S(1)}, u32[]{:S(2)}, u32[]{:S(2)}) collective-permute-start(bf16[7,16,1024]{2,1,0:T(8,128)(2,1)S(1)} %add.78), channel_id=1, source_target_pairs={{0,4},{8,0},{16,8},{24,16},{28,24},{20,28},{12,20},{4,12},{1,5},{9... | collective-permute-start | bytes 688136 | tf_op jit(solution)/shard_map/scatter/ppermute | solution.py:155
  40.3 9.8 %collective-permute-start.23 = (bf16[7,16,1024]{2,1,0:T(8,128)(2,1)S(1)}, bf16[7,16,1024]{2,1,0:T(8,128)(2,1)S(1)}, u32[]{:S(2)}, u32[]{:S(2)}) collective-permute-start(bf16[7,16,1024]{2,1,0:T(8,128)(2,1)S(1)} %add.74), channel_id=1, source_target_pairs={{0,8},{8,16},{16,24},{24,28},{28,20},{20,12},{12,4},{4,0},{1,9},{9... | collective-permute-start | bytes 688136 | tf_op jit(solution)/shard_map/scatter/ppermute | solution.py:155
  45.2 10.6 %collective-permute-start.13 = (bf16[7,16,1024]{2,1,0:T(8,128)(2,1)S(1)}, bf16[7,16,1024]{2,1,0:T(8,128)(2,1)S(1)}, u32[]{:S(2)}, u32[]{:S(2)}) collective-permute-start(bf16[7,16,1024]{2,1,0:T(8,128)(2,1)S(1)} %add_add_fusion.1.refs_6_), channel_id=1, source_target_pairs={{0,4},{8,0},{16,8},{24,16},{28,24},{20,28},{12,20},{4,12},{1,5},{9... | collective-permute-start | bytes 688136 | tf_op jit(solution)/shard_map/gather/ppermute | solution.py:155
  47.0 8.5 %collective-permute-start.12 = (bf16[7,16,1024]{2,1,0:T(8,128)(2,1)S(1)}, bf16[7,16,1024]{2,1,0:T(8,128)(2,1)S(1)}, u32[]{:S(2)}, u32[]{:S(2)}) collective-permute-start(bf16[7,16,1024]{2,1,0:T(8,128)(2,1)S(1)} %add_add_fusion.1.refs_6_), channel_id=1, source_target_pairs={{0,8},{8,16},{16,24},{24,28},{28,20},{20,12},{12,4},{4,0},{1,9},{9... | collective-permute-start | bytes 688136 | tf_op jit(solution)/shard_map/gather/ppermute | solution.py:155
  50.1 8.5 %collective-permute-start.29 = (bf16[7,16,1024]{2,1,0:T(8,128)(2,1)S(1)}, bf16[7,16,1024]{2,1,0:T(8,128)(2,1)S(1)}, u32[]{:S(2)}, u32[]{:S(2)}) collective-permute-start(bf16[7,16,1024]{2,1,0:T(8,128)(2,1)S(1)} %add_add_fusion.refs_6_), channel_id=1, source_target_pairs={{0,4},{8,0},{16,8},{24,16},{28,24},{20,28},{12,20},{4,12},{1,5},{9... | collective-permute-start | bytes 688136 | tf_op jit(solution)/shard_map/gather/ppermute | solution.py:155
  51.9 8.5 %collective-permute-start.28 = (bf16[7,16,1024]{2,1,0:T(8,128)(2,1)S(1)}, bf16[7,16,1024]{2,1,0:T(8,128)(2,1)S(1)}, u32[]{:S(2)}, u32[]{:S(2)}) collective-permute-start(bf16[7,16,1024]{2,1,0:T(8,128)(2,1)S(1)} %add_add_fusion.refs_6_), channel_id=1, source_target_pairs={{0,8},{8,16},{16,24},{24,28},{28,20},{20,12},{12,4},{4,0},{1,9},{9... | collective-permute-start | bytes 688136 | tf_op jit(solution)/shard_map/gather/ppermute | solution.py:155
  55.5 9.8 %collective-permute-start.14 = (bf16[7,16,1024]{2,1,0:T(8,128)(2,1)S(1)}, bf16[7,16,1024]{2,1,0:T(8,128)(2,1)S(1)}, u32[]{:S(2)}, u32[]{:S(2)}) collective-permute-start(bf16[7,16,1024]{2,1,0:T(8,128)(2,1)S(1)} %collective-permute-done.12.refs_7_), channel_id=1, source_target_pairs={{0,8},{8,16},{16,24},{24,28},{28,20},{20,12},{12,4},{4,0},{1,9},{9... | collective-permute-start | bytes 688136 | tf_op jit(solution)/shard_map/gather/ppermute | solution.py:155
  55.8 9.8 %collective-permute-start.15 = (bf16[7,16,1024]{2,1,0:T(8,128)(2,1)S(1)}, bf16[7,16,1024]{2,1,0:T(8,128)(2,1)S(1)}, u32[]{:S(2)}, u32[]{:S(2)}) collective-permute-start(bf16[7,16,1024]{2,1,0:T(8,128)(2,1)S(1)} %collective-permute-done.13.refs_8_), channel_id=1, source_target_pairs={{0,4},{8,0},{16,8},{24,16},{28,24},{20,28},{12,20},{4,12},{1,5},{9... | collective-permute-start | bytes 688136 | tf_op jit(solution)/shard_map/gather/ppermute | solution.py:155
  58.7 16.6 %collective-permute-start.31 = (bf16[7,16,1024]{2,1,0:T(8,128)(2,1)S(1)}, bf16[7,16,1024]{2,1,0:T(8,128)(2,1)S(1)}, u32[]{:S(2)}, u32[]{:S(2)}) collective-permute-start(bf16[7,16,1024]{2,1,0:T(8,128)(2,1)S(1)} %collective-permute-done.29.refs_8_), channel_id=1, source_target_pairs={{0,4},{8,0},{16,8},{24,16},{28,24},{20,28},{12,20},{4,12},{1,5},{9... | collective-permute-start | bytes 688136 | tf_op jit(solution)/shard_map/gather/ppermute | solution.py:155
  60.4 15.3 %collective-permute-start.30 = (bf16[7,16,1024]{2,1,0:T(8,128)(2,1)S(1)}, bf16[7,16,1024]{2,1,0:T(8,128)(2,1)S(1)}, u32[]{:S(2)}, u32[]{:S(2)}) collective-permute-start(bf16[7,16,1024]{2,1,0:T(8,128)(2,1)S(1)} %collective-permute-done.28.refs_7_), channel_id=1, source_target_pairs={{0,8},{8,16},{16,24},{24,28},{28,20},{20,12},{12,4},{4,0},{1,9},{9... | collective-permute-start | bytes 688136 | tf_op jit(solution)/shard_map/gather/ppermute | solution.py:155
  65.3 12.1 %collective-permute-start.16 = (bf16[7,16,1024]{2,1,0:T(8,128)(2,1)S(1)}, bf16[7,16,1024]{2,1,0:T(8,128)(2,1)S(1)}, u32[]{:S(2)}, u32[]{:S(2)}) collective-permute-start(bf16[7,16,1024]{2,1,0:T(8,128)(2,1)S(1)} %collective-permute-done.14.refs_9_), channel_id=1, source_target_pairs={{0,8},{8,16},{16,24},{24,28},{28,20},{20,12},{12,4},{4,0},{1,9},{9... | collective-permute-start | bytes 688136 | tf_op jit(solution)/shard_map/gather/ppermute | solution.py:155
  65.7 16.7 %collective-permute-start.17 = (bf16[7,16,1024]{2,1,0:T(8,128)(2,1)S(1)}, bf16[7,16,1024]{2,1,0:T(8,128)(2,1)S(1)}, u32[]{:S(2)}, u32[]{:S(2)}) collective-permute-start(bf16[7,16,1024]{2,1,0:T(8,128)(2,1)S(1)} %collective-permute-done.15.refs_10_), channel_id=1, source_target_pairs={{0,4},{8,0},{16,8},{24,16},{28,24},{20,28},{12,20},{4,12},{1,5},{9... | collective-permute-start | bytes 688136 | tf_op jit(solution)/shard_map/gather/ppermute | solution.py:155
  71.9 14.0 %collective-permute-start = (bf16[128,1024]{1,0:T(8,128)(2,1)S(1)}, bf16[128,1024]{1,0:T(8,128)(2,1)S(1)}, u32[]{:S(2)}, u32[]{:S(2)}) collective-permute-start(bf16[128,1024]{1,0:T(8,128)(2,1)S(1)} %slice.165), channel_id=1, source_target_pairs={{0,4},{4,8},{8,12},{12,16},{16,20},{20,24},{24,28},{1,5},{5,9},{9,... | collective-permute-start | bytes 786440 | tf_op jit(solution)/shard_map/ppermute | solution.py:280
  75.3 17.9 %collective-permute-start.33 = (bf16[7,16,1024]{2,1,0:T(8,128)(2,1)S(1)}, bf16[7,16,1024]{2,1,0:T(8,128)(2,1)S(1)}, u32[]{:S(2)}, u32[]{:S(2)}) collective-permute-start(bf16[7,16,1024]{2,1,0:T(8,128)(2,1)S(1)} %collective-permute-done.31.refs_10_), channel_id=1, source_target_pairs={{0,4},{8,0},{16,8},{24,16},{28,24},{20,28},{12,20},{4,12},{1,5},{9... | collective-permute-start | bytes 688136 | tf_op jit(solution)/shard_map/gather/ppermute | solution.py:155
  75.7 18.4 %collective-permute-start.32 = (bf16[7,16,1024]{2,1,0:T(8,128)(2,1)S(1)}, bf16[7,16,1024]{2,1,0:T(8,128)(2,1)S(1)}, u32[]{:S(2)}, u32[]{:S(2)}) collective-permute-start(bf16[7,16,1024]{2,1,0:T(8,128)(2,1)S(1)} %collective-permute-done.30.refs_9_), channel_id=1, source_target_pairs={{0,8},{8,16},{16,24},{24,28},{28,20},{20,12},{12,4},{4,0},{1,9},{9... | collective-permute-start | bytes 688136 | tf_op jit(solution)/shard_map/gather/ppermute | solution.py:155
  82.4 13.1 %collective-permute-start.18 = (bf16[4,16,1024]{2,1,0:T(8,128)(2,1)S(1)}, bf16[4,16,1024]{2,1,0:T(8,128)(2,1)S(1)}, u32[]{:S(2)}, u32[]{:S(2)}) collective-permute-start(bf16[4,16,1024]{2,1,0:T(8,128)(2,1)S(1)} %slice.192), channel_id=1, source_target_pairs={{0,8},{8,16},{16,24},{24,28},{28,20},{20,12},{12,4},{4,0},{1,9},{9... | collective-permute-start | bytes 393224 | tf_op jit(solution)/shard_map/gather/ppermute | solution.py:155
  84.9 10.6 %collective-permute-start.19 = (bf16[3,16,1024]{2,1,0:T(8,128)(2,1)S(1)}, bf16[3,16,1024]{2,1,0:T(8,128)(2,1)S(1)}, u32[]{:S(2)}, u32[]{:S(2)}) collective-permute-start(bf16[3,16,1024]{2,1,0:T(8,128)(2,1)S(1)} %slice.193), channel_id=1, source_target_pairs={{0,4},{8,0},{16,8},{24,16},{28,24},{20,28},{12,20},{4,12},{1,5},{9... | collective-permute-start | bytes 294920 | tf_op jit(solution)/shard_map/gather/ppermute | solution.py:155
  93.2 27.0 %collective-permute-start.35 = (bf16[3,16,1024]{2,1,0:T(8,128)(2,1)S(1)}, bf16[3,16,1024]{2,1,0:T(8,128)(2,1)S(1)}, u32[]{:S(2)}, u32[]{:S(2)}) collective-permute-start(bf16[3,16,1024]{2,1,0:T(8,128)(2,1)S(1)} %slice.199), channel_id=1, source_target_pairs={{0,4},{8,0},{16,8},{24,16},{28,24},{20,28},{12,20},{4,12},{1,5},{9... | collective-permute-start | bytes 294920 | tf_op jit(solution)/shard_map/gather/ppermute | solution.py:155
  94.1 26.1 %collective-permute-start.34 = (bf16[4,16,1024]{2,1,0:T(8,128)(2,1)S(1)}, bf16[4,16,1024]{2,1,0:T(8,128)(2,1)}, u32[]{:S(2)}, u32[]{:S(2)}) collective-permute-start(bf16[4,16,1024]{2,1,0:T(8,128)(2,1)S(1)} %slice.198), channel_id=1, source_target_pairs={{0,8},{8,16},{16,24},{24,28},{28,20},{20,12},{12,4},{4,0},{1,9},{9... | collective-permute-start | bytes 393224 | tf_op jit(solution)/shard_map/gather/ppermute | solution.py:155
  116.6 24.6 %all-to-all-start = ((f32[8,32,128]{2,1,0:T(8,128)}), f32[8,32,128]{2,1,0:T(8,128)S(1)}, u32[]{:S(2)}, u32[]{:S(2)}) async-start(f32[8,32,128]{2,1,0:T(8,128)} %panel.2), calls=%async_computation | async-start | bytes 262144 | tf_op jit(solution)/shard_map/all_to_all | solution.py:300
  141.1 13.9 %all-to-all-start.1 = ((f32[8,32,128]{2,1,0:T(8,128)}), f32[8,32,128]{2,1,0:T(8,128)S(1)}, u32[]{:S(2)}, u32[]{:S(2)}) async-start(f32[8,32,128]{2,1,0:T(8,128)} %panel.3), calls=%async_computation.1 | async-start | bytes 262144 | tf_op jit(solution)/shard_map/all_to_all | solution.py:300
  (30 other events, 631.2 us)

commit v3 on v2

v3 whole, which is shorter than its diff:
```python
import jax
import jax.numpy as jnp
from jax import lax
from jax.experimental import pallas as pl
from jax.experimental.pallas import tpu as pltpu
from jax.sharding import PartitionSpec as P

DELAYS = 64
PANEL = 768
SLOTS = 2
GROUP = 16
LANES = 128
MODES = 32
BIG = 1e30


def panel_kernel(homes, places, starts, scale, record, rim, vectors, norms, *rest):
    parts = len(places)
    shards = [rest[slot * parts : (slot + 1) * parts] for slot in range(SLOTS)]
    out, window, turned, energies, gram, strips, weights, sums, result = rest[SLOTS * parts :]
    columns = record.shape[0]
    width = columns + LANES
    tiles = width // LANES
    used = turned.shape[1]
    kept = used - DELAYS
    position = ring_position(homes)
    share = PANEL // homes
    third = share // 3
    factor = scale[0]

    def collect(slot):
        for number, (hop, skipped, deal) in enumerate(places):
            chunk = lax.rem(position + (hop % homes), homes)
            shard = shards[slot][number]
            for step in range(0, shard.shape[0], GROUP):
                place = pl.multiple_of(chunk * deal + (skipped + step), GROUP)
                window[pl.ds(place, GROUP), :] = shard[step : step + GROUP, :]
        low = 0
        while low < used:
            count = min(LANES, used - low)
            turn = lax.broadcasted_iota(jnp.int32, (count, count), 0) + lax.broadcasted_iota(jnp.int32, (count, count), 1)
            flip = jnp.where(turn == count - 1, 2.0, 0.0).astype(jnp.bfloat16)
            block = jnp.dot(flip, window[used - low - count : used - low, :], preferred_element_type=jnp.float32)
            turned[slot, low : low + count, :] = block.astype(jnp.bfloat16)
            energy = jnp.sum(block * block, axis=1, keepdims=True) * 0.25
            energies[slot, low : low + count, :] = jnp.broadcast_to(energy, (count, LANES))
            low += count

    def product_with(slot, rows):
        return lax.dot_general(
            turned[slot], rows, (((1,), (1,)), ((), ())), preferred_element_type=jnp.float32
        )

    def turn_rows():
        for row in range(0, used, 8):
            line = pltpu.roll(gram[row : row + 8, :], row % width, 1, stride=1, stride_axis=0)
            for tile in range(tiles):
                strips[tile, row : row + 8, :] = line[:, tile * LANES : (tile + 1) * LANES]

    def add_lags(tile):
        value = strips[tile, 1:, :] + strips[tile, : used - 1, :]
        stride = 2
        while stride < DELAYS:
            value = value[stride:] + value[:-stride]
            stride *= 2
        strips[tile, DELAYS:used, :] = value[1:]

    def weigh(slot):
        for row in range(DELAYS, used, 16):
            halves = []
            for part in range(2):
                at = row + 8 * part
                line = jnp.concatenate([strips[tile, at : at + 8, :] for tile in range(tiles)], axis=1)
                line = pltpu.roll(line, (DELAYS - 1 - at) % width, 1)
                own = jnp.concatenate([strips[tiles, at : at + 8, :]] * tiles, axis=1)
                value = jnp.exp2(((own + norms[...]) - line) * factor)
                total = value[:, :LANES]
                for tile in range(1, tiles):
                    total = total + value[:, tile * LANES : (tile + 1) * LANES]
                sums[at - DELAYS : at - DELAYS + 8, :] = total
                halves.append(value)
            weights[row - DELAYS : row - DELAYS + 16, :] = jnp.concatenate(halves, axis=0).astype(jnp.bfloat16)
        product = jnp.dot(weights[...], vectors[...], preferred_element_type=jnp.float32)
        lane = lax.broadcasted_iota(jnp.int32, (kept, 2 * LANES), 1)
        sub = lax.broadcasted_iota(jnp.int32, (kept, 2 * LANES), 0)
        product = jnp.where(lane // MODES == sub % 8, product, 0.0)
        product = product[:, :LANES] + product[:, LANES:]
        product = product + pltpu.roll(product, 64, 1)
        product = product + pltpu.roll(product, 32, 1)
        lane = lax.broadcasted_iota(jnp.int32, (kept, LANES), 1)
        total = jnp.sum(sums[...], axis=1, keepdims=True)
        product = jnp.where(lane == MODES, total, product)
        result[...] = jnp.where(lane <= MODES, product, 0.0)
        offset = lax.bitwise_and(starts[slot] - (DELAYS - 1), GROUP - 1)
        for home in range(homes):
            start = kept - share * (home + 1) - offset
            packed = result[pl.ds(start, third), :]
            for part in range(1, 3):
                packed = packed + pltpu.roll(result[pl.ds(start + part * third, third), :], 40 * part, 1)
            out[home, slot * third : (slot + 1) * third, :] = packed

    for slot in range(SLOTS):
        collect(slot)
    gram[:, :columns] = product_with(0, record[...])
    gram[:, columns:] = product_with(0, rim[...])
    for slot in range(SLOTS):
        turn_rows()
        strips[tiles] = energies[slot]
        if slot + 1 < SLOTS:

            def add_and_multiply(pair, carry):
                add_lags(2 * pair)
                add_lags(2 * pair + 1)
                part = pl.ds(pl.multiple_of(pair * 2 * LANES, 2 * LANES), 2 * LANES)
                gram[:, part] = product_with(slot + 1, record[part, :])
                return carry

            lax.fori_loop(0, tiles // 2, add_and_multiply, 0)
            gram[:, columns:] = product_with(slot + 1, rim[...])
            add_lags(tiles - 1)
            add_lags(tiles)
        else:

            def add_only(tile, carry):
                add_lags(tile)
                return carry

            lax.fori_loop(0, tiles + 1, add_only, 0)
        weigh(slot)


def panel_call(homes, arrived, record, rim, vectors, norms, starts, scale):
    deal = arrived[0][0][2].shape[0]
    parts = len(arrived[0])
    places = [(hop, skipped, deal) for hop, skipped, _ in arrived[0]]
    shards = [part for slot in range(SLOTS) for _, _, part in arrived[slot]]
    columns = record.shape[0]
    width = columns + LANES
    tiles = width // LANES
    used = -(-(PANEL + DELAYS - 1 + GROUP - 1) // GROUP) * GROUP
    kept = used - DELAYS
    share = PANEL // homes
    vm = pl.BlockSpec(memory_space=pltpu.VMEM)
    sm = pl.BlockSpec(memory_space=pltpu.SMEM)
    return pl.pallas_call(
        lambda *refs: panel_kernel(homes, places, *refs),
        out_shape=jax.ShapeDtypeStruct((homes, SLOTS * (share // 3), LANES), jnp.float32),
        in_specs=[sm, sm] + [vm] * (4 + SLOTS * parts),
        out_specs=vm,
        scratch_shapes=[
            pltpu.VMEM((homes * deal, record.shape[1]), jnp.bfloat16),
            pltpu.VMEM((SLOTS, used, record.shape[1]), jnp.bfloat16),
            pltpu.VMEM((SLOTS, used, LANES), jnp.float32),
            pltpu.VMEM((used, width), jnp.float32),
            pltpu.VMEM((tiles + 1, used, LANES), jnp.float32),
            pltpu.VMEM((kept, width), jnp.bfloat16),
            pltpu.VMEM((kept, LANES), jnp.float32),
            pltpu.VMEM((kept, LANES), jnp.float32),
        ],
        compiler_params=pltpu.CompilerParams(vmem_limit_bytes=56 * 1024 * 1024),
        cost_estimate=pl.CostEstimate(
            flops=2 * SLOTS * used * width * record.shape[1], bytes_accessed=10_000_000, transcendentals=SLOTS * kept * width
        ),
    )(starts, scale, record, rim, vectors, norms, *shards)


def ring_position(homes):
    home = lax.axis_index("tm")
    if homes != 8:
        return home
    return jnp.where(lax.bitwise_and(home, 1) == 0, home, 2 * homes - 1 - home) // 2


def tour(homes):
    if homes != 8:
        return list(range(homes))
    return [0, 2, 4, 6, 7, 5, 3, 1]


def step_round(value, way):
    homes = lax.axis_size("tm")
    order = tour(homes)
    return lax.ppermute(value, "tm", [(order[i], order[(i + way) % homes]) for i in range(homes)])


def own_kernel(homes, deal, starts, record, *outs):
    home = lax.axis_index("tm")
    position = ring_position(homes)
    held = record.shape[0] // GROUP
    for slot in range(SLOTS):
        first = lax.shift_right_arithmetic(starts[slot] - (DELAYS - 1), 4) - home * held
        for hop in range(homes):
            out = outs[slot * homes + hop]
            chunk = lax.rem(position + hop, homes)
            for step in range(deal):
                group = first + chunk * deal + step
                inside = (group >= 0) & (group < held)

                place = slice(step * GROUP, (step + 1) * GROUP)

                @pl.when(inside)
                def _():
                    out[place, :] = record[pl.ds(pl.multiple_of(group * GROUP, GROUP), GROUP), :]

                @pl.when(jnp.logical_not(inside))
                def _():
                    out[place, :] = jnp.zeros((GROUP, out.shape[1]), out.dtype)


def own_rows(homes, deal, starts, record):
    vm = pl.BlockSpec(memory_space=pltpu.VMEM)
    sm = pl.BlockSpec(memory_space=pltpu.SMEM)
    shape = jax.ShapeDtypeStruct((deal * GROUP, record.shape[1]), record.dtype)
    flat = pl.pallas_call(
        lambda *refs: own_kernel(homes, deal, *refs),
        out_shape=[shape] * (SLOTS * homes),
        in_specs=[sm, vm],
        out_specs=[vm] * (SLOTS * homes),
        compiler_params=pltpu.CompilerParams(vmem_limit_bytes=40 * 1024 * 1024),
    )(starts, record)
    return [flat[slot * homes : (slot + 1) * homes] for slot in range(SLOTS)]


def prepare_kernel(record, rim, *rest):
    pieces = rest[:-4]
    norms, fanned, energy, spread = rest[-4:]
    columns = record.shape[0]
    width = columns + LANES
    sharers = len(pieces)
    sharer = lax.axis_index("panel")
    for source, low, high in ((record, 0, columns), (rim, columns, width)):
        for row in range(low, high, LANES):
            value = source[row - low : row - low + LANES, :].astype(jnp.float32)
            value = value * value
            total = value[:, :LANES]
            for lane in range(LANES, value.shape[1], LANES):
                total = total + value[:, lane : lane + LANES]
            energy[:, row : row + LANES] = lax.dot_general(
                jnp.ones((8, LANES), jnp.float32),
                total,
                (((1,), (1,)), ((), ())),
                precision=lax.Precision.HIGHEST,
                preferred_element_type=jnp.float32,
            )
    value = energy[...]
    stride = 1
    while stride < DELAYS:
        value = value + pltpu.roll(value, stride, 1)
        stride *= 2
    lane = lax.broadcasted_iota(jnp.int32, (8, width), 1)
    value = jnp.where(lane < columns, value, BIG)
    norms[...] = pltpu.roll(value, 0, 1, stride=1, stride_axis=0)
    lane = lax.broadcasted_iota(jnp.int32, (MODES, LANES), 1)
    mode = lax.broadcasted_iota(jnp.int32, (MODES, LANES), 0)
    copies = jnp.where(lax.bitwise_and(lane, MODES - 1) == mode, 1.0, 0.0).astype(jnp.bfloat16)
    rows = columns // sharers
    for hop in range(sharers):
        place = pl.multiple_of(lax.rem(sharer + hop, sharers) * rows, rows)
        spread[pl.ds(place, rows), :] = jnp.dot(pieces[hop][...], copies, preferred_element_type=jnp.float32)
    spread[columns:, :] = jnp.zeros((LANES, LANES), jnp.float32)
    value = spread[...]
    block = lax.broadcasted_iota(jnp.int32, (width, LANES), 1) // MODES
    per = LANES // MODES
    for half in range(2):
        result = jnp.zeros((width, LANES), jnp.float32)
        for part in range(per):
            result = jnp.where(block == part, pltpu.roll(value, half * per + part, 0), result)
        fanned[:, half * LANES : (half + 1) * LANES] = result.astype(jnp.bfloat16)


def prepare(record, rim, pieces):
    width = record.shape[0] + LANES
    vm = pl.BlockSpec(memory_space=pltpu.VMEM)
    return pl.pallas_call(
        prepare_kernel,
        out_shape=[
            jax.ShapeDtypeStruct((8, width), jnp.float32),
            jax.ShapeDtypeStruct((width, 2 * LANES), jnp.bfloat16),
        ],
        in_specs=[vm] * (2 + len(pieces)),
        out_specs=[vm] * 2,
        scratch_shapes=[pltpu.VMEM((8, width), jnp.float32), pltpu.VMEM((width, LANES), jnp.float32)],
        compiler_params=pltpu.CompilerParams(vmem_limit_bytes=40 * 1024 * 1024),
    )(record, rim, *pieces)


def body(record, eigvecs, starts, kernel_width):
    homes = lax.axis_size("tm")
    sharers = lax.axis_size("panel")
    columns, channels = record.shape
    groups = -(-(PANEL + DELAYS - 1 + GROUP - 1) // GROUP)
    deal = -(-groups // homes)
    half = homes // 2
    cut = (deal + 1) // 2 * GROUP
    with jax.named_scope("own_rows"):
        chunks = own_rows(homes, deal, starts, record)
    shards = []
    for slot in range(SLOTS):
        with jax.named_scope("scatter"):
            mine = chunks[slot]
            ahead = step_round(mine[half][:cut], 1)
            back = step_round(mine[half][cut:], -1)
            ahead = mine[half - 1].at[:cut].add(ahead)
            back = mine[half + 1].at[cut:].add(back)
            for hop in range(half - 2, -1, -1):
                ahead = mine[hop] + step_round(ahead, 1)
                back = step_round(back, -1)
                back = back if hop == 0 else mine[homes - hop] + back
            shards.append(ahead + back)
    rim = lax.ppermute(record[columns - LANES :], "tm", [(i, i + 1) for i in range(homes - 1)])
    pieces = [eigvecs]
    for hop in range(1, sharers):
        pieces.append(lax.ppermute(eigvecs, "panel", [((i + hop) % sharers, i) for i in range(sharers)]))
    with jax.named_scope("prepare"):
        norms, fanned = prepare(record, rim, pieces)
        shards, norms, fanned = lax.optimization_barrier((shards, norms, fanned))
    scale = -1.4426950408889634 / (kernel_width * (DELAYS * channels))
    results = []
    with jax.named_scope("gather"):
        for slot in range(SLOTS):
            ahead = back = shards[slot]
            arrived = [(0, 0, ahead)]
            for hop in range(1, half):
                ahead = step_round(ahead, 1)
                back = step_round(back, -1)
                arrived += [(-hop, 0, ahead), (hop, 0, back)]
            arrived.append((half, 0, step_round(ahead[:cut], 1)))
            arrived.append((half, cut, step_round(back[cut:], -1)))
            results.append(arrived)
    with jax.named_scope("panels"):
        partial = panel_call(homes, results, record, rim, fanned, norms, starts, scale)
    total = jnp.sum(lax.all_to_all(partial, "tm", 0, 0), axis=0)
    third = total.shape[0] // SLOTS
    finished = []
    for slot in range(SLOTS):
        own = total[slot * third : (slot + 1) * third]
        rows = jnp.concatenate([own[:, 40 * part : 40 * part + MODES + 1] for part in range(3)], axis=0)
        rows = jnp.flip(rows, axis=0)
        finished.append(rows[:, :MODES] / rows[:, MODES:])
    return jnp.stack(finished)


def solution(mesh):
    placed = (P("tm", None), P(("tm", "panel"), None), P("panel"), P())
    return jax.shard_map(
        body, mesh=mesh, in_specs=placed, out_specs=P("panel", "tm", None), check_vma=False
    )
```

time: 157 us -> 142 us (0.904)
  blocking collectives: 0 us -> 12 us
  Pallas kernels: 45.7 us -> 35.1 us
  starting transfers between devices: 49.6 us -> 40.5 us
  waiting for transfers between devices: 48.1 us -> 40.8 us
  other arithmetic: 1.76 us -> 4.07 us
  local copies, waits for them, and re-layouts: 10.1 us -> 8.39 us
    all_to_all x0 -> x1, blocking collectives: none -> 12 us  [body(): total = jnp.sum(lax.all_to_all(partial, 'tm', 0, 0), axis=0)]
    pallas_call x2 -> x1, Pallas kernels: 40.6 us -> 29.9 us  [panel_call(): pl.pallas_call(lambda *refs: panel_kernel(homes, places, *refs), out_shap...]
    all_to_all x2 -> x0, starting transfers between devices: 9.61 us -> none  [body(): results.append(lax.all_to_all(partial, 'tm', 0, 0))]
    all_to_all x2 -> x0, waiting for transfers between devices: 7.34 us -> none  [body(): results.append(lax.all_to_all(partial, 'tm', 0, 0))]
    ppermute x32, waiting for transfers between devices: 32.7 us -> 37.2 us  [step_round(): lax.ppermute(value, 'tm', [(order[i], order[(i + way) % homes]) for i in...]
    ppermute x3, waiting for transfers between devices: 8.1 us -> 3.58 us  [body(): lax.ppermute(eigvecs, 'panel', [((i + hop) % sharers, i) for i in range(s...]
    unnamed x49 -> x51, local copies, waits for them, and re-layouts: 8.09 us -> 6.42 us
    add x4, other arithmetic: 0.24 us -> 1.86 us  [body(): ahead = mine[hop] + step_round(ahead, 1)]
  transfers between devices with their start and end apart: 38 -> 36, of which waited for: 17 -> 17; matrix products, arithmetic and copies ran while one was open for 2% -> 3% of each run, Pallas kernels for 28% -> 2%
where the time goes in v3:
time: 142 us
  waiting for transfers between devices  40.8 us (29%)
  starting transfers between devices  40.5 us (29%)
  Pallas kernels  35.1 us (25%)
  blocking collectives  12 us (8%)
  local copies, waits for them, and re-layouts  8.39 us (6%)
  other arithmetic  4.07 us (3%)
    ppermute x32, waiting for transfers between devices, step_round(): lax.ppermute(value, 'tm', [(order[i], order[(i + way) % homes]) for i in...  37.2 us
    ppermute x32, starting transfers between devices, step_round(): lax.ppermute(value, 'tm', [(order[i], order[(i + way) % homes]) for i in...  35.5 us
    pallas_call x1, Pallas kernels, panel_call(): pl.pallas_call(lambda *refs: panel_kernel(homes, places, *refs), out_shap...  29.9 us
    all_to_all x1, blocking collectives, body(): total = jnp.sum(lax.all_to_all(partial, 'tm', 0, 0), axis=0)  12 us
    unnamed x51, local copies, waits for them, and re-layouts  6.42 us
    ppermute x3, waiting for transfers between devices, body(): lax.ppermute(eigvecs, 'panel', [((i + hop) % sharers, i) for i in range(s...  3.58 us
    ppermute x1, starting transfers between devices, body(): lax.ppermute(record[columns - LANES:], 'tm', [(i, i + 1) for i in range(h...  3.43 us
    pallas_call x1, Pallas kernels, prepare(): pl.pallas_call(prepare_kernel, out_shape=[jax.ShapeDtypeStruct((8, width)...  3.39 us
  transfers between devices with their start and end apart: 36, of which 17 were waited for; matrix products, arithmetic and copies ran while one was open for 3% of the time, Pallas kernels for 2%

profile of v3, /device:TPU:0, one launch (start us, length us, event | category | flops | bytes accessed | tf_op | source)
XLA Modules:
  0.0 141.9 jit_solution(14272519318946375962)
XLA Ops:
  0.0 2.2 %copy-done = bf16[2048,1024]{1,0:T(8,128)(2,1)S(1)} copy-done((bf16[2048,1024]{1,0:T(8,128)(2,1)S(1)}, bf16[2048,1024]{1,0:T(8,128)(2,1)}, u32[]{:S(2)}) %copy-start) | copy-done | bytes 4194328
  2.8 1.8 %own_rows.1 = (bf16[112,1024]{1,0:T(8,128)(2,1)S(1)}, bf16[112,1024]{1,0:T(8,128)(2,1)S(1)}, bf16[112,1024]{1,0:T(8,128)(2,1)S(1)}, bf16[112,1024]{1,0:T(8,128)(...) custom-call(s32[2]{0:T(128)S(1)} %copy-done.3, ...), custom_call_target="tpu_custom_call" | custom-call | tf_op jit(solution)/shard_map/own_rows/pallas_call | solution.py:214
  4.6 3.0 %collective-permute-start.5 = (bf16[48,1024]{1,0:T(8,128)(2,1)S(1)}, bf16[48,1024]{1,0:T(8,128)(2,1)S(1)}, u32[]{:S(2)}, u32[]{:S(2)}) collective-permute-start(bf16[48,1024]{1,0:T(8,128)(2,1)S(1)} %slice.157), channel_id=1, source_target_pairs={{0,4},{8,0},{16,8},{24,16},{28,24},{20,28},{12,20},{4,12},{1,5},{9... | collective-permute-start | bytes 294920 | tf_op jit(solution)/shard_map/scatter/ppermute | solution.py:183
  7.6 1.7 %collective-permute-start.13 = (bf16[48,1024]{1,0:T(8,128)(2,1)S(1)}, bf16[48,1024]{1,0:T(8,128)(2,1)S(1)}, u32[]{:S(2)}, u32[]{:S(2)}) collective-permute-start(bf16[48,1024]{1,0:T(8,128)(2,1)S(1)} %slice.161), channel_id=1, source_target_pairs={{0,4},{8,0},{16,8},{24,16},{28,24},{20,28},{12,20},{4,12},{1,5},{9... | collective-permute-start | bytes 294920 | tf_op jit(solution)/shard_map/scatter/ppermute | solution.py:183
  11.2 2.0 %collective-permute-start.6 = (bf16[112,1024]{1,0:T(8,128)(2,1)S(1)}, bf16[112,1024]{1,0:T(8,128)(2,1)S(1)}, u32[]{:S(2)}, u32[]{:S(2)}) collective-permute-start(bf16[112,1024]{1,0:T(8,128)(2,1)S(1)} %add_dynamic-update-slice_fusion.3), channel_id=1, source_target_pairs={{0,4},{8,0},{16,8},{24,16},{28,24},{20,28},{12,20},{4,12},{1,5},{9... | collective-permute-start | bytes 688136 | tf_op jit(solution)/shard_map/scatter/ppermute | solution.py:183
  13.2 1.8 %collective-permute-start.14 = (bf16[112,1024]{1,0:T(8,128)(2,1)S(1)}, bf16[112,1024]{1,0:T(8,128)(2,1)S(1)}, u32[]{:S(2)}, u32[]{:S(2)}) collective-permute-start(bf16[112,1024]{1,0:T(8,128)(2,1)S(1)} %add_dynamic-update-slice_fusion.2), channel_id=1, source_target_pairs={{0,4},{8,0},{16,8},{24,16},{28,24},{20,28},{12,20},{4,12},{1,5},{9... | collective-permute-start | bytes 688136 | tf_op jit(solution)/shard_map/scatter/ppermute | solution.py:183
  15.1 1.8 %collective-permute-done.1 = bf16[64,1024]{1,0:T(8,128)(2,1)S(1)} collective-permute-done((bf16[64,1024]{1,0:T(8,128)(2,1)S(1)}, bf16[64,1024]{1,0:T(8,128)(2,1)S(1)}, u32[]{:S(2)}, u32[]{:S(2)}) %collective-permute-start.1) | collective-permute-done | bytes 131104 | tf_op jit(solution)/shard_map/scatter/ppermute | solution.py:183
  17.9 2.0 %collective-permute-done.6 = bf16[112,1024]{1,0:T(8,128)(2,1)S(1)} collective-permute-done((bf16[112,1024]{1,0:T(8,128)(2,1)S(1)}, bf16[112,1024]{1,0:T(8,128)(2,1)S(1)}, u32[]{:S(2)}, u32[]{:S(2)}) %collective-permute-start.6) | collective-permute-done | bytes 229408 | tf_op jit(solution)/shard_map/scatter/ppermute | solution.py:183
  20.7 1.8 %collective-permute-start.7 = (bf16[112,1024]{1,0:T(8,128)(2,1)}, bf16[112,1024]{1,0:T(8,128)(2,1)S(1)}, u32[]{:S(2)}, u32[]{:S(2)}) collective-permute-start(bf16[112,1024]{1,0:T(8,128)(2,1)} %add.69), channel_id=1, source_target_pairs={{0,4},{8,0},{16,8},{24,16},{28,24},{20,28},{12,20},{4,12},{1,5},{9... | collective-permute-start | bytes 688136 | tf_op jit(solution)/shard_map/scatter/ppermute | solution.py:183
  22.5 3.0 %collective-permute-done.2 = bf16[112,1024]{1,0:T(8,128)(2,1)S(1)} collective-permute-done((bf16[112,1024]{1,0:T(8,128)(2,1)S(1)}, bf16[112,1024]{1,0:T(8,128)(2,1)S(1)}, u32[]{:S(2)}, u32[]{:S(2)}) %collective-permute-start.2) | collective-permute-done | bytes 229408 | tf_op jit(solution)/shard_map/scatter/ppermute | solution.py:183
  27.9 3.4 %collective-permute-done.19.rest_3_ = bf16[512,32]{1,0:T(8,128)(2,1)S(1)} collective-permute-done((bf16[512,32]{1,0:T(8,128)(2,1)S(1)}, bf16[512,32]{1,0:T(8,128)(2,1)S(1)}, u32[]{:S(2)}, u32[]{:S(2)}) %collective-permute-start.19) | collective-permute-done | bytes 32800 | tf_op jit(solution)/shard_map/ppermute | solution.py:313
  31.3 3.4 %collective-permute-start = (bf16[128,1024]{1,0:T(8,128)(2,1)S(1)}, bf16[128,1024]{1,0:T(8,128)(2,1)S(1)}, u32[]{:S(2)}, u32[]{:S(2)}) collective-permute-start(bf16[128,1024]{1,0:T(8,128)(2,1)S(1)} %slice.153), channel_id=1, source_target_pairs={{0,4},{4,8},{8,12},{12,16},{16,20},{20,24},{24,28},{1,5},{5,9},{9,... | collective-permute-start | bytes 786440 | tf_op jit(solution)/shard_map/ppermute | solution.py:310
  34.8 1.6 %collective-permute-start.18 = (bf16[512,32]{1,0:T(8,128)(2,1)S(1)}, bf16[512,32]{1,0:T(8,128)(2,1)S(1)}, u32[]{:S(2)}, u32[]{:S(2)}) collective-permute-start(bf16[512,32]{1,0:T(8,128)(2,1)S(1)} %copy.22.rest_0_), channel_id=1, source_target_pairs={{2,0},{3,1},{0,2},{1,3},{6,4},{7,5},{4,6},{5,7},{10,8},{11,9},{8,1... | collective-permute-start | bytes 98312 | tf_op jit(solution)/shard_map/ppermute | solution.py:313
  37.0 1.6 %collective-permute-start.11 = (bf16[112,1024]{1,0:T(8,128)(2,1)S(1)}, bf16[112,1024]{1,0:T(8,128)(2,1)S(1)}, u32[]{:S(2)}, u32[]{:S(2)}) collective-permute-start(bf16[112,1024]{1,0:T(8,128)(2,1)S(1)} %add.73), channel_id=1, source_target_pairs={{0,8},{8,16},{16,24},{24,28},{28,20},{20,12},{12,4},{4,0},{1,9},{9... | collective-permute-start | bytes 688136 | tf_op jit(solution)/shard_map/scatter/ppermute | solution.py:183
  40.2 1.6 %collective-permute-start.4 = (bf16[112,1024]{1,0:T(8,128)(2,1)S(1)}, bf16[112,1024]{1,0:T(8,128)(2,1)S(1)}, u32[]{:S(2)}, u32[]{:S(2)}) collective-permute-start(bf16[112,1024]{1,0:T(8,128)(2,1)S(1)} %add.66), channel_id=1, source_target_pairs={{0,8},{8,16},{16,24},{24,28},{28,20},{20,12},{12,4},{4,0},{1,9},{9... | collective-permute-start | bytes 688136 | tf_op jit(solution)/shard_map/scatter/ppermute | solution.py:183
  41.8 2.2 %copy-done.1 = bf16[2048,1024]{1,0:T(8,128)(2,1)S(1)} copy-done((bf16[2048,1024]{1,0:T(8,128)(2,1)S(1)}, bf16[2048,1024]{1,0:T(8,128)(2,1)}, u32[]{:S(2)}) %copy-start.1) | copy-done | bytes 4194328
  44.0 3.4 %prepare.1 = (f32[8,2176]{1,0:T(8,128)S(1)}, bf16[2176,256]{1,0:T(8,128)(2,1)S(1)}) custom-call(bf16[2048,1024]{1,0:T(8,128)(2,1)S(1)} %copy-done.1, bf16[128,1024]{1,0:T(8,128)(2,1)S(1)} %collective-permute-done.rim.refs_3_, bf16[512,32]{1,0:T(8,128)(2,1)S(1)} %copy.22.rest_0_, bf16[512,32]{1,0:T(8,128)(2,1)S(1)} %collective-permute-done.17.rest_1_, ...), custom_call_target="tpu_custom_call" | custom-call | tf_op jit(solution)/shard_map/prepare/pallas_call | solution.py:274
  47.5 2.2 %collective-permute-start.16 = (bf16[112,1024]{1,0:T(8,128)(2,1)S(1)}, bf16[112,1024]{1,0:T(8,128)(2,1)S(1)}, u32[]{:S(2)}, u32[]{:S(2)}) collective-permute-start(bf16[112,1024]{1,0:T(8,128)(2,1)S(1)} %add.78), channel_id=1, source_target_pairs={{0,4},{8,0},{16,8},{24,16},{28,24},{20,28},{12,20},{4,12},{1,5},{9... | collective-permute-start | bytes 688136 | tf_op jit(solution)/shard_map/scatter/ppermute | solution.py:183
  50.0 5.8 %collective-permute-done.16 = bf16[112,1024]{1,0:T(8,128)(2,1)S(1)} collective-permute-done((bf16[112,1024]{1,0:T(8,128)(2,1)S(1)}, bf16[112,1024]{1,0:T(8,128)(2,1)S(1)}, u32[]{:S(2)}, u32[]{:S(2)}) %collective-permute-start.16) | collective-permute-done | bytes 229408 | tf_op jit(solution)/shard_map/scatter/ppermute | solution.py:183
  56.2 1.6 %collective-permute-start.20 = (bf16[112,1024]{1,0:T(8,128)(2,1)S(1)}, bf16[112,1024]{1,0:T(8,128)(2,1)S(1)}, u32[]{:S(2)}, u32[]{:S(2)}) collective-permute-start(bf16[112,1024]{1,0:T(8,128)(2,1)S(1)} %add_add_fusion.1.refs_6_), channel_id=1, source_target_pairs={{0,8},{8,16},{16,24},{24,28},{28,20},{20,12},{12,4},{4,0},{1,9},{9... | collective-permute-start | bytes 688136 | tf_op jit(solution)/shard_map/gather/ppermute | solution.py:183
  57.8 1.7 %collective-permute-start.28 = (bf16[112,1024]{1,0:T(8,128)(2,1)S(1)}, bf16[112,1024]{1,0:T(8,128)(2,1)S(1)}, u32[]{:S(2)}, u32[]{:S(2)}) collective-permute-start(bf16[112,1024]{1,0:T(8,128)(2,1)S(1)} %add_add_fusion.refs_15_), channel_id=1, source_target_pairs={{0,8},{8,16},{16,24},{24,28},{28,20},{20,12},{12,4},{4,0},{1,9},{9... | collective-permute-start | bytes 688136 | tf_op jit(solution)/shard_map/gather/ppermute | solution.py:183
  60.3 4.5 %collective-permute-done.20.refs_7_ = bf16[112,1024]{1,0:T(8,128)(2,1)S(1)} collective-permute-done((bf16[112,1024]{1,0:T(8,128)(2,1)S(1)}, bf16[112,1024]{1,0:T(8,128)(2,1)S(1)}, u32[]{:S(2)}, u32[]{:S(2)}) %collective-permute-start.20) | collective-permute-done | bytes 229408 | tf_op jit(solution)/shard_map/gather/ppermute | solution.py:183
  66.3 3.4 %collective-permute-done.28.refs_16_ = bf16[112,1024]{1,0:T(8,128)(2,1)S(1)} collective-permute-done((bf16[112,1024]{1,0:T(8,128)(2,1)S(1)}, bf16[112,1024]{1,0:T(8,128)(2,1)S(1)}, u32[]{:S(2)}, u32[]{:S(2)}) %collective-permute-start.28) | collective-permute-done | bytes 229408 | tf_op jit(solution)/shard_map/gather/ppermute | solution.py:183
  72.4 2.1 %collective-permute-done.22.refs_9_ = bf16[112,1024]{1,0:T(8,128)(2,1)S(1)} collective-permute-done((bf16[112,1024]{1,0:T(8,128)(2,1)S(1)}, bf16[112,1024]{1,0:T(8,128)(2,1)S(1)}, u32[]{:S(2)}, u32[]{:S(2)}) %collective-permute-start.22) | collective-permute-done | bytes 229408 | tf_op jit(solution)/shard_map/gather/ppermute | solution.py:183
  76.1 3.4 %collective-permute-done.30.refs_18_ = bf16[112,1024]{1,0:T(8,128)(2,1)S(1)} collective-permute-done((bf16[112,1024]{1,0:T(8,128)(2,1)S(1)}, bf16[112,1024]{1,0:T(8,128)(2,1)S(1)}, u32[]{:S(2)}, u32[]{:S(2)}) %collective-permute-start.30) | collective-permute-done | bytes 229408 | tf_op jit(solution)/shard_map/gather/ppermute | solution.py:183
  82.3 2.1 %collective-permute-done.24.refs_11_ = bf16[112,1024]{1,0:T(8,128)(2,1)S(1)} collective-permute-done((bf16[112,1024]{1,0:T(8,128)(2,1)S(1)}, bf16[112,1024]{1,0:T(8,128)(2,1)S(1)}, u32[]{:S(2)}, u32[]{:S(2)}) %collective-permute-start.24) | collective-permute-done | bytes 229408 | tf_op jit(solution)/shard_map/gather/ppermute | solution.py:183
  84.4 1.6 %collective-permute-start.26 = (bf16[64,1024]{1,0:T(8,128)(2,1)S(1)}, bf16[64,1024]{1,0:T(8,128)(2,1)S(1)}, u32[]{:S(2)}, u32[]{:S(2)}) collective-permute-start(bf16[64,1024]{1,0:T(8,128)(2,1)S(1)} %slice.180), channel_id=1, source_target_pairs={{0,8},{8,16},{16,24},{24,28},{28,20},{20,12},{12,4},{4,0},{1,9},{9... | collective-permute-start | bytes 393224 | tf_op jit(solution)/shard_map/gather/ppermute | solution.py:183
  86.0 3.3 %collective-permute-done.32.refs_20_ = bf16[112,1024]{1,0:T(8,128)(2,1)S(1)} collective-permute-done((bf16[112,1024]{1,0:T(8,128)(2,1)S(1)}, bf16[112,1024]{1,0:T(8,128)(2,1)S(1)}, u32[]{:S(2)}, u32[]{:S(2)}) %collective-permute-start.32) | collective-permute-done | bytes 229408 | tf_op jit(solution)/shard_map/gather/ppermute | solution.py:183
  89.3 1.6 %collective-permute-start.34 = (bf16[64,1024]{1,0:T(8,128)(2,1)S(1)}, bf16[64,1024]{1,0:T(8,128)(2,1)S(1)}, u32[]{:S(2)}, u32[]{:S(2)}) collective-permute-start(bf16[64,1024]{1,0:T(8,128)(2,1)S(1)} %slice.182), channel_id=1, source_target_pairs={{0,8},{8,16},{16,24},{24,28},{28,20},{20,12},{12,4},{4,0},{1,9},{9... | collective-permute-start | bytes 393224 | tf_op jit(solution)/shard_map/gather/ppermute | solution.py:183
  92.5 3.1 %collective-permute-done.27.refs_14_ = bf16[48,1024]{1,0:T(8,128)(2,1)S(1)} collective-permute-done((bf16[48,1024]{1,0:T(8,128)(2,1)S(1)}, bf16[48,1024]{1,0:T(8,128)(2,1)S(1)}, u32[]{:S(2)}, u32[]{:S(2)}) %collective-permute-start.27) | collective-permute-done | bytes 98336 | tf_op jit(solution)/shard_map/gather/ppermute | solution.py:183
  98.0 29.9 %panels.1 = f32[8,64,128]{2,1,0:T(8,128)} custom-call(s32[2]{0:T(128)} %refs_0_.3, f32[1]{0:T(128)S(6)} %div.23.refs_1_, bf16[2048,1024]{1,0:T(8,128)(2,1)} %refs_2_.1, bf16[128,1024]{1,0:T(8,128)(2,1)} %copy-done.2, bf16[2176,256]{1,0:T(8,128)(2,1)} %copy-done.4, f32[8,2176]{1,0:T(8,128)} %copy-done.5, bf16[112,1024]{1,0:T(8,128)(2,1)} %copy-done.6, ...), custom_call_target="tpu_custom_call" | custom-call | flops 7558135808 | bytes 10000000 | tf_op jit(solution)/shard_map/panels/pallas_call | solution.py:145
  127.9 12.0 %all_to_all.5 = f32[8,64,128]{2,1,0:T(8,128)S(1)} all-to-all(f32[8,64,128]{2,1,0:T(8,128)} %panels.1), channel_id=1, replica_groups=mesh['tm'=8,'panel'=4] {'tm'}, dimensions={0} | all-to-all | bytes 524288 | tf_op jit(solution)/shard_map/all_to_all | solution.py:332
  (138 shorter events, 24.2 us)
Async XLA Ops:
  4.6 6.5 %collective-permute-start.5 = (bf16[48,1024]{1,0:T(8,128)(2,1)S(1)}, bf16[48,1024]{1,0:T(8,128)(2,1)S(1)}, u32[]{:S(2)}, u32[]{:S(2)}) collective-permute-start(bf16[48,1024]{1,0:T(8,128)(2,1)S(1)} %slice.157), channel_id=1, source_target_pairs={{0,4},{8,0},{16,8},{24,16},{28,24},{20,28},{12,20},{4,12},{1,5},{9... | collective-permute-start | bytes 294920 | tf_op jit(solution)/shard_map/scatter/ppermute | solution.py:183
  7.6 5.5 %collective-permute-start.13 = (bf16[48,1024]{1,0:T(8,128)(2,1)S(1)}, bf16[48,1024]{1,0:T(8,128)(2,1)S(1)}, u32[]{:S(2)}, u32[]{:S(2)}) collective-permute-start(bf16[48,1024]{1,0:T(8,128)(2,1)S(1)} %slice.161), channel_id=1, source_target_pairs={{0,4},{8,0},{16,8},{24,16},{28,24},{20,28},{12,20},{4,12},{1,5},{9... | collective-permute-start | bytes 294920 | tf_op jit(solution)/shard_map/scatter/ppermute | solution.py:183
  9.3 8.1 %collective-permute-start.9 = (bf16[64,1024]{1,0:T(8,128)(2,1)S(1)}, bf16[64,1024]{1,0:T(8,128)(2,1)S(1)}, u32[]{:S(2)}, u32[]{:S(2)}) collective-permute-start(bf16[64,1024]{1,0:T(8,128)(2,1)S(1)} %slice.159), channel_id=1, source_target_pairs={{0,8},{8,16},{16,24},{24,28},{28,20},{20,12},{12,4},{4,0},{1,9},{9... | collective-permute-start | bytes 393224 | tf_op jit(solution)/shard_map/scatter/ppermute | solution.py:183
  9.8 7.0 %collective-permute-start.1 = (bf16[64,1024]{1,0:T(8,128)(2,1)S(1)}, bf16[64,1024]{1,0:T(8,128)(2,1)S(1)}, u32[]{:S(2)}, u32[]{:S(2)}) collective-permute-start(bf16[64,1024]{1,0:T(8,128)(2,1)S(1)} %slice.155), channel_id=1, source_target_pairs={{0,8},{8,16},{16,24},{24,28},{28,20},{20,12},{12,4},{4,0},{1,9},{9... | collective-permute-start | bytes 393224 | tf_op jit(solution)/shard_map/scatter/ppermute | solution.py:183
  11.2 8.7 %collective-permute-start.6 = (bf16[112,1024]{1,0:T(8,128)(2,1)S(1)}, bf16[112,1024]{1,0:T(8,128)(2,1)S(1)}, u32[]{:S(2)}, u32[]{:S(2)}) collective-permute-start(bf16[112,1024]{1,0:T(8,128)(2,1)S(1)} %add_dynamic-update-slice_fusion.3), channel_id=1, source_target_pairs={{0,4},{8,0},{16,8},{24,16},{28,24},{20,28},{12,20},{4,12},{1,5},{9... | collective-permute-start | bytes 688136 | tf_op jit(solution)/shard_map/scatter/ppermute | solution.py:183
  13.2 21.5 %collective-permute-start.14 = (bf16[112,1024]{1,0:T(8,128)(2,1)S(1)}, bf16[112,1024]{1,0:T(8,128)(2,1)S(1)}, u32[]{:S(2)}, u32[]{:S(2)}) collective-permute-start(bf16[112,1024]{1,0:T(8,128)(2,1)S(1)} %add_dynamic-update-slice_fusion.2), channel_id=1, source_target_pairs={{0,4},{8,0},{16,8},{24,16},{28,24},{20,28},{12,20},{4,12},{1,5},{9... | collective-permute-start | bytes 688136 | tf_op jit(solution)/shard_map/scatter/ppermute | solution.py:183
  16.9 8.6 %collective-permute-start.2 = (bf16[112,1024]{1,0:T(8,128)(2,1)S(1)}, bf16[112,1024]{1,0:T(8,128)(2,1)S(1)}, u32[]{:S(2)}, u32[]{:S(2)}) collective-permute-start(bf16[112,1024]{1,0:T(8,128)(2,1)S(1)} %add_dynamic-update-slice_fusion.1), channel_id=1, source_target_pairs={{0,8},{8,16},{16,24},{24,28},{28,20},{20,12},{12,4},{4,0},{1,9},{9... | collective-permute-start | bytes 688136 | tf_op jit(solution)/shard_map/scatter/ppermute | solution.py:183
  17.5 18.8 %collective-permute-start.10 = (bf16[112,1024]{1,0:T(8,128)(2,1)S(1)}, bf16[112,1024]{1,0:T(8,128)(2,1)S(1)}, u32[]{:S(2)}, u32[]{:S(2)}) collective-permute-start(bf16[112,1024]{1,0:T(8,128)(2,1)S(1)} %add_dynamic-update-slice_fusion), channel_id=1, source_target_pairs={{0,8},{8,16},{16,24},{24,28},{28,20},{20,12},{12,4},{4,0},{1,9},{9... | collective-permute-start | bytes 688136 | tf_op jit(solution)/shard_map/scatter/ppermute | solution.py:183
  20.7 15.8 %collective-permute-start.7 = (bf16[112,1024]{1,0:T(8,128)(2,1)}, bf16[112,1024]{1,0:T(8,128)(2,1)S(1)}, u32[]{:S(2)}, u32[]{:S(2)}) collective-permute-start(bf16[112,1024]{1,0:T(8,128)(2,1)} %add.69), channel_id=1, source_target_pairs={{0,4},{8,0},{16,8},{24,16},{28,24},{20,28},{12,20},{4,12},{1,5},{9... | collective-permute-start | bytes 688136 | tf_op jit(solution)/shard_map/scatter/ppermute | solution.py:183
  26.2 10.8 %collective-permute-start.3 = (bf16[112,1024]{1,0:T(8,128)(2,1)}, bf16[112,1024]{1,0:T(8,128)(2,1)}, u32[]{:S(2)}, u32[]{:S(2)}) collective-permute-start(bf16[112,1024]{1,0:T(8,128)(2,1)} %add.65), channel_id=1, source_target_pairs={{0,8},{8,16},{16,24},{24,28},{28,20},{20,12},{12,4},{4,0},{1,9},{9... | collective-permute-start | bytes 688136 | tf_op jit(solution)/shard_map/scatter/ppermute | solution.py:183
  31.3 10.5 %collective-permute-start = (bf16[128,1024]{1,0:T(8,128)(2,1)S(1)}, bf16[128,1024]{1,0:T(8,128)(2,1)S(1)}, u32[]{:S(2)}, u32[]{:S(2)}) collective-permute-start(bf16[128,1024]{1,0:T(8,128)(2,1)S(1)} %slice.153), channel_id=1, source_target_pairs={{0,4},{4,8},{8,12},{12,16},{16,20},{20,24},{24,28},{1,5},{5,9},{9,... | collective-permute-start | bytes 786440 | tf_op jit(solution)/shard_map/ppermute | solution.py:310
  36.5 11.0 %collective-permute-start.15 = (bf16[112,1024]{1,0:T(8,128)(2,1)S(1)}, bf16[112,1024]{1,0:T(8,128)(2,1)S(1)}, u32[]{:S(2)}, u32[]{:S(2)}) collective-permute-start(bf16[112,1024]{1,0:T(8,128)(2,1)S(1)} %add.77), channel_id=1, source_target_pairs={{0,4},{8,0},{16,8},{24,16},{28,24},{20,28},{12,20},{4,12},{1,5},{9... | collective-permute-start | bytes 688136 | tf_op jit(solution)/shard_map/scatter/ppermute | solution.py:183
  37.0 12.7 %collective-permute-start.11 = (bf16[112,1024]{1,0:T(8,128)(2,1)S(1)}, bf16[112,1024]{1,0:T(8,128)(2,1)S(1)}, u32[]{:S(2)}, u32[]{:S(2)}) collective-permute-start(bf16[112,1024]{1,0:T(8,128)(2,1)S(1)} %add.73), channel_id=1, source_target_pairs={{0,8},{8,16},{16,24},{24,28},{28,20},{20,12},{12,4},{4,0},{1,9},{9... | collective-permute-start | bytes 688136 | tf_op jit(solution)/shard_map/scatter/ppermute | solution.py:183
  39.8 10.1 %collective-permute-start.8 = (bf16[112,1024]{1,0:T(8,128)(2,1)S(1)}, bf16[112,1024]{1,0:T(8,128)(2,1)S(1)}, u32[]{:S(2)}, u32[]{:S(2)}) collective-permute-start(bf16[112,1024]{1,0:T(8,128)(2,1)S(1)} %add.70), channel_id=1, source_target_pairs={{0,4},{8,0},{16,8},{24,16},{28,24},{20,28},{12,20},{4,12},{1,5},{9... | collective-permute-start | bytes 688136 | tf_op jit(solution)/shard_map/scatter/ppermute | solution.py:183
  40.2 9.7 %collective-permute-start.4 = (bf16[112,1024]{1,0:T(8,128)(2,1)S(1)}, bf16[112,1024]{1,0:T(8,128)(2,1)S(1)}, u32[]{:S(2)}, u32[]{:S(2)}) collective-permute-start(bf16[112,1024]{1,0:T(8,128)(2,1)S(1)} %add.66), channel_id=1, source_target_pairs={{0,8},{8,16},{16,24},{24,28},{28,20},{20,12},{12,4},{4,0},{1,9},{9... | collective-permute-start | bytes 688136 | tf_op jit(solution)/shard_map/scatter/ppermute | solution.py:183
  47.5 8.3 %collective-permute-start.16 = (bf16[112,1024]{1,0:T(8,128)(2,1)S(1)}, bf16[112,1024]{1,0:T(8,128)(2,1)S(1)}, u32[]{:S(2)}, u32[]{:S(2)}) collective-permute-start(bf16[112,1024]{1,0:T(8,128)(2,1)S(1)} %add.78), channel_id=1, source_target_pairs={{0,4},{8,0},{16,8},{24,16},{28,24},{20,28},{12,20},{4,12},{1,5},{9... | collective-permute-start | bytes 688136 | tf_op jit(solution)/shard_map/scatter/ppermute | solution.py:183
  49.7 6.4 %collective-permute-start.12 = (bf16[112,1024]{1,0:T(8,128)(2,1)S(1)}, bf16[112,1024]{1,0:T(8,128)(2,1)S(1)}, u32[]{:S(2)}, u32[]{:S(2)}) collective-permute-start(bf16[112,1024]{1,0:T(8,128)(2,1)S(1)} %add.74), channel_id=1, source_target_pairs={{0,8},{8,16},{16,24},{24,28},{28,20},{20,12},{12,4},{4,0},{1,9},{9... | collective-permute-start | bytes 688136 | tf_op jit(solution)/shard_map/scatter/ppermute | solution.py:183
  56.2 8.6 %collective-permute-start.20 = (bf16[112,1024]{1,0:T(8,128)(2,1)S(1)}, bf16[112,1024]{1,0:T(8,128)(2,1)S(1)}, u32[]{:S(2)}, u32[]{:S(2)}) collective-permute-start(bf16[112,1024]{1,0:T(8,128)(2,1)S(1)} %add_add_fusion.1.refs_6_), channel_id=1, source_target_pairs={{0,8},{8,16},{16,24},{24,28},{28,20},{20,12},{12,4},{4,0},{1,9},{9... | collective-permute-start | bytes 688136 | tf_op jit(solution)/shard_map/gather/ppermute | solution.py:183
  57.8 11.9 %collective-permute-start.28 = (bf16[112,1024]{1,0:T(8,128)(2,1)S(1)}, bf16[112,1024]{1,0:T(8,128)(2,1)S(1)}, u32[]{:S(2)}, u32[]{:S(2)}) collective-permute-start(bf16[112,1024]{1,0:T(8,128)(2,1)S(1)} %add_add_fusion.refs_15_), channel_id=1, source_target_pairs={{0,8},{8,16},{16,24},{24,28},{28,20},{20,12},{12,4},{4,0},{1,9},{9... | collective-permute-start | bytes 688136 | tf_op jit(solution)/shard_map/gather/ppermute | solution.py:183
  59.5 11.7 %collective-permute-start.21 = (bf16[112,1024]{1,0:T(8,128)(2,1)S(1)}, bf16[112,1024]{1,0:T(8,128)(2,1)S(1)}, u32[]{:S(2)}, u32[]{:S(2)}) collective-permute-start(bf16[112,1024]{1,0:T(8,128)(2,1)S(1)} %add_add_fusion.1.refs_6_), channel_id=1, source_target_pairs={{0,4},{8,0},{16,8},{24,16},{28,24},{20,28},{12,20},{4,12},{1,5},{9... | collective-permute-start | bytes 688136 | tf_op jit(solution)/shard_map/gather/ppermute | solution.py:183
  59.8 11.9 %collective-permute-start.29 = (bf16[112,1024]{1,0:T(8,128)(2,1)S(1)}, bf16[112,1024]{1,0:T(8,128)(2,1)S(1)}, u32[]{:S(2)}, u32[]{:S(2)}) collective-permute-start(bf16[112,1024]{1,0:T(8,128)(2,1)S(1)} %add_add_fusion.refs_15_), channel_id=1, source_target_pairs={{0,4},{8,0},{16,8},{24,16},{28,24},{20,28},{12,20},{4,12},{1,5},{9... | collective-permute-start | bytes 688136 | tf_op jit(solution)/shard_map/gather/ppermute | solution.py:183
  64.7 9.8 %collective-permute-start.22 = (bf16[112,1024]{1,0:T(8,128)(2,1)S(1)}, bf16[112,1024]{1,0:T(8,128)(2,1)S(1)}, u32[]{:S(2)}, u32[]{:S(2)}) collective-permute-start(bf16[112,1024]{1,0:T(8,128)(2,1)S(1)} %collective-permute-done.20.refs_7_), channel_id=1, source_target_pairs={{0,8},{8,16},{16,24},{24,28},{28,20},{20,12},{12,4},{4,0},{1,9},{9... | collective-permute-start | bytes 688136 | tf_op jit(solution)/shard_map/gather/ppermute | solution.py:183
  69.7 9.8 %collective-permute-start.30 = (bf16[112,1024]{1,0:T(8,128)(2,1)S(1)}, bf16[112,1024]{1,0:T(8,128)(2,1)S(1)}, u32[]{:S(2)}, u32[]{:S(2)}) collective-permute-start(bf16[112,1024]{1,0:T(8,128)(2,1)S(1)} %collective-permute-done.28.refs_16_), channel_id=1, source_target_pairs={{0,8},{8,16},{16,24},{24,28},{28,20},{20,12},{12,4},{4,0},{1,9},{9... | collective-permute-start | bytes 688136 | tf_op jit(solution)/shard_map/gather/ppermute | solution.py:183
  71.2 9.8 %collective-permute-start.23 = (bf16[112,1024]{1,0:T(8,128)(2,1)S(1)}, bf16[112,1024]{1,0:T(8,128)(2,1)S(1)}, u32[]{:S(2)}, u32[]{:S(2)}) collective-permute-start(bf16[112,1024]{1,0:T(8,128)(2,1)S(1)} %collective-permute-done.21.refs_8_), channel_id=1, source_target_pairs={{0,4},{8,0},{16,8},{24,16},{28,24},{20,28},{12,20},{4,12},{1,5},{9... | collective-permute-start | bytes 688136 | tf_op jit(solution)/shard_map/gather/ppermute | solution.py:183
  71.7 9.8 %collective-permute-start.31 = (bf16[112,1024]{1,0:T(8,128)(2,1)S(1)}, bf16[112,1024]{1,0:T(8,128)(2,1)S(1)}, u32[]{:S(2)}, u32[]{:S(2)}) collective-permute-start(bf16[112,1024]{1,0:T(8,128)(2,1)S(1)} %collective-permute-done.29.refs_17_), channel_id=1, source_target_pairs={{0,4},{8,0},{16,8},{24,16},{28,24},{20,28},{12,20},{4,12},{1,5},{9... | collective-permute-start | bytes 688136 | tf_op jit(solution)/shard_map/gather/ppermute | solution.py:183
  74.6 9.8 %collective-permute-start.24 = (bf16[112,1024]{1,0:T(8,128)(2,1)S(1)}, bf16[112,1024]{1,0:T(8,128)(2,1)S(1)}, u32[]{:S(2)}, u32[]{:S(2)}) collective-permute-start(bf16[112,1024]{1,0:T(8,128)(2,1)S(1)} %collective-permute-done.22.refs_9_), channel_id=1, source_target_pairs={{0,8},{8,16},{16,24},{24,28},{28,20},{20,12},{12,4},{4,0},{1,9},{9... | collective-permute-start | bytes 688136 | tf_op jit(solution)/shard_map/gather/ppermute | solution.py:183
  79.5 9.8 %collective-permute-start.32 = (bf16[112,1024]{1,0:T(8,128)(2,1)S(1)}, bf16[112,1024]{1,0:T(8,128)(2,1)S(1)}, u32[]{:S(2)}, u32[]{:S(2)}) collective-permute-start(bf16[112,1024]{1,0:T(8,128)(2,1)S(1)} %collective-permute-done.30.refs_18_), channel_id=1, source_target_pairs={{0,8},{8,16},{16,24},{24,28},{28,20},{20,12},{12,4},{4,0},{1,9},{9... | collective-permute-start | bytes 688136 | tf_op jit(solution)/shard_map/gather/ppermute | solution.py:183
  81.0 9.9 %collective-permute-start.25 = (bf16[112,1024]{1,0:T(8,128)(2,1)S(1)}, bf16[112,1024]{1,0:T(8,128)(2,1)S(1)}, u32[]{:S(2)}, u32[]{:S(2)}) collective-permute-start(bf16[112,1024]{1,0:T(8,128)(2,1)S(1)} %collective-permute-done.23.refs_10_), channel_id=1, source_target_pairs={{0,4},{8,0},{16,8},{24,16},{28,24},{20,28},{12,20},{4,12},{1,5},{9... | collective-permute-start | bytes 688136 | tf_op jit(solution)/shard_map/gather/ppermute | solution.py:183
  81.5 10.0 %collective-permute-start.33 = (bf16[112,1024]{1,0:T(8,128)(2,1)S(1)}, bf16[112,1024]{1,0:T(8,128)(2,1)S(1)}, u32[]{:S(2)}, u32[]{:S(2)}) collective-permute-start(bf16[112,1024]{1,0:T(8,128)(2,1)S(1)} %collective-permute-done.31.refs_19_), channel_id=1, source_target_pairs={{0,4},{8,0},{16,8},{24,16},{28,24},{20,28},{12,20},{4,12},{1,5},{9... | collective-permute-start | bytes 688136 | tf_op jit(solution)/shard_map/gather/ppermute | solution.py:183
  84.4 12.2 %collective-permute-start.26 = (bf16[64,1024]{1,0:T(8,128)(2,1)S(1)}, bf16[64,1024]{1,0:T(8,128)(2,1)S(1)}, u32[]{:S(2)}, u32[]{:S(2)}) collective-permute-start(bf16[64,1024]{1,0:T(8,128)(2,1)S(1)} %slice.180), channel_id=1, source_target_pairs={{0,8},{8,16},{16,24},{24,28},{28,20},{20,12},{12,4},{4,0},{1,9},{9... | collective-permute-start | bytes 393224 | tf_op jit(solution)/shard_map/gather/ppermute | solution.py:183
  89.3 7.3 %collective-permute-start.34 = (bf16[64,1024]{1,0:T(8,128)(2,1)S(1)}, bf16[64,1024]{1,0:T(8,128)(2,1)S(1)}, u32[]{:S(2)}, u32[]{:S(2)}) collective-permute-start(bf16[64,1024]{1,0:T(8,128)(2,1)S(1)} %slice.182), channel_id=1, source_target_pairs={{0,8},{8,16},{16,24},{24,28},{28,20},{20,12},{12,4},{4,0},{1,9},{9... | collective-permute-start | bytes 393224 | tf_op jit(solution)/shard_map/gather/ppermute | solution.py:183
  91.5 5.2 %collective-permute-start.35 = (bf16[48,1024]{1,0:T(8,128)(2,1)S(1)}, bf16[48,1024]{1,0:T(8,128)(2,1)S(1)}, u32[]{:S(2)}, u32[]{:S(2)}) collective-permute-start(bf16[48,1024]{1,0:T(8,128)(2,1)S(1)} %slice.183), channel_id=1, source_target_pairs={{0,4},{8,0},{16,8},{24,16},{28,24},{20,28},{12,20},{4,12},{1,5},{9... | collective-permute-start | bytes 294920 | tf_op jit(solution)/shard_map/gather/ppermute | solution.py:183
  (29 other events, 469.3 us)

commit v4 on v3

--- a/solution.py
+++ b/solution.py
@@ -51,18 +51,19 @@
             turned[slot], rows, (((1,), (1,)), ((), ())), preferred_element_type=jnp.float32
         )
 
-    def turn_rows():
+    def turn_rows(slot):
         for row in range(0, used, 8):
-            line = pltpu.roll(gram[row : row + 8, :], row % width, 1, stride=1, stride_axis=0)
+            line = pltpu.roll(gram[slot, row : row + 8, :], row % width, 1, stride=1, stride_axis=0)
             for tile in range(tiles):
                 strips[tile, row : row + 8, :] = line[:, tile * LANES : (tile + 1) * LANES]
 
     def add_lags(tile):
-        value = strips[tile, 1:, :] + strips[tile, : used - 1, :]
-        stride = 2
-        while stride < DELAYS:
+        value = strips[tile, :, :]
+        stride = 32
+        while stride >= 2:
             value = value[stride:] + value[:-stride]
-            stride *= 2
+            stride //= 2
+        value = value[1:] + value[:-1]
         strips[tile, DELAYS:used, :] = value[1:]
 
     def weigh(slot):
@@ -101,31 +102,14 @@
 
     for slot in range(SLOTS):
         collect(slot)
-    gram[:, :columns] = product_with(0, record[...])
-    gram[:, columns:] = product_with(0, rim[...])
-    for slot in range(SLOTS):
-        turn_rows()
+    for slot in range(SLOTS):
+        gram[slot, :, :columns] = product_with(slot, record[...])
+        gram[slot, :, columns:] = product_with(slot, rim[...])
+    for slot in range(SLOTS):
+        turn_rows(slot)
         strips[tiles] = energies[slot]
-        if slot + 1 < SLOTS:
-
-            def add_and_multiply(pair, carry):
-                add_lags(2 * pair)
-                add_lags(2 * pair + 1)
-                part = pl.ds(pl.multiple_of(pair * 2 * LANES, 2 * LANES), 2 * LANES)
-                gram[:, part] = product_with(slot + 1, record[part, :])
-                return carry
-
-            lax.fori_loop(0, tiles // 2, add_and_multiply, 0)
-            gram[:, columns:] = product_with(slot + 1, rim[...])
-            add_lags(tiles - 1)
-            add_lags(tiles)
-        else:
-
-            def add_only(tile, carry):
-                add_lags(tile)
-                return carry
-
-            lax.fori_loop(0, tiles + 1, add_only, 0)
+        for tile in range(tiles + 1):
+            add_lags(tile)
         weigh(slot)
 
 
@@ -151,13 +135,13 @@
             pltpu.VMEM((homes * deal, record.shape[1]), jnp.bfloat16),
             pltpu.VMEM((SLOTS, used, record.shape[1]), jnp.bfloat16),
             pltpu.VMEM((SLOTS, used, LANES), jnp.float32),
-            pltpu.VMEM((used, width), jnp.float32),
+            pltpu.VMEM((SLOTS, used, width), jnp.float32),
             pltpu.VMEM((tiles + 1, used, LANES), jnp.float32),
             pltpu.VMEM((kept, width), jnp.bfloat16),
             pltpu.VMEM((kept, LANES), jnp.float32),
             pltpu.VMEM((kept, LANES), jnp.float32),
         ],
-        compiler_params=pltpu.CompilerParams(vmem_limit_bytes=56 * 1024 * 1024),
+        compiler_params=pltpu.CompilerParams(vmem_limit_bytes=46 * 1024 * 1024),
         cost_estimate=pl.CostEstimate(
             flops=2 * SLOTS * used * width * record.shape[1], bytes_accessed=10_000_000, transcendentals=SLOTS * kept * width
         ),

time: 142 us -> 129 us (0.908)
  Pallas kernels: 35.1 us -> 23.8 us
    pallas_call x1, Pallas kernels: 29.9 us -> 18.5 us  [panel_call(): pl.pallas_call(lambda *refs: panel_kernel(homes, places, *refs), out_shap...]
    unnamed x51 -> x11, local copies, waits for them, and re-layouts: 6.42 us -> 5.16 us
  transfers between devices with their start and end apart: 36 -> 36, of which waited for: 17 -> 18; matrix products, arithmetic and copies ran while one was open for 3% -> 3% of each run, Pallas kernels for 2% -> 3%
where the time goes in v4:
time: 129 us
  waiting for transfers between devices  41.6 us (32%)
  starting transfers between devices  40.7 us (32%)
  Pallas kernels  23.8 us (18%)
  blocking collectives  11.9 us (9%)
  local copies, waits for them, and re-layouts  7.13 us (6%)
  other arithmetic  3.12 us (2%)
    ppermute x32, waiting for transfers between devices, step_round(): lax.ppermute(value, 'tm', [(order[i], order[(i + way) % homes]) for i in...  37 us
    ppermute x32, starting transfers between devices, step_round(): lax.ppermute(value, 'tm', [(order[i], order[(i + way) % homes]) for i in...  35.6 us
    pallas_call x1, Pallas kernels, panel_call(): pl.pallas_call(lambda *refs: panel_kernel(homes, places, *refs), out_shap...  18.5 us
    all_to_all x1, blocking collectives, body(): total = jnp.sum(lax.all_to_all(partial, 'tm', 0, 0), axis=0)  11.9 us
    unnamed x11, local copies, waits for them, and re-layouts  5.16 us
    ppermute x3, waiting for transfers between devices, body(): lax.ppermute(eigvecs, 'panel', [((i + hop) % sharers, i) for i in range(s...  4.57 us
    ppermute x1, starting transfers between devices, body(): lax.ppermute(record[columns - LANES:], 'tm', [(i, i + 1) for i in range(h...  3.48 us
    pallas_call x1, Pallas kernels, prepare(): pl.pallas_call(prepare_kernel, out_shape=[jax.ShapeDtypeStruct((8, width)...  3.39 us
  transfers between devices with their start and end apart: 36, of which 18 were waited for; matrix products, arithmetic and copies ran while one was open for 3% of the time, Pallas kernels for 3%

profile of v4, /device:TPU:0, one launch (start us, length us, event | category | flops | bytes accessed | tf_op | source)
XLA Modules:
  0.0 129.0 jit_solution(16569284273809636987)
XLA Ops:
  0.0 2.2 %copy-done = bf16[2048,1024]{1,0:T(8,128)(2,1)S(1)} copy-done((bf16[2048,1024]{1,0:T(8,128)(2,1)S(1)}, bf16[2048,1024]{1,0:T(8,128)(2,1)}, u32[]{:S(2)}) %copy-start) | copy-done | bytes 4194328
  2.8 1.9 %own_rows.1 = (bf16[112,1024]{1,0:T(8,128)(2,1)S(1)}, bf16[112,1024]{1,0:T(8,128)(2,1)S(1)}, bf16[112,1024]{1,0:T(8,128)(2,1)S(1)}, bf16[112,1024]{1,0:T(8,128)(...) custom-call(s32[2]{0:T(128)S(1)} %copy-done.2, ...), custom_call_target="tpu_custom_call" | custom-call | tf_op jit(solution)/shard_map/own_rows/pallas_call | solution.py:198
  4.8 2.9 %collective-permute-start.5 = (bf16[48,1024]{1,0:T(8,128)(2,1)S(1)}, bf16[48,1024]{1,0:T(8,128)(2,1)S(1)}, u32[]{:S(2)}, u32[]{:S(2)}) collective-permute-start(bf16[48,1024]{1,0:T(8,128)(2,1)S(1)} %slice.157), channel_id=1, source_target_pairs={{0,4},{8,0},{16,8},{24,16},{28,24},{20,28},{12,20},{4,12},{1,5},{9... | collective-permute-start | bytes 294920 | tf_op jit(solution)/shard_map/scatter/ppermute | solution.py:167
  7.6 1.6 %collective-permute-start.13 = (bf16[48,1024]{1,0:T(8,128)(2,1)S(1)}, bf16[48,1024]{1,0:T(8,128)(2,1)S(1)}, u32[]{:S(2)}, u32[]{:S(2)}) collective-permute-start(bf16[48,1024]{1,0:T(8,128)(2,1)S(1)} %slice.161), channel_id=1, source_target_pairs={{0,4},{8,0},{16,8},{24,16},{28,24},{20,28},{12,20},{4,12},{1,5},{9... | collective-permute-start | bytes 294920 | tf_op jit(solution)/shard_map/scatter/ppermute | solution.py:167
  11.2 1.9 %collective-permute-start.6 = (bf16[112,1024]{1,0:T(8,128)(2,1)S(1)}, bf16[112,1024]{1,0:T(8,128)(2,1)S(1)}, u32[]{:S(2)}, u32[]{:S(2)}) collective-permute-start(bf16[112,1024]{1,0:T(8,128)(2,1)S(1)} %add_dynamic-update-slice_fusion.3), channel_id=1, source_target_pairs={{0,4},{8,0},{16,8},{24,16},{28,24},{20,28},{12,20},{4,12},{1,5},{9... | collective-permute-start | bytes 688136 | tf_op jit(solution)/shard_map/scatter/ppermute | solution.py:167
  13.2 1.9 %collective-permute-start.14 = (bf16[112,1024]{1,0:T(8,128)(2,1)S(1)}, bf16[112,1024]{1,0:T(8,128)(2,1)S(1)}, u32[]{:S(2)}, u32[]{:S(2)}) collective-permute-start(bf16[112,1024]{1,0:T(8,128)(2,1)S(1)} %add_dynamic-update-slice_fusion.2), channel_id=1, source_target_pairs={{0,4},{8,0},{16,8},{24,16},{28,24},{20,28},{12,20},{4,12},{1,5},{9... | collective-permute-start | bytes 688136 | tf_op jit(solution)/shard_map/scatter/ppermute | solution.py:167
  15.1 1.7 %collective-permute-done.1 = bf16[64,1024]{1,0:T(8,128)(2,1)S(1)} collective-permute-done((bf16[64,1024]{1,0:T(8,128)(2,1)S(1)}, bf16[64,1024]{1,0:T(8,128)(2,1)S(1)}, u32[]{:S(2)}, u32[]{:S(2)}) %collective-permute-start.1) | collective-permute-done | bytes 131104 | tf_op jit(solution)/shard_map/scatter/ppermute | solution.py:167
  17.9 2.0 %collective-permute-done.6 = bf16[112,1024]{1,0:T(8,128)(2,1)S(1)} collective-permute-done((bf16[112,1024]{1,0:T(8,128)(2,1)S(1)}, bf16[112,1024]{1,0:T(8,128)(2,1)S(1)}, u32[]{:S(2)}, u32[]{:S(2)}) %collective-permute-start.6) | collective-permute-done | bytes 229408 | tf_op jit(solution)/shard_map/scatter/ppermute | solution.py:167
  20.6 1.8 %collective-permute-start.7 = (bf16[112,1024]{1,0:T(8,128)(2,1)}, bf16[112,1024]{1,0:T(8,128)(2,1)S(1)}, u32[]{:S(2)}, u32[]{:S(2)}) collective-permute-start(bf16[112,1024]{1,0:T(8,128)(2,1)} %add.69), channel_id=1, source_target_pairs={{0,4},{8,0},{16,8},{24,16},{28,24},{20,28},{12,20},{4,12},{1,5},{9... | collective-permute-start | bytes 688136 | tf_op jit(solution)/shard_map/scatter/ppermute | solution.py:167
  22.5 3.0 %collective-permute-done.2 = bf16[112,1024]{1,0:T(8,128)(2,1)S(1)} collective-permute-done((bf16[112,1024]{1,0:T(8,128)(2,1)S(1)}, bf16[112,1024]{1,0:T(8,128)(2,1)S(1)}, u32[]{:S(2)}, u32[]{:S(2)}) %collective-permute-start.2) | collective-permute-done | bytes 229408 | tf_op jit(solution)/shard_map/scatter/ppermute | solution.py:167
  27.8 3.4 %collective-permute-done.19.rest_3_ = bf16[512,32]{1,0:T(8,128)(2,1)S(1)} collective-permute-done((bf16[512,32]{1,0:T(8,128)(2,1)S(1)}, bf16[512,32]{1,0:T(8,128)(2,1)S(1)}, u32[]{:S(2)}, u32[]{:S(2)}) %collective-permute-start.19) | collective-permute-done | bytes 32800 | tf_op jit(solution)/shard_map/ppermute | solution.py:297
  31.3 3.5 %collective-permute-start = (bf16[128,1024]{1,0:T(8,128)(2,1)S(1)}, bf16[128,1024]{1,0:T(8,128)(2,1)S(1)}, u32[]{:S(2)}, u32[]{:S(2)}) collective-permute-start(bf16[128,1024]{1,0:T(8,128)(2,1)S(1)} %slice.153), channel_id=1, source_target_pairs={{0,4},{4,8},{8,12},{12,16},{16,20},{20,24},{24,28},{1,5},{5,9},{9,... | collective-permute-start | bytes 786440 | tf_op jit(solution)/shard_map/ppermute | solution.py:294
  37.0 1.6 %collective-permute-start.11 = (bf16[112,1024]{1,0:T(8,128)(2,1)S(1)}, bf16[112,1024]{1,0:T(8,128)(2,1)S(1)}, u32[]{:S(2)}, u32[]{:S(2)}) collective-permute-start(bf16[112,1024]{1,0:T(8,128)(2,1)S(1)} %add.73), channel_id=1, source_target_pairs={{0,8},{8,16},{16,24},{24,28},{28,20},{20,12},{12,4},{4,0},{1,9},{9... | collective-permute-start | bytes 688136 | tf_op jit(solution)/shard_map/scatter/ppermute | solution.py:167
  40.2 1.6 %collective-permute-start.4 = (bf16[112,1024]{1,0:T(8,128)(2,1)S(1)}, bf16[112,1024]{1,0:T(8,128)(2,1)S(1)}, u32[]{:S(2)}, u32[]{:S(2)}) collective-permute-start(bf16[112,1024]{1,0:T(8,128)(2,1)S(1)} %add.66), channel_id=1, source_target_pairs={{0,8},{8,16},{16,24},{24,28},{28,20},{20,12},{12,4},{4,0},{1,9},{9... | collective-permute-start | bytes 688136 | tf_op jit(solution)/shard_map/scatter/ppermute | solution.py:167
  41.8 2.2 %copy-done.1 = bf16[2048,1024]{1,0:T(8,128)(2,1)S(1)} copy-done((bf16[2048,1024]{1,0:T(8,128)(2,1)S(1)}, bf16[2048,1024]{1,0:T(8,128)(2,1)}, u32[]{:S(2)}) %copy-start.1) | copy-done | bytes 4194328
  44.0 3.4 %prepare.1 = (f32[8,2176]{1,0:T(8,128)S(1)}, bf16[2176,256]{1,0:T(8,128)(2,1)S(1)}) custom-call(bf16[2048,1024]{1,0:T(8,128)(2,1)S(1)} %copy-done.1, bf16[128,1024]{1,0:T(8,128)(2,1)S(1)} %collective-permute-done.rim.refs_3_, bf16[512,32]{1,0:T(8,128)(2,1)S(1)} %copy.22.rest_0_, bf16[512,32]{1,0:T(8,128)(2,1)S(1)} %collective-permute-done.17.rest_1_, ...), custom_call_target="tpu_custom_call" | custom-call | tf_op jit(solution)/shard_map/prepare/pallas_call | solution.py:258
  47.5 2.2 %collective-permute-start.16 = (bf16[112,1024]{1,0:T(8,128)(2,1)S(1)}, bf16[112,1024]{1,0:T(8,128)(2,1)S(1)}, u32[]{:S(2)}, u32[]{:S(2)}) collective-permute-start(bf16[112,1024]{1,0:T(8,128)(2,1)S(1)} %add.78), channel_id=1, source_target_pairs={{0,4},{8,0},{16,8},{24,16},{28,24},{20,28},{12,20},{4,12},{1,5},{9... | collective-permute-start | bytes 688136 | tf_op jit(solution)/shard_map/scatter/ppermute | solution.py:167
  50.0 5.9 %collective-permute-done.16 = bf16[112,1024]{1,0:T(8,128)(2,1)S(1)} collective-permute-done((bf16[112,1024]{1,0:T(8,128)(2,1)S(1)}, bf16[112,1024]{1,0:T(8,128)(2,1)S(1)}, u32[]{:S(2)}, u32[]{:S(2)}) %collective-permute-start.16) | collective-permute-done | bytes 229408 | tf_op jit(solution)/shard_map/scatter/ppermute | solution.py:167
  56.1 1.7 %collective-permute-start.20 = (bf16[112,1024]{1,0:T(8,128)(2,1)S(1)}, bf16[112,1024]{1,0:T(8,128)(2,1)S(1)}, u32[]{:S(2)}, u32[]{:S(2)}) collective-permute-start(bf16[112,1024]{1,0:T(8,128)(2,1)S(1)} %add_add_fusion.1.refs_6_), channel_id=1, source_target_pairs={{0,8},{8,16},{16,24},{24,28},{28,20},{20,12},{12,4},{4,0},{1,9},{9... | collective-permute-start | bytes 688136 | tf_op jit(solution)/shard_map/gather/ppermute | solution.py:167
  60.3 4.5 %collective-permute-done.20.refs_7_ = bf16[112,1024]{1,0:T(8,128)(2,1)S(1)} collective-permute-done((bf16[112,1024]{1,0:T(8,128)(2,1)S(1)}, bf16[112,1024]{1,0:T(8,128)(2,1)S(1)}, u32[]{:S(2)}, u32[]{:S(2)}) %collective-permute-start.20) | collective-permute-done | bytes 229408 | tf_op jit(solution)/shard_map/gather/ppermute | solution.py:167
  66.3 3.3 %collective-permute-done.28.refs_16_ = bf16[112,1024]{1,0:T(8,128)(2,1)S(1)} collective-permute-done((bf16[112,1024]{1,0:T(8,128)(2,1)S(1)}, bf16[112,1024]{1,0:T(8,128)(2,1)S(1)}, u32[]{:S(2)}, u32[]{:S(2)}) %collective-permute-start.28) | collective-permute-done | bytes 229408 | tf_op jit(solution)/shard_map/gather/ppermute | solution.py:167
  69.6 1.6 %collective-permute-start.30 = (bf16[112,1024]{1,0:T(8,128)(2,1)S(1)}, bf16[112,1024]{1,0:T(8,128)(2,1)S(1)}, u32[]{:S(2)}, u32[]{:S(2)}) collective-permute-start(bf16[112,1024]{1,0:T(8,128)(2,1)S(1)} %collective-permute-done.28.refs_16_), channel_id=1, source_target_pairs={{0,8},{8,16},{16,24},{24,28},{28,20},{20,12},{12,4},{4,0},{1,9},{9... | collective-permute-start | bytes 688136 | tf_op jit(solution)/shard_map/gather/ppermute | solution.py:167
  72.4 2.1 %collective-permute-done.22.refs_9_ = bf16[112,1024]{1,0:T(8,128)(2,1)S(1)} collective-permute-done((bf16[112,1024]{1,0:T(8,128)(2,1)S(1)}, bf16[112,1024]{1,0:T(8,128)(2,1)S(1)}, u32[]{:S(2)}, u32[]{:S(2)}) %collective-permute-start.22) | collective-permute-done | bytes 229408 | tf_op jit(solution)/shard_map/gather/ppermute | solution.py:167
  74.5 1.6 %collective-permute-start.24 = (bf16[112,1024]{1,0:T(8,128)(2,1)S(1)}, bf16[112,1024]{1,0:T(8,128)(2,1)S(1)}, u32[]{:S(2)}, u32[]{:S(2)}) collective-permute-start(bf16[112,1024]{1,0:T(8,128)(2,1)S(1)} %collective-permute-done.22.refs_9_), channel_id=1, source_target_pairs={{0,8},{8,16},{16,24},{24,28},{28,20},{20,12},{12,4},{4,0},{1,9},{9... | collective-permute-start | bytes 688136 | tf_op jit(solution)/shard_map/gather/ppermute | solution.py:167
  76.2 3.3 %collective-permute-done.30.refs_18_ = bf16[112,1024]{1,0:T(8,128)(2,1)S(1)} collective-permute-done((bf16[112,1024]{1,0:T(8,128)(2,1)S(1)}, bf16[112,1024]{1,0:T(8,128)(2,1)S(1)}, u32[]{:S(2)}, u32[]{:S(2)}) %collective-permute-start.30) | collective-permute-done | bytes 229408 | tf_op jit(solution)/shard_map/gather/ppermute | solution.py:167
  82.2 2.1 %collective-permute-done.24.refs_11_ = bf16[112,1024]{1,0:T(8,128)(2,1)S(1)} collective-permute-done((bf16[112,1024]{1,0:T(8,128)(2,1)S(1)}, bf16[112,1024]{1,0:T(8,128)(2,1)S(1)}, u32[]{:S(2)}, u32[]{:S(2)}) %collective-permute-start.24) | collective-permute-done | bytes 229408 | tf_op jit(solution)/shard_map/gather/ppermute | solution.py:167
  84.4 1.7 %collective-permute-start.26 = (bf16[64,1024]{1,0:T(8,128)(2,1)S(1)}, bf16[64,1024]{1,0:T(8,128)(2,1)S(1)}, u32[]{:S(2)}, u32[]{:S(2)}) collective-permute-start(bf16[64,1024]{1,0:T(8,128)(2,1)S(1)} %slice.180), channel_id=1, source_target_pairs={{0,8},{8,16},{16,24},{24,28},{28,20},{20,12},{12,4},{4,0},{1,9},{9... | collective-permute-start | bytes 393224 | tf_op jit(solution)/shard_map/gather/ppermute | solution.py:167
  86.0 3.2 %collective-permute-done.32.refs_20_ = bf16[112,1024]{1,0:T(8,128)(2,1)S(1)} collective-permute-done((bf16[112,1024]{1,0:T(8,128)(2,1)S(1)}, bf16[112,1024]{1,0:T(8,128)(2,1)S(1)}, u32[]{:S(2)}, u32[]{:S(2)}) %collective-permute-start.32) | collective-permute-done | bytes 229408 | tf_op jit(solution)/shard_map/gather/ppermute | solution.py:167
  89.3 1.7 %collective-permute-start.34 = (bf16[64,1024]{1,0:T(8,128)(2,1)S(1)}, bf16[64,1024]{1,0:T(8,128)(2,1)S(1)}, u32[]{:S(2)}, u32[]{:S(2)}) collective-permute-start(bf16[64,1024]{1,0:T(8,128)(2,1)S(1)} %slice.182), channel_id=1, source_target_pairs={{0,8},{8,16},{16,24},{24,28},{28,20},{20,12},{12,4},{4,0},{1,9},{9... | collective-permute-start | bytes 393224 | tf_op jit(solution)/shard_map/gather/ppermute | solution.py:167
  92.4 3.2 %collective-permute-done.27.refs_14_ = bf16[48,1024]{1,0:T(8,128)(2,1)S(1)} collective-permute-done((bf16[48,1024]{1,0:T(8,128)(2,1)S(1)}, bf16[48,1024]{1,0:T(8,128)(2,1)S(1)}, u32[]{:S(2)}, u32[]{:S(2)}) %collective-permute-start.27) | collective-permute-done | bytes 98336 | tf_op jit(solution)/shard_map/gather/ppermute | solution.py:167
  96.7 18.5 %panels.1 = f32[8,64,128]{2,1,0:T(8,128)S(1)} custom-call(s32[2]{0:T(128)S(1)} %copy-done.3, f32[1]{0:T(128)S(6)} %div.23.refs_1_, bf16[2048,1024]{1,0:T(8,128)(2,1)} %refs_2_.1, bf16[128,1024]{1,0:T(8,128)(2,1)S(1)} %collective-permute-done.rim.refs_3_, bf16[2176,256]{1,0:T(8,128)(2,1)S(1)} %get-tuple-element.93.refs_4_, ...), custom_call_target="tpu_custom_call" | custom-call | flops 7558135808 | bytes 10000000 | tf_op jit(solution)/shard_map/panels/pallas_call | solution.py:129
  115.2 11.9 %all_to_all.5 = f32[8,64,128]{2,1,0:T(8,128)S(1)} all-to-all(f32[8,64,128]{2,1,0:T(8,128)S(1)} %panels.1), channel_id=1, replica_groups=mesh['tm'=8,'panel'=4] {'tm'}, dimensions={0} | all-to-all | bytes 524288 | tf_op jit(solution)/shard_map/all_to_all | solution.py:316
  (98 shorter events, 23.1 us)
Async XLA Ops:
  4.8 6.4 %collective-permute-start.5 = (bf16[48,1024]{1,0:T(8,128)(2,1)S(1)}, bf16[48,1024]{1,0:T(8,128)(2,1)S(1)}, u32[]{:S(2)}, u32[]{:S(2)}) collective-permute-start(bf16[48,1024]{1,0:T(8,128)(2,1)S(1)} %slice.157), channel_id=1, source_target_pairs={{0,4},{8,0},{16,8},{24,16},{28,24},{20,28},{12,20},{4,12},{1,5},{9... | collective-permute-start | bytes 294920 | tf_op jit(solution)/shard_map/scatter/ppermute | solution.py:167
  7.6 5.5 %collective-permute-start.13 = (bf16[48,1024]{1,0:T(8,128)(2,1)S(1)}, bf16[48,1024]{1,0:T(8,128)(2,1)S(1)}, u32[]{:S(2)}, u32[]{:S(2)}) collective-permute-start(bf16[48,1024]{1,0:T(8,128)(2,1)S(1)} %slice.161), channel_id=1, source_target_pairs={{0,4},{8,0},{16,8},{24,16},{28,24},{20,28},{12,20},{4,12},{1,5},{9... | collective-permute-start | bytes 294920 | tf_op jit(solution)/shard_map/scatter/ppermute | solution.py:167
  9.3 8.1 %collective-permute-start.9 = (bf16[64,1024]{1,0:T(8,128)(2,1)S(1)}, bf16[64,1024]{1,0:T(8,128)(2,1)S(1)}, u32[]{:S(2)}, u32[]{:S(2)}) collective-permute-start(bf16[64,1024]{1,0:T(8,128)(2,1)S(1)} %slice.159), channel_id=1, source_target_pairs={{0,8},{8,16},{16,24},{24,28},{28,20},{20,12},{12,4},{4,0},{1,9},{9... | collective-permute-start | bytes 393224 | tf_op jit(solution)/shard_map/scatter/ppermute | solution.py:167
  9.8 7.0 %collective-permute-start.1 = (bf16[64,1024]{1,0:T(8,128)(2,1)S(1)}, bf16[64,1024]{1,0:T(8,128)(2,1)S(1)}, u32[]{:S(2)}, u32[]{:S(2)}) collective-permute-start(bf16[64,1024]{1,0:T(8,128)(2,1)S(1)} %slice.155), channel_id=1, source_target_pairs={{0,8},{8,16},{16,24},{24,28},{28,20},{20,12},{12,4},{4,0},{1,9},{9... | collective-permute-start | bytes 393224 | tf_op jit(solution)/shard_map/scatter/ppermute | solution.py:167
  11.2 8.7 %collective-permute-start.6 = (bf16[112,1024]{1,0:T(8,128)(2,1)S(1)}, bf16[112,1024]{1,0:T(8,128)(2,1)S(1)}, u32[]{:S(2)}, u32[]{:S(2)}) collective-permute-start(bf16[112,1024]{1,0:T(8,128)(2,1)S(1)} %add_dynamic-update-slice_fusion.3), channel_id=1, source_target_pairs={{0,4},{8,0},{16,8},{24,16},{28,24},{20,28},{12,20},{4,12},{1,5},{9... | collective-permute-start | bytes 688136 | tf_op jit(solution)/shard_map/scatter/ppermute | solution.py:167
  13.2 21.5 %collective-permute-start.14 = (bf16[112,1024]{1,0:T(8,128)(2,1)S(1)}, bf16[112,1024]{1,0:T(8,128)(2,1)S(1)}, u32[]{:S(2)}, u32[]{:S(2)}) collective-permute-start(bf16[112,1024]{1,0:T(8,128)(2,1)S(1)} %add_dynamic-update-slice_fusion.2), channel_id=1, source_target_pairs={{0,4},{8,0},{16,8},{24,16},{28,24},{20,28},{12,20},{4,12},{1,5},{9... | collective-permute-start | bytes 688136 | tf_op jit(solution)/shard_map/scatter/ppermute | solution.py:167
  16.9 8.6 %collective-permute-start.2 = (bf16[112,1024]{1,0:T(8,128)(2,1)S(1)}, bf16[112,1024]{1,0:T(8,128)(2,1)S(1)}, u32[]{:S(2)}, u32[]{:S(2)}) collective-permute-start(bf16[112,1024]{1,0:T(8,128)(2,1)S(1)} %add_dynamic-update-slice_fusion.1), channel_id=1, source_target_pairs={{0,8},{8,16},{16,24},{24,28},{28,20},{20,12},{12,4},{4,0},{1,9},{9... | collective-permute-start | bytes 688136 | tf_op jit(solution)/shard_map/scatter/ppermute | solution.py:167
  17.5 18.9 %collective-permute-start.10 = (bf16[112,1024]{1,0:T(8,128)(2,1)S(1)}, bf16[112,1024]{1,0:T(8,128)(2,1)S(1)}, u32[]{:S(2)}, u32[]{:S(2)}) collective-permute-start(bf16[112,1024]{1,0:T(8,128)(2,1)S(1)} %add_dynamic-update-slice_fusion), channel_id=1, source_target_pairs={{0,8},{8,16},{16,24},{24,28},{28,20},{20,12},{12,4},{4,0},{1,9},{9... | collective-permute-start | bytes 688136 | tf_op jit(solution)/shard_map/scatter/ppermute | solution.py:167
  20.6 15.8 %collective-permute-start.7 = (bf16[112,1024]{1,0:T(8,128)(2,1)}, bf16[112,1024]{1,0:T(8,128)(2,1)S(1)}, u32[]{:S(2)}, u32[]{:S(2)}) collective-permute-start(bf16[112,1024]{1,0:T(8,128)(2,1)} %add.69), channel_id=1, source_target_pairs={{0,4},{8,0},{16,8},{24,16},{28,24},{20,28},{12,20},{4,12},{1,5},{9... | collective-permute-start | bytes 688136 | tf_op jit(solution)/shard_map/scatter/ppermute | solution.py:167
  26.2 10.8 %collective-permute-start.3 = (bf16[112,1024]{1,0:T(8,128)(2,1)}, bf16[112,1024]{1,0:T(8,128)(2,1)S(1)}, u32[]{:S(2)}, u32[]{:S(2)}) collective-permute-start(bf16[112,1024]{1,0:T(8,128)(2,1)} %add.65), channel_id=1, source_target_pairs={{0,8},{8,16},{16,24},{24,28},{28,20},{20,12},{12,4},{4,0},{1,9},{9... | collective-permute-start | bytes 688136 | tf_op jit(solution)/shard_map/scatter/ppermute | solution.py:167
  31.3 10.6 %collective-permute-start = (bf16[128,1024]{1,0:T(8,128)(2,1)S(1)}, bf16[128,1024]{1,0:T(8,128)(2,1)S(1)}, u32[]{:S(2)}, u32[]{:S(2)}) collective-permute-start(bf16[128,1024]{1,0:T(8,128)(2,1)S(1)} %slice.153), channel_id=1, source_target_pairs={{0,4},{4,8},{8,12},{12,16},{16,20},{20,24},{24,28},{1,5},{5,9},{9,... | collective-permute-start | bytes 786440 | tf_op jit(solution)/shard_map/ppermute | solution.py:294
  36.5 10.9 %collective-permute-start.15 = (bf16[112,1024]{1,0:T(8,128)(2,1)S(1)}, bf16[112,1024]{1,0:T(8,128)(2,1)S(1)}, u32[]{:S(2)}, u32[]{:S(2)}) collective-permute-start(bf16[112,1024]{1,0:T(8,128)(2,1)S(1)} %add.77), channel_id=1, source_target_pairs={{0,4},{8,0},{16,8},{24,16},{28,24},{20,28},{12,20},{4,12},{1,5},{9... | collective-permute-start | bytes 688136 | tf_op jit(solution)/shard_map/scatter/ppermute | solution.py:167
  37.0 12.6 %collective-permute-start.11 = (bf16[112,1024]{1,0:T(8,128)(2,1)S(1)}, bf16[112,1024]{1,0:T(8,128)(2,1)S(1)}, u32[]{:S(2)}, u32[]{:S(2)}) collective-permute-start(bf16[112,1024]{1,0:T(8,128)(2,1)S(1)} %add.73), channel_id=1, source_target_pairs={{0,8},{8,16},{16,24},{24,28},{28,20},{20,12},{12,4},{4,0},{1,9},{9... | collective-permute-start | bytes 688136 | tf_op jit(solution)/shard_map/scatter/ppermute | solution.py:167
  39.8 10.1 %collective-permute-start.8 = (bf16[112,1024]{1,0:T(8,128)(2,1)S(1)}, bf16[112,1024]{1,0:T(8,128)(2,1)S(1)}, u32[]{:S(2)}, u32[]{:S(2)}) collective-permute-start(bf16[112,1024]{1,0:T(8,128)(2,1)S(1)} %add.70), channel_id=1, source_target_pairs={{0,4},{8,0},{16,8},{24,16},{28,24},{20,28},{12,20},{4,12},{1,5},{9... | collective-permute-start | bytes 688136 | tf_op jit(solution)/shard_map/scatter/ppermute | solution.py:167
  40.2 9.7 %collective-permute-start.4 = (bf16[112,1024]{1,0:T(8,128)(2,1)S(1)}, bf16[112,1024]{1,0:T(8,128)(2,1)S(1)}, u32[]{:S(2)}, u32[]{:S(2)}) collective-permute-start(bf16[112,1024]{1,0:T(8,128)(2,1)S(1)} %add.66), channel_id=1, source_target_pairs={{0,8},{8,16},{16,24},{24,28},{28,20},{20,12},{12,4},{4,0},{1,9},{9... | collective-permute-start | bytes 688136 | tf_op jit(solution)/shard_map/scatter/ppermute | solution.py:167
  47.5 8.4 %collective-permute-start.16 = (bf16[112,1024]{1,0:T(8,128)(2,1)S(1)}, bf16[112,1024]{1,0:T(8,128)(2,1)S(1)}, u32[]{:S(2)}, u32[]{:S(2)}) collective-permute-start(bf16[112,1024]{1,0:T(8,128)(2,1)S(1)} %add.78), channel_id=1, source_target_pairs={{0,4},{8,0},{16,8},{24,16},{28,24},{20,28},{12,20},{4,12},{1,5},{9... | collective-permute-start | bytes 688136 | tf_op jit(solution)/shard_map/scatter/ppermute | solution.py:167
  49.7 6.4 %collective-permute-start.12 = (bf16[112,1024]{1,0:T(8,128)(2,1)S(1)}, bf16[112,1024]{1,0:T(8,128)(2,1)S(1)}, u32[]{:S(2)}, u32[]{:S(2)}) collective-permute-start(bf16[112,1024]{1,0:T(8,128)(2,1)S(1)} %add.74), channel_id=1, source_target_pairs={{0,8},{8,16},{16,24},{24,28},{28,20},{20,12},{12,4},{4,0},{1,9},{9... | collective-permute-start | bytes 688136 | tf_op jit(solution)/shard_map/scatter/ppermute | solution.py:167
  56.1 8.6 %collective-permute-start.20 = (bf16[112,1024]{1,0:T(8,128)(2,1)S(1)}, bf16[112,1024]{1,0:T(8,128)(2,1)S(1)}, u32[]{:S(2)}, u32[]{:S(2)}) collective-permute-start(bf16[112,1024]{1,0:T(8,128)(2,1)S(1)} %add_add_fusion.1.refs_6_), channel_id=1, source_target_pairs={{0,8},{8,16},{16,24},{24,28},{28,20},{20,12},{12,4},{4,0},{1,9},{9... | collective-permute-start | bytes 688136 | tf_op jit(solution)/shard_map/gather/ppermute | solution.py:167
  57.8 11.8 %collective-permute-start.28 = (bf16[112,1024]{1,0:T(8,128)(2,1)S(1)}, bf16[112,1024]{1,0:T(8,128)(2,1)S(1)}, u32[]{:S(2)}, u32[]{:S(2)}) collective-permute-start(bf16[112,1024]{1,0:T(8,128)(2,1)S(1)} %add_add_fusion.refs_15_), channel_id=1, source_target_pairs={{0,8},{8,16},{16,24},{24,28},{28,20},{20,12},{12,4},{4,0},{1,9},{9... | collective-permute-start | bytes 688136 | tf_op jit(solution)/shard_map/gather/ppermute | solution.py:167
  59.4 11.8 %collective-permute-start.21 = (bf16[112,1024]{1,0:T(8,128)(2,1)S(1)}, bf16[112,1024]{1,0:T(8,128)(2,1)S(1)}, u32[]{:S(2)}, u32[]{:S(2)}) collective-permute-start(bf16[112,1024]{1,0:T(8,128)(2,1)S(1)} %add_add_fusion.1.refs_6_), channel_id=1, source_target_pairs={{0,4},{8,0},{16,8},{24,16},{28,24},{20,28},{12,20},{4,12},{1,5},{9... | collective-permute-start | bytes 688136 | tf_op jit(solution)/shard_map/gather/ppermute | solution.py:167
  59.8 11.8 %collective-permute-start.29 = (bf16[112,1024]{1,0:T(8,128)(2,1)S(1)}, bf16[112,1024]{1,0:T(8,128)(2,1)S(1)}, u32[]{:S(2)}, u32[]{:S(2)}) collective-permute-start(bf16[112,1024]{1,0:T(8,128)(2,1)S(1)} %add_add_fusion.refs_15_), channel_id=1, source_target_pairs={{0,4},{8,0},{16,8},{24,16},{28,24},{20,28},{12,20},{4,12},{1,5},{9... | collective-permute-start | bytes 688136 | tf_op jit(solution)/shard_map/gather/ppermute | solution.py:167
  64.7 9.8 %collective-permute-start.22 = (bf16[112,1024]{1,0:T(8,128)(2,1)S(1)}, bf16[112,1024]{1,0:T(8,128)(2,1)S(1)}, u32[]{:S(2)}, u32[]{:S(2)}) collective-permute-start(bf16[112,1024]{1,0:T(8,128)(2,1)S(1)} %collective-permute-done.20.refs_7_), channel_id=1, source_target_pairs={{0,8},{8,16},{16,24},{24,28},{28,20},{20,12},{12,4},{4,0},{1,9},{9... | collective-permute-start | bytes 688136 | tf_op jit(solution)/shard_map/gather/ppermute | solution.py:167
  69.6 9.8 %collective-permute-start.30 = (bf16[112,1024]{1,0:T(8,128)(2,1)S(1)}, bf16[112,1024]{1,0:T(8,128)(2,1)S(1)}, u32[]{:S(2)}, u32[]{:S(2)}) collective-permute-start(bf16[112,1024]{1,0:T(8,128)(2,1)S(1)} %collective-permute-done.28.refs_16_), channel_id=1, source_target_pairs={{0,8},{8,16},{16,24},{24,28},{28,20},{20,12},{12,4},{4,0},{1,9},{9... | collective-permute-start | bytes 688136 | tf_op jit(solution)/shard_map/gather/ppermute | solution.py:167
  71.2 9.8 %collective-permute-start.23 = (bf16[112,1024]{1,0:T(8,128)(2,1)S(1)}, bf16[112,1024]{1,0:T(8,128)(2,1)S(1)}, u32[]{:S(2)}, u32[]{:S(2)}) collective-permute-start(bf16[112,1024]{1,0:T(8,128)(2,1)S(1)} %collective-permute-done.21.refs_8_), channel_id=1, source_target_pairs={{0,4},{8,0},{16,8},{24,16},{28,24},{20,28},{12,20},{4,12},{1,5},{9... | collective-permute-start | bytes 688136 | tf_op jit(solution)/shard_map/gather/ppermute | solution.py:167
  71.7 9.8 %collective-permute-start.31 = (bf16[112,1024]{1,0:T(8,128)(2,1)S(1)}, bf16[112,1024]{1,0:T(8,128)(2,1)S(1)}, u32[]{:S(2)}, u32[]{:S(2)}) collective-permute-start(bf16[112,1024]{1,0:T(8,128)(2,1)S(1)} %collective-permute-done.29.refs_17_), channel_id=1, source_target_pairs={{0,4},{8,0},{16,8},{24,16},{28,24},{20,28},{12,20},{4,12},{1,5},{9... | collective-permute-start | bytes 688136 | tf_op jit(solution)/shard_map/gather/ppermute | solution.py:167
  74.5 9.8 %collective-permute-start.24 = (bf16[112,1024]{1,0:T(8,128)(2,1)S(1)}, bf16[112,1024]{1,0:T(8,128)(2,1)S(1)}, u32[]{:S(2)}, u32[]{:S(2)}) collective-permute-start(bf16[112,1024]{1,0:T(8,128)(2,1)S(1)} %collective-permute-done.22.refs_9_), channel_id=1, source_target_pairs={{0,8},{8,16},{16,24},{24,28},{28,20},{20,12},{12,4},{4,0},{1,9},{9... | collective-permute-start | bytes 688136 | tf_op jit(solution)/shard_map/gather/ppermute | solution.py:167
  79.5 9.8 %collective-permute-start.32 = (bf16[112,1024]{1,0:T(8,128)(2,1)S(1)}, bf16[112,1024]{1,0:T(8,128)(2,1)S(1)}, u32[]{:S(2)}, u32[]{:S(2)}) collective-permute-start(bf16[112,1024]{1,0:T(8,128)(2,1)S(1)} %collective-permute-done.30.refs_18_), channel_id=1, source_target_pairs={{0,8},{8,16},{16,24},{24,28},{28,20},{20,12},{12,4},{4,0},{1,9},{9... | collective-permute-start | bytes 688136 | tf_op jit(solution)/shard_map/gather/ppermute | solution.py:167
  81.1 9.9 %collective-permute-start.25 = (bf16[112,1024]{1,0:T(8,128)(2,1)S(1)}, bf16[112,1024]{1,0:T(8,128)(2,1)S(1)}, u32[]{:S(2)}, u32[]{:S(2)}) collective-permute-start(bf16[112,1024]{1,0:T(8,128)(2,1)S(1)} %collective-permute-done.23.refs_10_), channel_id=1, source_target_pairs={{0,4},{8,0},{16,8},{24,16},{28,24},{20,28},{12,20},{4,12},{1,5},{9... | collective-permute-start | bytes 688136 | tf_op jit(solution)/shard_map/gather/ppermute | solution.py:167
  81.5 10.0 %collective-permute-start.33 = (bf16[112,1024]{1,0:T(8,128)(2,1)S(1)}, bf16[112,1024]{1,0:T(8,128)(2,1)S(1)}, u32[]{:S(2)}, u32[]{:S(2)}) collective-permute-start(bf16[112,1024]{1,0:T(8,128)(2,1)S(1)} %collective-permute-done.31.refs_19_), channel_id=1, source_target_pairs={{0,4},{8,0},{16,8},{24,16},{28,24},{20,28},{12,20},{4,12},{1,5},{9... | collective-permute-start | bytes 688136 | tf_op jit(solution)/shard_map/gather/ppermute | solution.py:167
  84.4 12.3 %collective-permute-start.26 = (bf16[64,1024]{1,0:T(8,128)(2,1)S(1)}, bf16[64,1024]{1,0:T(8,128)(2,1)S(1)}, u32[]{:S(2)}, u32[]{:S(2)}) collective-permute-start(bf16[64,1024]{1,0:T(8,128)(2,1)S(1)} %slice.180), channel_id=1, source_target_pairs={{0,8},{8,16},{16,24},{24,28},{28,20},{20,12},{12,4},{4,0},{1,9},{9... | collective-permute-start | bytes 393224 | tf_op jit(solution)/shard_map/gather/ppermute | solution.py:167
  89.3 7.4 %collective-permute-start.34 = (bf16[64,1024]{1,0:T(8,128)(2,1)S(1)}, bf16[64,1024]{1,0:T(8,128)(2,1)S(1)}, u32[]{:S(2)}, u32[]{:S(2)}) collective-permute-start(bf16[64,1024]{1,0:T(8,128)(2,1)S(1)} %slice.182), channel_id=1, source_target_pairs={{0,8},{8,16},{16,24},{24,28},{28,20},{20,12},{12,4},{4,0},{1,9},{9... | collective-permute-start | bytes 393224 | tf_op jit(solution)/shard_map/gather/ppermute | solution.py:167
  91.5 5.2 %collective-permute-start.35 = (bf16[48,1024]{1,0:T(8,128)(2,1)S(1)}, bf16[48,1024]{1,0:T(8,128)(2,1)S(1)}, u32[]{:S(2)}, u32[]{:S(2)}) collective-permute-start(bf16[48,1024]{1,0:T(8,128)(2,1)S(1)} %slice.183), channel_id=1, source_target_pairs={{0,4},{8,0},{16,8},{24,16},{28,24},{20,28},{12,20},{4,12},{1,5},{9... | collective-permute-start | bytes 294920 | tf_op jit(solution)/shard_map/gather/ppermute | solution.py:167
  (9 other events, 105.0 us)

commit v5 on v4

--- a/solution.py
+++ b/solution.py
@@ -167,19 +167,90 @@
     return lax.ppermute(value, "tm", [(order[i], order[(i + way) % homes]) for i in range(homes)])
 
 
-def own_kernel(homes, deal, starts, record, *outs):
+def first_kernel(homes, deal, cut, starts, record, rim, *rest):
+    outs, flags = rest[:-1], rest[-1]
+    home = lax.axis_index("tm")
+    position = ring_position(homes)
+    rows = record.shape[0]
+    held = rows // GROUP
+    edge = pltpu.make_async_copy(record.at[pl.ds(rows - LANES, LANES)], rim, flags.at[0])
+    edge.start()
+    waits = []
+    for slot in range(SLOTS):
+        first = lax.shift_right_arithmetic(starts[slot] - (DELAYS - 1), 4) - home * held
+        chunk = lax.rem(position + homes // 2, homes)
+        for step in range(deal):
+            group = first + chunk * deal + step
+            inside = (group >= 0) & (group < held)
+            side = 0 if step < cut else 1
+            place = (step - cut * side) * GROUP
+            target = outs[2 * slot + side].at[pl.ds(place, GROUP)]
+            group = lax.clamp(0, group, held - 1)
+            source = record.at[pl.ds(pl.multiple_of(group * GROUP, GROUP), GROUP)]
+            copy = pltpu.make_async_copy(source, target, flags.at[1 + len(waits)])
+            waits.append((inside, copy, target))
+
+            @pl.when(inside)
+            def _():
+                copy.start()
+
+            @pl.when(jnp.logical_not(inside))
+            def _():
+                target[...] = jnp.zeros((GROUP, record.shape[1]), record.dtype)
+
+    for inside, copy, _ in waits:
+
+        @pl.when(inside)
+        def _():
+            copy.wait()
+
+    edge.wait()
+
+
+def first_rows(homes, deal, cut, starts, record):
+    sm = pl.BlockSpec(memory_space=pltpu.SMEM)
+    vm = pl.BlockSpec(memory_space=pltpu.VMEM)
+    shapes = [jax.ShapeDtypeStruct((LANES, record.shape[1]), record.dtype)]
+    for count in (cut, deal - cut) * SLOTS:
+        shapes.append(jax.ShapeDtypeStruct((count * GROUP, record.shape[1]), record.dtype))
+    return pl.pallas_call(
+        lambda *refs: first_kernel(homes, deal, cut, *refs),
+        out_shape=shapes,
+        in_specs=[sm, pl.BlockSpec(memory_space=pl.ANY)],
+        out_specs=[vm] * len(shapes),
+        scratch_shapes=[pltpu.SemaphoreType.DMA((1 + SLOTS * deal,))],
+        compiler_params=pltpu.CompilerParams(vmem_limit_bytes=60 * 1024 * 1024),
+    )(starts, record)
+
+
+def lane_energy(source, low):
+    value = source[low : low + LANES, :].astype(jnp.float32)
+    value = value * value
+    total = value[:, :LANES]
+    for lane in range(LANES, value.shape[1], LANES):
+        total = total + value[:, lane : lane + LANES]
+    return lax.dot_general(
+        jnp.ones((8, LANES), jnp.float32),
+        total,
+        (((1,), (1,)), ((), ())),
+        precision=lax.Precision.HIGHEST,
+        preferred_element_type=jnp.float32,
+    )
+
+
+def own_kernel(homes, deal, starts, record, energy, *outs):
     home = lax.axis_index("tm")
     position = ring_position(homes)
     held = record.shape[0] // GROUP
+    hops = [hop for hop in range(homes) if hop != homes // 2]
     for slot in range(SLOTS):
         first = lax.shift_right_arithmetic(starts[slot] - (DELAYS - 1), 4) - home * held
-        for hop in range(homes):
-            out = outs[slot * homes + hop]
+        for number, hop in enumerate(hops):
+            out = outs[slot * len(hops) + number]
             chunk = lax.rem(position + hop, homes)
             for step in range(deal):
                 group = first + chunk * deal + step
                 inside = (group >= 0) & (group < held)
-
                 place = slice(step * GROUP, (step + 1) * GROUP)
 
                 @pl.when(inside)
@@ -189,43 +260,40 @@
                 @pl.when(jnp.logical_not(inside))
                 def _():
                     out[place, :] = jnp.zeros((GROUP, out.shape[1]), out.dtype)
+
+    for row in range(0, record.shape[0], LANES):
+        energy[:, row : row + LANES] = lane_energy(record, row)
 
 
 def own_rows(homes, deal, starts, record):
     vm = pl.BlockSpec(memory_space=pltpu.VMEM)
     sm = pl.BlockSpec(memory_space=pltpu.SMEM)
     shape = jax.ShapeDtypeStruct((deal * GROUP, record.shape[1]), record.dtype)
-    flat = pl.pallas_call(
+    count = SLOTS * (homes - 1)
+    energy, *flat = pl.pallas_call(
         lambda *refs: own_kernel(homes, deal, *refs),
-        out_shape=[shape] * (SLOTS * homes),
+        out_shape=[jax.ShapeDtypeStruct((8, record.shape[0]), jnp.float32)] + [shape] * count,
         in_specs=[sm, vm],
-        out_specs=[vm] * (SLOTS * homes),
-        compiler_params=pltpu.CompilerParams(vmem_limit_bytes=40 * 1024 * 1024),
+        out_specs=[vm] * (1 + count),
+        compiler_params=pltpu.CompilerParams(vmem_limit_bytes=24 * 1024 * 1024),
     )(starts, record)
-    return [flat[slot * homes : (slot + 1) * homes] for slot in range(SLOTS)]
-
-
-def prepare_kernel(record, rim, *rest):
+    chunks = []
+    for slot in range(SLOTS):
+        part = list(flat[slot * (homes - 1) : (slot + 1) * (homes - 1)])
+        part.insert(homes // 2, None)
+        chunks.append(part)
+    return energy, chunks
+
+
+def prepare_kernel(energies, rim, *rest):
     pieces = rest[:-4]
     norms, fanned, energy, spread = rest[-4:]
-    columns = record.shape[0]
+    columns = energies.shape[1]
     width = columns + LANES
     sharers = len(pieces)
     sharer = lax.axis_index("panel")
-    for source, low, high in ((record, 0, columns), (rim, columns, width)):
-        for row in range(low, high, LANES):
-            value = source[row - low : row - low + LANES, :].astype(jnp.float32)
-            value = value * value
-            total = value[:, :LANES]
-            for lane in range(LANES, value.shape[1], LANES):
-                total = total + value[:, lane : lane + LANES]
-            energy[:, row : row + LANES] = lax.dot_general(
-                jnp.ones((8, LANES), jnp.float32),
-                total,
-                (((1,), (1,)), ((), ())),
-                precision=lax.Precision.HIGHEST,
-                preferred_element_type=jnp.float32,
-            )
+    energy[:, :columns] = energies[...]
+    energy[:, columns:] = lane_energy(rim, 0)
     value = energy[...]
     stride = 1
     while stride < DELAYS:
@@ -252,8 +320,8 @@
         fanned[:, half * LANES : (half + 1) * LANES] = result.astype(jnp.bfloat16)
 
 
-def prepare(record, rim, pieces):
-    width = record.shape[0] + LANES
+def prepare(energies, rim, pieces):
+    width = energies.shape[1] + LANES
     vm = pl.BlockSpec(memory_space=pltpu.VMEM)
     return pl.pallas_call(
         prepare_kernel,
@@ -264,8 +332,8 @@
         in_specs=[vm] * (2 + len(pieces)),
         out_specs=[vm] * 2,
         scratch_shapes=[pltpu.VMEM((8, width), jnp.float32), pltpu.VMEM((width, LANES), jnp.float32)],
-        compiler_params=pltpu.CompilerParams(vmem_limit_bytes=40 * 1024 * 1024),
-    )(record, rim, *pieces)
+        compiler_params=pltpu.CompilerParams(vmem_limit_bytes=16 * 1024 * 1024),
+    )(energies, rim, *pieces)
 
 
 def body(record, eigvecs, starts, kernel_width):
@@ -275,15 +343,24 @@
     groups = -(-(PANEL + DELAYS - 1 + GROUP - 1) // GROUP)
     deal = -(-groups // homes)
     half = homes // 2
-    cut = (deal + 1) // 2 * GROUP
+    cut = (deal + 1) // 2
+    with jax.named_scope("first_rows"):
+        rim, *opening = first_rows(homes, deal, cut, starts, record)
+    cut = cut * GROUP
+    leading = [(step_round(opening[2 * slot], 1), step_round(opening[2 * slot + 1], -1)) for slot in range(SLOTS)]
+    eigvecs, leading[1] = lax.optimization_barrier((eigvecs, leading[1]))
+    rim, leading[0] = lax.optimization_barrier((rim, leading[0]))
+    rim = lax.ppermute(rim, "tm", [(i, i + 1) for i in range(homes - 1)])
+    pieces = [eigvecs]
+    for hop in range(1, sharers):
+        pieces.append(lax.ppermute(eigvecs, "panel", [((i + hop) % sharers, i) for i in range(sharers)]))
     with jax.named_scope("own_rows"):
-        chunks = own_rows(homes, deal, starts, record)
+        energies, chunks = own_rows(homes, deal, starts, record)
     shards = []
     for slot in range(SLOTS):
         with jax.named_scope("scatter"):
             mine = chunks[slot]
-            ahead = step_round(mine[half][:cut], 1)
-            back = step_round(mine[half][cut:], -1)
+            ahead, back = leading[slot]
             ahead = mine[half - 1].at[:cut].add(ahead)
             back = mine[half + 1].at[cut:].add(back)
             for hop in range(half - 2, -1, -1):
@@ -291,13 +368,9 @@
                 back = step_round(back, -1)
                 back = back if hop == 0 else mine[homes - hop] + back
             shards.append(ahead + back)
-    rim = lax.ppermute(record[columns - LANES :], "tm", [(i, i + 1) for i in range(homes - 1)])
-    pieces = [eigvecs]
-    for hop in range(1, sharers):
-        pieces.append(lax.ppermute(eigvecs, "panel", [((i + hop) % sharers, i) for i in range(sharers)]))
+    energies, shards[0] = lax.optimization_barrier((energies, shards[0]))
     with jax.named_scope("prepare"):
-        norms, fanned = prepare(record, rim, pieces)
-        shards, norms, fanned = lax.optimization_barrier((shards, norms, fanned))
+        norms, fanned = prepare(energies, rim, pieces)
     scale = -1.4426950408889634 / (kernel_width * (DELAYS * channels))
     results = []
     with jax.named_scope("gather"):

time: 129 us -> 123 us (0.953)
  waiting for transfers between devices: 41.6 us -> 31.4 us
  starting transfers between devices: 40.7 us -> 46 us
  local copies, waits for them, and re-layouts: 7.13 us -> 3.29 us
  Pallas kernels: 23.8 us -> 26.8 us
  other arithmetic: 3.12 us -> 1.76 us
    ppermute x32, waiting for transfers between devices: 37 us -> 30.4 us  [step_round(): lax.ppermute(value, 'tm', [(order[i], order[(i + way) % homes]) for i in...]
    pallas_call x1 -> x2, Pallas kernels: 1.9 us -> 6.22 us  [the longest x1 3.47 us: own_rows(): pl.pallas_call(lambda *refs: own_kernel(homes, deal, *refs), out_shape=[j...]
    ppermute x3, waiting for transfers between devices: 4.57 us -> 1.02 us  [body(): lax.ppermute(eigvecs, 'panel', [((i + hop) % sharers, i) for i in range(s...]
    unnamed x11 -> x6, local copies, waits for them, and re-layouts: 5.16 us -> 2.2 us
    ppermute x3, starting transfers between devices: 1.62 us -> 4.38 us  [body(): lax.ppermute(eigvecs, 'panel', [((i + hop) % sharers, i) for i in range(s...]
    ppermute x32, starting transfers between devices: 35.6 us -> 38.1 us  [step_round(): lax.ppermute(value, 'tm', [(order[i], order[(i + way) % homes]) for i in...]
    pallas_call x1, Pallas kernels: 3.39 us -> 1.79 us  [prepare(): pl.pallas_call(prepare_kernel, out_shape=[jax.ShapeDtypeStruct((8, width)...]
  transfers between devices with their start and end apart: 36 -> 36, of which waited for: 18 -> 15; matrix products, arithmetic and copies ran while one was open for 3% -> 1% of each run, Pallas kernels for 3% -> 4%
where the time goes in v5:
time: 123 us
  starting transfers between devices  46 us (37%)
  waiting for transfers between devices  31.4 us (26%)
  Pallas kernels  26.8 us (22%)
  blocking collectives  12.9 us (10%)
  local copies, waits for them, and re-layouts  3.29 us (3%)
  other arithmetic  1.76 us (1%)
    ppermute x32, starting transfers between devices, step_round(): lax.ppermute(value, 'tm', [(order[i], order[(i + way) % homes]) for i in...  38.1 us
    ppermute x32, waiting for transfers between devices, step_round(): lax.ppermute(value, 'tm', [(order[i], order[(i + way) % homes]) for i in...  30.4 us
    pallas_call x1, Pallas kernels, panel_call(): pl.pallas_call(lambda *refs: panel_kernel(homes, places, *refs), out_shap...  18.8 us
    all_to_all x1, blocking collectives, body(): total = jnp.sum(lax.all_to_all(partial, 'tm', 0, 0), axis=0)  12.9 us
    ppermute x3, starting transfers between devices, body(): lax.ppermute(eigvecs, 'panel', [((i + hop) % sharers, i) for i in range(s...  4.38 us
    ppermute x1, starting transfers between devices, body(): rim = lax.ppermute(rim, 'tm', [(i, i + 1) for i in range(homes - 1)])  3.49 us
    pallas_call x1, Pallas kernels, own_rows(): pl.pallas_call(lambda *refs: own_kernel(homes, deal, *refs), out_shape=[j...  3.47 us
    pallas_call x1, Pallas kernels, first_rows(): pl.pallas_call(lambda *refs: first_kernel(homes, deal, cut, *refs), out_s...  2.75 us
  transfers between devices with their start and end apart: 36, of which 15 were waited for; matrix products, arithmetic and copies ran while one was open for 1% of the time, Pallas kernels for 4%

profile of v5, /device:TPU:0, one launch (start us, length us, event | category | flops | bytes accessed | tf_op | source)
XLA Modules:
  0.0 123.0 jit_solution(15519165290027982473)
XLA Ops:
  0.0 2.7 %first_rows.1 = (bf16[128,1024]{1,0:T(8,128)(2,1)}, bf16[64,1024]{1,0:T(8,128)(2,1)}, bf16[48,1024]{1,0:T(8,128)(2,1)}, bf16[64,1024]{1,0:T(8,128)(2,1)}, bf16[48,1024]{1,0:T(8,128)(2,1)}) custom-call(s32[2]{0:T(128)} %refs_0_.5, bf16[2048,1024]{1,0:T(8,128)(2,1)} %refs_2_.1), custom_call_target="tpu_custom_call" | custom-call | tf_op jit(solution)/shard_map/first_rows/pallas_call | solution.py:216
  2.8 3.1 %collective-permute-start = (bf16[64,1024]{1,0:T(8,128)(2,1)}, bf16[64,1024]{1,0:T(8,128)(2,1)S(1)}, u32[]{:S(2)}, u32[]{:S(2)}) collective-permute-start(bf16[64,1024]{1,0:T(8,128)(2,1)} %get-tuple-element.84), channel_id=1, source_target_pairs={{0,8},{8,16},{16,24},{24,28},{28,20},{20,12},{12,4},{4,0},{1,9},{9... | collective-permute-start | bytes 393224 | tf_op jit(solution)/shard_map/ppermute | solution.py:167
  5.8 2.0 %collective-permute-start.9 = (bf16[64,1024]{1,0:T(8,128)(2,1)}, bf16[64,1024]{1,0:T(8,128)(2,1)S(1)}, u32[]{:S(2)}, u32[]{:S(2)}) collective-permute-start(bf16[64,1024]{1,0:T(8,128)(2,1)} %get-tuple-element.98), channel_id=1, source_target_pairs={{0,8},{8,16},{16,24},{24,28},{28,20},{20,12},{12,4},{4,0},{1,9},{9... | collective-permute-start | bytes 393224 | tf_op jit(solution)/shard_map/ppermute | solution.py:167
  7.9 2.2 %copy-done = bf16[2048,1024]{1,0:T(8,128)(2,1)S(1)} copy-done((bf16[2048,1024]{1,0:T(8,128)(2,1)S(1)}, bf16[2048,1024]{1,0:T(8,128)(2,1)}, u32[]{:S(2)}) %copy-start) | copy-done | bytes 4194328
  10.1 3.5 %own_rows.1 = (f32[8,2048]{1,0:T(8,128)S(1)}, bf16[112,1024]{1,0:T(8,128)(2,1)S(1)}, bf16[112,1024]{1,0:T(8,128)(2,1)S(1)}, bf16[112,1024]{1,0:T(8,128)(2,1)S(1)...) custom-call(s32[2]{0:T(128)S(1)} %copy-done.1, ...), custom_call_target="tpu_custom_call" | custom-call | tf_op jit(solution)/shard_map/own_rows/pallas_call | solution.py:273
  13.6 2.0 %collective-permute-start.3 = (bf16[112,1024]{1,0:T(8,128)(2,1)S(1)}, bf16[112,1024]{1,0:T(8,128)(2,1)S(1)}, u32[]{:S(2)}, u32[]{:S(2)}) collective-permute-start(bf16[112,1024]{1,0:T(8,128)(2,1)S(1)} %add_dynamic-update-slice_fusion.1), channel_id=1, source_target_pairs={{0,8},{8,16},{16,24},{24,28},{28,20},{20,12},{12,4},{4,0},{1,9},{9... | collective-permute-start | bytes 688136 | tf_op jit(solution)/shard_map/scatter/ppermute | solution.py:167
  15.9 2.0 %collective-permute-start.22 = (bf16[112,1024]{1,0:T(8,128)(2,1)S(1)}, bf16[112,1024]{1,0:T(8,128)(2,1)S(1)}, u32[]{:S(2)}, u32[]{:S(2)}) collective-permute-start(bf16[112,1024]{1,0:T(8,128)(2,1)S(1)} %add_dynamic-update-slice_fusion), channel_id=1, source_target_pairs={{0,8},{8,16},{16,24},{24,28},{28,20},{20,12},{12,4},{4,0},{1,9},{9... | collective-permute-start | bytes 688136 | tf_op jit(solution)/shard_map/scatter/ppermute | solution.py:167
  18.0 4.2 %collective-permute-done.3 = bf16[112,1024]{1,0:T(8,128)(2,1)S(1)} collective-permute-done((bf16[112,1024]{1,0:T(8,128)(2,1)S(1)}, bf16[112,1024]{1,0:T(8,128)(2,1)S(1)}, u32[]{:S(2)}, u32[]{:S(2)}) %collective-permute-start.3) | collective-permute-done | bytes 229408 | tf_op jit(solution)/shard_map/scatter/ppermute | solution.py:167
  22.3 2.0 %collective-permute-start.4 = (bf16[112,1024]{1,0:T(8,128)(2,1)S(1)}, bf16[112,1024]{1,0:T(8,128)(2,1)S(1)}, u32[]{:S(2)}, u32[]{:S(2)}) collective-permute-start(bf16[112,1024]{1,0:T(8,128)(2,1)S(1)} %add.65), channel_id=1, source_target_pairs={{0,8},{8,16},{16,24},{24,28},{28,20},{20,12},{12,4},{4,0},{1,9},{9... | collective-permute-start | bytes 688136 | tf_op jit(solution)/shard_map/scatter/ppermute | solution.py:167
  24.5 2.7 %collective-permute-done.22 = bf16[112,1024]{1,0:T(8,128)(2,1)S(1)} collective-permute-done((bf16[112,1024]{1,0:T(8,128)(2,1)S(1)}, bf16[112,1024]{1,0:T(8,128)(2,1)S(1)}, u32[]{:S(2)}, u32[]{:S(2)}) %collective-permute-start.22) | collective-permute-done | bytes 229408 | tf_op jit(solution)/shard_map/scatter/ppermute | solution.py:167
  27.2 2.0 %collective-permute-start.23 = (bf16[112,1024]{1,0:T(8,128)(2,1)S(1)}, bf16[112,1024]{1,0:T(8,128)(2,1)S(1)}, u32[]{:S(2)}, u32[]{:S(2)}) collective-permute-start(bf16[112,1024]{1,0:T(8,128)(2,1)S(1)} %add.73), channel_id=1, source_target_pairs={{0,8},{8,16},{16,24},{24,28},{28,20},{20,12},{12,4},{4,0},{1,9},{9... | collective-permute-start | bytes 688136 | tf_op jit(solution)/shard_map/scatter/ppermute | solution.py:167
  29.4 2.7 %collective-permute-done.4 = bf16[112,1024]{1,0:T(8,128)(2,1)S(1)} collective-permute-done((bf16[112,1024]{1,0:T(8,128)(2,1)S(1)}, bf16[112,1024]{1,0:T(8,128)(2,1)S(1)}, u32[]{:S(2)}, u32[]{:S(2)}) %collective-permute-start.4) | collective-permute-done | bytes 229408 | tf_op jit(solution)/shard_map/scatter/ppermute | solution.py:167
  32.1 2.0 %collective-permute-start.5 = (bf16[112,1024]{1,0:T(8,128)(2,1)S(1)}, bf16[112,1024]{1,0:T(8,128)(2,1)S(1)}, u32[]{:S(2)}, u32[]{:S(2)}) collective-permute-start(bf16[112,1024]{1,0:T(8,128)(2,1)S(1)} %add.66), channel_id=1, source_target_pairs={{0,8},{8,16},{16,24},{24,28},{28,20},{20,12},{12,4},{4,0},{1,9},{9... | collective-permute-start | bytes 688136 | tf_op jit(solution)/shard_map/scatter/ppermute | solution.py:167
  34.3 2.7 %collective-permute-done.23 = bf16[112,1024]{1,0:T(8,128)(2,1)S(1)} collective-permute-done((bf16[112,1024]{1,0:T(8,128)(2,1)S(1)}, bf16[112,1024]{1,0:T(8,128)(2,1)S(1)}, u32[]{:S(2)}, u32[]{:S(2)}) %collective-permute-start.23) | collective-permute-done | bytes 229408 | tf_op jit(solution)/shard_map/scatter/ppermute | solution.py:167
  37.0 2.0 %collective-permute-start.24 = (bf16[112,1024]{1,0:T(8,128)(2,1)S(1)}, bf16[112,1024]{1,0:T(8,128)(2,1)S(1)}, u32[]{:S(2)}, u32[]{:S(2)}) collective-permute-start(bf16[112,1024]{1,0:T(8,128)(2,1)S(1)} %add.74), channel_id=1, source_target_pairs={{0,8},{8,16},{16,24},{24,28},{28,20},{20,12},{12,4},{4,0},{1,9},{9... | collective-permute-start | bytes 688136 | tf_op jit(solution)/shard_map/scatter/ppermute | solution.py:167
  39.2 2.7 %collective-permute-done.5 = bf16[112,1024]{1,0:T(8,128)(2,1)S(1)} collective-permute-done((bf16[112,1024]{1,0:T(8,128)(2,1)S(1)}, bf16[112,1024]{1,0:T(8,128)(2,1)S(1)}, u32[]{:S(2)}, u32[]{:S(2)}) %collective-permute-start.5) | collective-permute-done | bytes 229408 | tf_op jit(solution)/shard_map/scatter/ppermute | solution.py:167
  41.9 1.9 %collective-permute-done.8 = bf16[112,1024]{1,0:T(8,128)(2,1)S(1)} collective-permute-done((bf16[112,1024]{1,0:T(8,128)(2,1)S(1)}, bf16[112,1024]{1,0:T(8,128)(2,1)S(1)}, u32[]{:S(2)}, u32[]{:S(2)}) %collective-permute-start.8) | collective-permute-done | bytes 229408 | tf_op jit(solution)/shard_map/scatter/ppermute | solution.py:167
  43.8 1.6 %collective-permute-start.14 = (bf16[112,1024]{1,0:T(8,128)(2,1)S(1)}, bf16[112,1024]{1,0:T(8,128)(2,1)S(1)}, u32[]{:S(2)}, u32[]{:S(2)}) collective-permute-start(bf16[112,1024]{1,0:T(8,128)(2,1)S(1)} %add_add_fusion.1.refs_6_), channel_id=1, source_target_pairs={{0,8},{8,16},{16,24},{24,28},{28,20},{20,12},{12,4},{4,0},{1,9},{9... | collective-permute-start | bytes 688136 | tf_op jit(solution)/shard_map/gather/ppermute | solution.py:167
  46.9 2.0 %collective-permute-start.28 = (bf16[112,1024]{1,0:T(8,128)(2,1)S(1)}, bf16[112,1024]{1,0:T(8,128)(2,1)S(1)}, u32[]{:S(2)}, u32[]{:S(2)}) collective-permute-start(bf16[112,1024]{1,0:T(8,128)(2,1)S(1)} %add_add_fusion.refs_15_), channel_id=1, source_target_pairs={{0,8},{8,16},{16,24},{24,28},{28,20},{20,12},{12,4},{4,0},{1,9},{9... | collective-permute-start | bytes 688136 | tf_op jit(solution)/shard_map/gather/ppermute | solution.py:167
  48.9 1.9 %collective-permute-start.29 = (bf16[112,1024]{1,0:T(8,128)(2,1)S(1)}, bf16[112,1024]{1,0:T(8,128)(2,1)S(1)}, u32[]{:S(2)}, u32[]{:S(2)}) collective-permute-start(bf16[112,1024]{1,0:T(8,128)(2,1)S(1)} %add_add_fusion.refs_15_), channel_id=1, source_target_pairs={{0,4},{8,0},{16,8},{24,16},{28,24},{20,28},{12,20},{4,12},{1,5},{9... | collective-permute-start | bytes 688136 | tf_op jit(solution)/shard_map/gather/ppermute | solution.py:167
  52.4 1.6 %collective-permute-start.16 = (bf16[112,1024]{1,0:T(8,128)(2,1)S(1)}, bf16[112,1024]{1,0:T(8,128)(2,1)S(1)}, u32[]{:S(2)}, u32[]{:S(2)}) collective-permute-start(bf16[112,1024]{1,0:T(8,128)(2,1)S(1)} %collective-permute-done.14.refs_7_), channel_id=1, source_target_pairs={{0,8},{8,16},{16,24},{24,28},{28,20},{20,12},{12,4},{4,0},{1,9},{9... | collective-permute-start | bytes 688136 | tf_op jit(solution)/shard_map/gather/ppermute | solution.py:167
  54.0 3.3 %collective-permute-done.28.refs_16_ = bf16[112,1024]{1,0:T(8,128)(2,1)S(1)} collective-permute-done((bf16[112,1024]{1,0:T(8,128)(2,1)S(1)}, bf16[112,1024]{1,0:T(8,128)(2,1)S(1)}, u32[]{:S(2)}, u32[]{:S(2)}) %collective-permute-start.28) | collective-permute-done | bytes 229408 | tf_op jit(solution)/shard_map/gather/ppermute | solution.py:167
  57.3 1.6 %collective-permute-start.30 = (bf16[112,1024]{1,0:T(8,128)(2,1)S(1)}, bf16[112,1024]{1,0:T(8,128)(2,1)S(1)}, u32[]{:S(2)}, u32[]{:S(2)}) collective-permute-start(bf16[112,1024]{1,0:T(8,128)(2,1)S(1)} %collective-permute-done.28.refs_16_), channel_id=1, source_target_pairs={{0,8},{8,16},{16,24},{24,28},{28,20},{20,12},{12,4},{4,0},{1,9},{9... | collective-permute-start | bytes 688136 | tf_op jit(solution)/shard_map/gather/ppermute | solution.py:167
  60.6 1.7 %collective-permute-done.16.refs_9_ = bf16[112,1024]{1,0:T(8,128)(2,1)S(1)} collective-permute-done((bf16[112,1024]{1,0:T(8,128)(2,1)S(1)}, bf16[112,1024]{1,0:T(8,128)(2,1)S(1)}, u32[]{:S(2)}, u32[]{:S(2)}) %collective-permute-start.16) | collective-permute-done | bytes 229408 | tf_op jit(solution)/shard_map/gather/ppermute | solution.py:167
  63.8 3.3 %collective-permute-done.30.refs_18_ = bf16[112,1024]{1,0:T(8,128)(2,1)S(1)} collective-permute-done((bf16[112,1024]{1,0:T(8,128)(2,1)S(1)}, bf16[112,1024]{1,0:T(8,128)(2,1)S(1)}, u32[]{:S(2)}, u32[]{:S(2)}) %collective-permute-start.30) | collective-permute-done | bytes 229408 | tf_op jit(solution)/shard_map/gather/ppermute | solution.py:167
  70.4 3.5 %collective-permute-start.2 = (bf16[128,1024]{1,0:T(8,128)(2,1)}, bf16[128,1024]{1,0:T(8,128)(2,1)S(1)}, u32[]{:S(2)}, u32[]{:S(2)}) collective-permute-start(bf16[128,1024]{1,0:T(8,128)(2,1)} %get-tuple-element.86), channel_id=1, source_target_pairs={{0,4},{4,8},{8,12},{12,16},{16,20},{20,24},{24,28},{1,5},{5,9},{9,... | collective-permute-start | bytes 786440 | tf_op jit(solution)/shard_map/ppermute | solution.py:353
  74.3 1.6 %collective-permute-start.12 = (bf16[512,32]{1,0:T(8,128)(2,1)S(1)}, bf16[512,32]{1,0:T(8,128)(2,1)S(1)}, u32[]{:S(2)}, u32[]{:S(2)}) collective-permute-start(bf16[512,32]{1,0:T(8,128)(2,1)S(1)} %copy.22.rest_0_), channel_id=1, source_target_pairs={{2,0},{3,1},{0,2},{1,3},{6,4},{7,5},{4,6},{5,7},{10,8},{11,9},{8,1... | collective-permute-start | bytes 98312 | tf_op jit(solution)/shard_map/ppermute | solution.py:356
  76.9 2.7 %collective-permute-start.13 = (bf16[512,32]{1,0:T(8,128)(2,1)S(1)}, bf16[512,32]{1,0:T(8,128)(2,1)S(1)}, u32[]{:S(2)}, u32[]{:S(2)}) collective-permute-start(bf16[512,32]{1,0:T(8,128)(2,1)S(1)} %copy.22.rest_0_), channel_id=1, source_target_pairs={{3,0},{0,1},{1,2},{2,3},{7,4},{4,5},{5,6},{6,7},{11,8},{8,9},{9,10... | collective-permute-start | bytes 98312 | tf_op jit(solution)/shard_map/ppermute | solution.py:356
  79.6 1.8 %collective-permute-start.20 = (bf16[64,1024]{1,0:T(8,128)(2,1)S(1)}, bf16[64,1024]{1,0:T(8,128)(2,1)S(1)}, u32[]{:S(2)}, u32[]{:S(2)}) collective-permute-start(bf16[64,1024]{1,0:T(8,128)(2,1)S(1)} %slice.160), channel_id=1, source_target_pairs={{0,8},{8,16},{16,24},{24,28},{28,20},{20,12},{12,4},{4,0},{1,9},{9... | collective-permute-start | bytes 393224 | tf_op jit(solution)/shard_map/gather/ppermute | solution.py:167
  85.3 1.8 %prepare.1 = (f32[8,2176]{1,0:T(8,128)S(1)}, bf16[2176,256]{1,0:T(8,128)(2,1)S(1)}) custom-call(f32[8,2048]{1,0:T(8,128)S(1)} %get-tuple-element.97.energies, bf16[128,1024]{1,0:T(8,128)(2,1)S(1)} %collective-permute-done.2.rim.refs_3_, bf16[512,32]{1,0:T(8,128)(2,1)S(1)} %copy.22.rest_0_, bf16[512,32]{1,0:T(8,128)(2,1)S(1)} %collective-permute-done.11.rest_1_, ...), custom_call_target="tpu_custom_call" | custom-call | tf_op jit(solution)/shard_map/prepare/pallas_call | solution.py:326
  89.3 18.8 %panels.1 = f32[8,64,128]{2,1,0:T(8,128)S(1)} custom-call(s32[2]{0:T(128)S(1)} %copy-done.1, f32[1]{0:T(128)S(6)} %div.23.refs_1_, bf16[2048,1024]{1,0:T(8,128)(2,1)} %refs_2_.1, bf16[128,1024]{1,0:T(8,128)(2,1)S(1)} %collective-permute-done.2.rim.refs_3_, bf16[2176,256]{1,0:T(8,128)(2,1)S(1)} %get-tuple-element.101.refs_4_, ...), custom_call_target="tpu_custom_call" | custom-call | flops 7558135808 | bytes 10000000 | tf_op jit(solution)/shard_map/panels/pallas_call | solution.py:129
  108.1 12.9 %all_to_all.5 = f32[8,64,128]{2,1,0:T(8,128)S(1)} all-to-all(f32[8,64,128]{2,1,0:T(8,128)S(1)} %panels.1), channel_id=1, replica_groups=mesh['tm'=8,'panel'=4] {'tm'}, dimensions={0} | all-to-all | bytes 524288 | tf_op jit(solution)/shard_map/all_to_all | solution.py:389
  (90 shorter events, 19.5 us)
Async XLA Ops:
  2.8 10.8 %collective-permute-start = (bf16[64,1024]{1,0:T(8,128)(2,1)}, bf16[64,1024]{1,0:T(8,128)(2,1)S(1)}, u32[]{:S(2)}, u32[]{:S(2)}) collective-permute-start(bf16[64,1024]{1,0:T(8,128)(2,1)} %get-tuple-element.84), channel_id=1, source_target_pairs={{0,8},{8,16},{16,24},{24,28},{28,20},{20,12},{12,4},{4,0},{1,9},{9... | collective-permute-start | bytes 393224 | tf_op jit(solution)/shard_map/ppermute | solution.py:167
  5.8 7.7 %collective-permute-start.1 = (bf16[48,1024]{1,0:T(8,128)(2,1)}, bf16[48,1024]{1,0:T(8,128)(2,1)S(1)}, u32[]{:S(2)}, u32[]{:S(2)}) collective-permute-start(bf16[48,1024]{1,0:T(8,128)(2,1)} %get-tuple-element.85), channel_id=1, source_target_pairs={{0,4},{8,0},{16,8},{24,16},{28,24},{20,28},{12,20},{4,12},{1,5},{9... | collective-permute-start | bytes 294920 | tf_op jit(solution)/shard_map/ppermute | solution.py:167
  5.8 10.0 %collective-permute-start.9 = (bf16[64,1024]{1,0:T(8,128)(2,1)}, bf16[64,1024]{1,0:T(8,128)(2,1)S(1)}, u32[]{:S(2)}, u32[]{:S(2)}) collective-permute-start(bf16[64,1024]{1,0:T(8,128)(2,1)} %get-tuple-element.98), channel_id=1, source_target_pairs={{0,8},{8,16},{16,24},{24,28},{28,20},{20,12},{12,4},{4,0},{1,9},{9... | collective-permute-start | bytes 393224 | tf_op jit(solution)/shard_map/ppermute | solution.py:167
  7.9 7.9 %collective-permute-start.10 = (bf16[48,1024]{1,0:T(8,128)(2,1)}, bf16[48,1024]{1,0:T(8,128)(2,1)S(1)}, u32[]{:S(2)}, u32[]{:S(2)}) collective-permute-start(bf16[48,1024]{1,0:T(8,128)(2,1)} %get-tuple-element.99), channel_id=1, source_target_pairs={{0,4},{8,0},{16,8},{24,16},{28,24},{20,28},{12,20},{4,12},{1,5},{9... | collective-permute-start | bytes 294920 | tf_op jit(solution)/shard_map/ppermute | solution.py:167
  13.6 8.6 %collective-permute-start.3 = (bf16[112,1024]{1,0:T(8,128)(2,1)S(1)}, bf16[112,1024]{1,0:T(8,128)(2,1)S(1)}, u32[]{:S(2)}, u32[]{:S(2)}) collective-permute-start(bf16[112,1024]{1,0:T(8,128)(2,1)S(1)} %add_dynamic-update-slice_fusion.1), channel_id=1, source_target_pairs={{0,8},{8,16},{16,24},{24,28},{28,20},{20,12},{12,4},{4,0},{1,9},{9... | collective-permute-start | bytes 688136 | tf_op jit(solution)/shard_map/scatter/ppermute | solution.py:167
  15.7 8.6 %collective-permute-start.6 = (bf16[112,1024]{1,0:T(8,128)(2,1)S(1)}, bf16[112,1024]{1,0:T(8,128)(2,1)S(1)}, u32[]{:S(2)}, u32[]{:S(2)}) collective-permute-start(bf16[112,1024]{1,0:T(8,128)(2,1)S(1)} %add_dynamic-update-slice_fusion.3), channel_id=1, source_target_pairs={{0,4},{8,0},{16,8},{24,16},{28,24},{20,28},{12,20},{4,12},{1,5},{9... | collective-permute-start | bytes 688136 | tf_op jit(solution)/shard_map/scatter/ppermute | solution.py:167
  15.9 11.3 %collective-permute-start.22 = (bf16[112,1024]{1,0:T(8,128)(2,1)S(1)}, bf16[112,1024]{1,0:T(8,128)(2,1)S(1)}, u32[]{:S(2)}, u32[]{:S(2)}) collective-permute-start(bf16[112,1024]{1,0:T(8,128)(2,1)S(1)} %add_dynamic-update-slice_fusion), channel_id=1, source_target_pairs={{0,8},{8,16},{16,24},{24,28},{28,20},{20,12},{12,4},{4,0},{1,9},{9... | collective-permute-start | bytes 688136 | tf_op jit(solution)/shard_map/scatter/ppermute | solution.py:167
  17.9 11.3 %collective-permute-start.25 = (bf16[112,1024]{1,0:T(8,128)(2,1)S(1)}, bf16[112,1024]{1,0:T(8,128)(2,1)S(1)}, u32[]{:S(2)}, u32[]{:S(2)}) collective-permute-start(bf16[112,1024]{1,0:T(8,128)(2,1)S(1)} %add_dynamic-update-slice_fusion.2), channel_id=1, source_target_pairs={{0,4},{8,0},{16,8},{24,16},{28,24},{20,28},{12,20},{4,12},{1,5},{9... | collective-permute-start | bytes 688136 | tf_op jit(solution)/shard_map/scatter/ppermute | solution.py:167
  22.3 9.8 %collective-permute-start.4 = (bf16[112,1024]{1,0:T(8,128)(2,1)S(1)}, bf16[112,1024]{1,0:T(8,128)(2,1)S(1)}, u32[]{:S(2)}, u32[]{:S(2)}) collective-permute-start(bf16[112,1024]{1,0:T(8,128)(2,1)S(1)} %add.65), channel_id=1, source_target_pairs={{0,8},{8,16},{16,24},{24,28},{28,20},{20,12},{12,4},{4,0},{1,9},{9... | collective-permute-start | bytes 688136 | tf_op jit(solution)/shard_map/scatter/ppermute | solution.py:167
  24.4 9.8 %collective-permute-start.7 = (bf16[112,1024]{1,0:T(8,128)(2,1)S(1)}, bf16[112,1024]{1,0:T(8,128)(2,1)S(1)}, u32[]{:S(2)}, u32[]{:S(2)}) collective-permute-start(bf16[112,1024]{1,0:T(8,128)(2,1)S(1)} %add.69), channel_id=1, source_target_pairs={{0,4},{8,0},{16,8},{24,16},{28,24},{20,28},{12,20},{4,12},{1,5},{9... | collective-permute-start | bytes 688136 | tf_op jit(solution)/shard_map/scatter/ppermute | solution.py:167
  27.2 9.8 %collective-permute-start.23 = (bf16[112,1024]{1,0:T(8,128)(2,1)S(1)}, bf16[112,1024]{1,0:T(8,128)(2,1)S(1)}, u32[]{:S(2)}, u32[]{:S(2)}) collective-permute-start(bf16[112,1024]{1,0:T(8,128)(2,1)S(1)} %add.73), channel_id=1, source_target_pairs={{0,8},{8,16},{16,24},{24,28},{28,20},{20,12},{12,4},{4,0},{1,9},{9... | collective-permute-start | bytes 688136 | tf_op jit(solution)/shard_map/scatter/ppermute | solution.py:167
  29.3 9.8 %collective-permute-start.26 = (bf16[112,1024]{1,0:T(8,128)(2,1)S(1)}, bf16[112,1024]{1,0:T(8,128)(2,1)S(1)}, u32[]{:S(2)}, u32[]{:S(2)}) collective-permute-start(bf16[112,1024]{1,0:T(8,128)(2,1)S(1)} %add.77), channel_id=1, source_target_pairs={{0,4},{8,0},{16,8},{24,16},{28,24},{20,28},{12,20},{4,12},{1,5},{9... | collective-permute-start | bytes 688136 | tf_op jit(solution)/shard_map/scatter/ppermute | solution.py:167
  32.1 9.8 %collective-permute-start.5 = (bf16[112,1024]{1,0:T(8,128)(2,1)S(1)}, bf16[112,1024]{1,0:T(8,128)(2,1)S(1)}, u32[]{:S(2)}, u32[]{:S(2)}) collective-permute-start(bf16[112,1024]{1,0:T(8,128)(2,1)S(1)} %add.66), channel_id=1, source_target_pairs={{0,8},{8,16},{16,24},{24,28},{28,20},{20,12},{12,4},{4,0},{1,9},{9... | collective-permute-start | bytes 688136 | tf_op jit(solution)/shard_map/scatter/ppermute | solution.py:167
  34.2 9.6 %collective-permute-start.8 = (bf16[112,1024]{1,0:T(8,128)(2,1)S(1)}, bf16[112,1024]{1,0:T(8,128)(2,1)S(1)}, u32[]{:S(2)}, u32[]{:S(2)}) collective-permute-start(bf16[112,1024]{1,0:T(8,128)(2,1)S(1)} %add.70), channel_id=1, source_target_pairs={{0,4},{8,0},{16,8},{24,16},{28,24},{20,28},{12,20},{4,12},{1,5},{9... | collective-permute-start | bytes 688136 | tf_op jit(solution)/shard_map/scatter/ppermute | solution.py:167
  37.0 9.8 %collective-permute-start.24 = (bf16[112,1024]{1,0:T(8,128)(2,1)S(1)}, bf16[112,1024]{1,0:T(8,128)(2,1)S(1)}, u32[]{:S(2)}, u32[]{:S(2)}) collective-permute-start(bf16[112,1024]{1,0:T(8,128)(2,1)S(1)} %add.74), channel_id=1, source_target_pairs={{0,8},{8,16},{16,24},{24,28},{28,20},{20,12},{12,4},{4,0},{1,9},{9... | collective-permute-start | bytes 688136 | tf_op jit(solution)/shard_map/scatter/ppermute | solution.py:167
  39.1 7.7 %collective-permute-start.27 = (bf16[112,1024]{1,0:T(8,128)(2,1)S(1)}, bf16[112,1024]{1,0:T(8,128)(2,1)S(1)}, u32[]{:S(2)}, u32[]{:S(2)}) collective-permute-start(bf16[112,1024]{1,0:T(8,128)(2,1)S(1)} %add.78), channel_id=1, source_target_pairs={{0,4},{8,0},{16,8},{24,16},{28,24},{20,28},{12,20},{4,12},{1,5},{9... | collective-permute-start | bytes 688136 | tf_op jit(solution)/shard_map/scatter/ppermute | solution.py:167
  43.8 8.6 %collective-permute-start.14 = (bf16[112,1024]{1,0:T(8,128)(2,1)S(1)}, bf16[112,1024]{1,0:T(8,128)(2,1)S(1)}, u32[]{:S(2)}, u32[]{:S(2)}) collective-permute-start(bf16[112,1024]{1,0:T(8,128)(2,1)S(1)} %add_add_fusion.1.refs_6_), channel_id=1, source_target_pairs={{0,8},{8,16},{16,24},{24,28},{28,20},{20,12},{12,4},{4,0},{1,9},{9... | collective-permute-start | bytes 688136 | tf_op jit(solution)/shard_map/gather/ppermute | solution.py:167
  46.9 10.5 %collective-permute-start.28 = (bf16[112,1024]{1,0:T(8,128)(2,1)S(1)}, bf16[112,1024]{1,0:T(8,128)(2,1)S(1)}, u32[]{:S(2)}, u32[]{:S(2)}) collective-permute-start(bf16[112,1024]{1,0:T(8,128)(2,1)S(1)} %add_add_fusion.refs_15_), channel_id=1, source_target_pairs={{0,8},{8,16},{16,24},{24,28},{28,20},{20,12},{12,4},{4,0},{1,9},{9... | collective-permute-start | bytes 688136 | tf_op jit(solution)/shard_map/gather/ppermute | solution.py:167
  48.9 10.0 %collective-permute-start.15 = (bf16[112,1024]{1,0:T(8,128)(2,1)S(1)}, bf16[112,1024]{1,0:T(8,128)(2,1)S(1)}, u32[]{:S(2)}, u32[]{:S(2)}) collective-permute-start(bf16[112,1024]{1,0:T(8,128)(2,1)S(1)} %add_add_fusion.1.refs_6_), channel_id=1, source_target_pairs={{0,4},{8,0},{16,8},{24,16},{28,24},{20,28},{12,20},{4,12},{1,5},{9... | collective-permute-start | bytes 688136 | tf_op jit(solution)/shard_map/gather/ppermute | solution.py:167
  48.9 10.4 %collective-permute-start.29 = (bf16[112,1024]{1,0:T(8,128)(2,1)S(1)}, bf16[112,1024]{1,0:T(8,128)(2,1)S(1)}, u32[]{:S(2)}, u32[]{:S(2)}) collective-permute-start(bf16[112,1024]{1,0:T(8,128)(2,1)S(1)} %add_add_fusion.refs_15_), channel_id=1, source_target_pairs={{0,4},{8,0},{16,8},{24,16},{28,24},{20,28},{12,20},{4,12},{1,5},{9... | collective-permute-start | bytes 688136 | tf_op jit(solution)/shard_map/gather/ppermute | solution.py:167
  52.4 9.8 %collective-permute-start.16 = (bf16[112,1024]{1,0:T(8,128)(2,1)S(1)}, bf16[112,1024]{1,0:T(8,128)(2,1)S(1)}, u32[]{:S(2)}, u32[]{:S(2)}) collective-permute-start(bf16[112,1024]{1,0:T(8,128)(2,1)S(1)} %collective-permute-done.14.refs_7_), channel_id=1, source_target_pairs={{0,8},{8,16},{16,24},{24,28},{28,20},{20,12},{12,4},{4,0},{1,9},{9... | collective-permute-start | bytes 688136 | tf_op jit(solution)/shard_map/gather/ppermute | solution.py:167
  57.3 9.8 %collective-permute-start.30 = (bf16[112,1024]{1,0:T(8,128)(2,1)S(1)}, bf16[112,1024]{1,0:T(8,128)(2,1)S(1)}, u32[]{:S(2)}, u32[]{:S(2)}) collective-permute-start(bf16[112,1024]{1,0:T(8,128)(2,1)S(1)} %collective-permute-done.28.refs_16_), channel_id=1, source_target_pairs={{0,8},{8,16},{16,24},{24,28},{28,20},{20,12},{12,4},{4,0},{1,9},{9... | collective-permute-start | bytes 688136 | tf_op jit(solution)/shard_map/gather/ppermute | solution.py:167
  58.9 9.8 %collective-permute-start.17 = (bf16[112,1024]{1,0:T(8,128)(2,1)S(1)}, bf16[112,1024]{1,0:T(8,128)(2,1)S(1)}, u32[]{:S(2)}, u32[]{:S(2)}) collective-permute-start(bf16[112,1024]{1,0:T(8,128)(2,1)S(1)} %collective-permute-done.15.refs_8_), channel_id=1, source_target_pairs={{0,4},{8,0},{16,8},{24,16},{28,24},{20,28},{12,20},{4,12},{1,5},{9... | collective-permute-start | bytes 688136 | tf_op jit(solution)/shard_map/gather/ppermute | solution.py:167
  59.4 9.8 %collective-permute-start.31 = (bf16[112,1024]{1,0:T(8,128)(2,1)S(1)}, bf16[112,1024]{1,0:T(8,128)(2,1)}, u32[]{:S(2)}, u32[]{:S(2)}) collective-permute-start(bf16[112,1024]{1,0:T(8,128)(2,1)S(1)} %collective-permute-done.29.refs_17_), channel_id=1, source_target_pairs={{0,4},{8,0},{16,8},{24,16},{28,24},{20,28},{12,20},{4,12},{1,5},{9... | collective-permute-start | bytes 688136 | tf_op jit(solution)/shard_map/gather/ppermute | solution.py:167
  62.3 11.8 %collective-permute-start.18 = (bf16[112,1024]{1,0:T(8,128)(2,1)S(1)}, bf16[112,1024]{1,0:T(8,128)(2,1)S(1)}, u32[]{:S(2)}, u32[]{:S(2)}) collective-permute-start(bf16[112,1024]{1,0:T(8,128)(2,1)S(1)} %collective-permute-done.16.refs_9_), channel_id=1, source_target_pairs={{0,8},{8,16},{16,24},{24,28},{28,20},{20,12},{12,4},{4,0},{1,9},{9... | collective-permute-start | bytes 688136 | tf_op jit(solution)/shard_map/gather/ppermute | solution.py:167
  67.2 7.1 %collective-permute-start.32 = (bf16[112,1024]{1,0:T(8,128)(2,1)S(1)}, bf16[112,1024]{1,0:T(8,128)(2,1)S(1)}, u32[]{:S(2)}, u32[]{:S(2)}) collective-permute-start(bf16[112,1024]{1,0:T(8,128)(2,1)S(1)} %collective-permute-done.30.refs_18_), channel_id=1, source_target_pairs={{0,8},{8,16},{16,24},{24,28},{28,20},{20,12},{12,4},{4,0},{1,9},{9... | collective-permute-start | bytes 688136 | tf_op jit(solution)/shard_map/gather/ppermute | solution.py:167
  68.8 10.9 %collective-permute-start.19 = (bf16[112,1024]{1,0:T(8,128)(2,1)S(1)}, bf16[112,1024]{1,0:T(8,128)(2,1)S(1)}, u32[]{:S(2)}, u32[]{:S(2)}) collective-permute-start(bf16[112,1024]{1,0:T(8,128)(2,1)S(1)} %collective-permute-done.17.refs_10_), channel_id=1, source_target_pairs={{0,4},{8,0},{16,8},{24,16},{28,24},{20,28},{12,20},{4,12},{1,5},{9... | collective-permute-start | bytes 688136 | tf_op jit(solution)/shard_map/gather/ppermute | solution.py:167
  69.2 12.2 %collective-permute-start.33 = (bf16[112,1024]{1,0:T(8,128)(2,1)}, bf16[112,1024]{1,0:T(8,128)(2,1)S(1)}, u32[]{:S(2)}, u32[]{:S(2)}) collective-permute-start(bf16[112,1024]{1,0:T(8,128)(2,1)} %collective-permute-done.31.refs_19_), channel_id=1, source_target_pairs={{0,4},{8,0},{16,8},{24,16},{28,24},{20,28},{12,20},{4,12},{1,5},{9... | collective-permute-start | bytes 688136 | tf_op jit(solution)/shard_map/gather/ppermute | solution.py:167
  70.4 14.9 %collective-permute-start.2 = (bf16[128,1024]{1,0:T(8,128)(2,1)}, bf16[128,1024]{1,0:T(8,128)(2,1)S(1)}, u32[]{:S(2)}, u32[]{:S(2)}) collective-permute-start(bf16[128,1024]{1,0:T(8,128)(2,1)} %get-tuple-element.86), channel_id=1, source_target_pairs={{0,4},{4,8},{8,12},{12,16},{16,20},{20,24},{24,28},{1,5},{5,9},{9,... | collective-permute-start | bytes 786440 | tf_op jit(solution)/shard_map/ppermute | solution.py:353
  74.3 8.7 %collective-permute-start.12 = (bf16[512,32]{1,0:T(8,128)(2,1)S(1)}, bf16[512,32]{1,0:T(8,128)(2,1)S(1)}, u32[]{:S(2)}, u32[]{:S(2)}) collective-permute-start(bf16[512,32]{1,0:T(8,128)(2,1)S(1)} %copy.22.rest_0_), channel_id=1, source_target_pairs={{2,0},{3,1},{0,2},{1,3},{6,4},{7,5},{4,6},{5,7},{10,8},{11,9},{8,1... | collective-permute-start | bytes 98312 | tf_op jit(solution)/shard_map/ppermute | solution.py:356
  79.6 9.7 %collective-permute-start.20 = (bf16[64,1024]{1,0:T(8,128)(2,1)S(1)}, bf16[64,1024]{1,0:T(8,128)(2,1)S(1)}, u32[]{:S(2)}, u32[]{:S(2)}) collective-permute-start(bf16[64,1024]{1,0:T(8,128)(2,1)S(1)} %slice.160), channel_id=1, source_target_pairs={{0,8},{8,16},{16,24},{24,28},{28,20},{20,12},{12,4},{4,0},{1,9},{9... | collective-permute-start | bytes 393224 | tf_op jit(solution)/shard_map/gather/ppermute | solution.py:167
  81.4 7.9 %collective-permute-start.34 = (bf16[64,1024]{1,0:T(8,128)(2,1)S(1)}, bf16[64,1024]{1,0:T(8,128)(2,1)S(1)}, u32[]{:S(2)}, u32[]{:S(2)}) collective-permute-start(bf16[64,1024]{1,0:T(8,128)(2,1)S(1)} %slice.162), channel_id=1, source_target_pairs={{0,8},{8,16},{16,24},{24,28},{28,20},{20,12},{12,4},{4,0},{1,9},{9... | collective-permute-start | bytes 393224 | tf_op jit(solution)/shard_map/gather/ppermute | solution.py:167
  (7 other events, 90.9 us)
